TPU v7x, 512 devices: a whole 4x4x16 slice. The times are simulated.
512 devices in a mesh: seq: 32 (over y, x, core), grp: 16 (over z).
Axes of the slice: x: 4, y: 4, z: 16, core: 2. Of those that a mesh axis runs over, the one named last changes fastest.
Arguments:
- query: bfloat16 [16, 32, 4, 24, 4096], P('grp', 'seq'), may hold values from -6 to 6
- key_states: bfloat16 [16, 32, 4, 24, 4096], P('grp', 'seq'), may hold values from -6 to 6
- value_states: bfloat16 [16, 32, 4, 24, 4096], P('grp', 'seq'), may hold values from -12 to 12
- latent: float32 [16, 32, 4, 24, 64], P('grp', 'seq'), may hold values from -6 to 6
- sigma: float32 [16], P('grp'), may hold values from 0.3 to 1
- head_weight: bfloat16 [4096, 64], replicated, may hold values from -0.09375 to 0.09375
- latent_scale: float32 [16], replicated, may hold values from 0.5 to 2
- latent_shift: float32 [16], replicated, may hold values from -2 to 2
- frame_tail: bfloat16 [16, 2, 64, 48, 16], P(None, None, 'seq', 'grp'), may hold values from -6 to 6
- conv_weight: bfloat16 [432, 384], replicated, may hold values from -0.3125 to 0.3125
- conv_bias: float32 [384], replicated, may hold values from -4 to 4
Outputs:
- decoded: bfloat16 [16, 4, 64, 48, 384], P(None, None, 'seq', 'grp')
All inputs are finite; a program needn't handle non-finite values.
Results may differ from a plain program's by a relative error of at most 0.011.
Values may be sent and summed in bfloat16 or wider, within the bound.
No kernel may reach another device: no remote copies, remote signals or barrier semaphores. Data moves between devices by JAX's collectives and lax.ppermute only.
A program may use at most 64 MiB of HBM per device.

v0:
```python
from functools import partial
import math

import jax
import jax.numpy as jnp
from jax import lax
from jax.sharding import PartitionSpec as P

HD = 128
LAT_CH = 16


norm_eps = 1e-06


def with_halo(cells, sides, width):
    for axis, dim in sides:
        count = lax.axis_size(axis)
        ends = count - 1
        head = lax.slice_in_dim(cells, 0, width, axis=dim)
        tail = lax.slice_in_dim(cells, cells.shape[dim] - width, cells.shape[dim], axis=dim)
        cells = jnp.concatenate(
            [
                lax.ppermute(tail, axis, [(i, (i + 1) % count) for i in range(ends)]),
                cells,
                lax.ppermute(head, axis, [((i + 1) % count, i) for i in range(ends)]),
            ],
            axis=dim,
        )
    return cells


def attend_block(query_rows, keys_all, values_all):
    scores = jnp.einsum(
        "qhd,khd->hqk", query_rows, keys_all, preferred_element_type=jnp.float32
    ) * (1.0 / math.sqrt(HD))
    peak = jnp.max(scores, axis=2, keepdims=True)
    exponent_vals = jnp.exp(scores - peak)
    totals = jnp.sum(exponent_vals, axis=2)
    weights = exponent_vals.astype(jnp.bfloat16)
    mixed = jnp.einsum("hqk,khd->qhd", weights, values_all, preferred_element_type=jnp.float32)
    mixed = mixed / jnp.transpose(totals)[:, :, None]
    return mixed.astype(jnp.bfloat16).reshape(query_rows.shape[0], -1)


def decode_block(padded, conv_weight, conv_bias, frame_count, row_count, col_count):
    channels, videos, frames_all, rows_pad, cols_pad = padded.shape
    flat = padded.reshape(channels, -1)
    total = flat.shape[1]
    reach = 2 * rows_pad * cols_pad + 2 * cols_pad + 2
    flat = jnp.pad(flat, ((0, 0), (0, reach)))
    pieces = []
    for time_off in range(3):
        for row_off in range(3):
            for col_off in range(3):
                offset = (time_off * rows_pad + row_off) * cols_pad + col_off
                pieces.append(flat[:, offset : offset + total])
    stacked = jnp.concatenate(pieces, axis=0)
    conv_out = (
        lax.dot_general(
            stacked, conv_weight, (((0,), (0,)), ((), ())), preferred_element_type=jnp.float32
        )
        + conv_bias
    )
    normed = conv_out / jnp.sqrt(jnp.mean(conv_out * conv_out, axis=1, keepdims=True) + norm_eps)
    result = jax.nn.silu(normed).astype(jnp.bfloat16)
    result = result.reshape(videos, frames_all, rows_pad, cols_pad, conv_weight.shape[1])
    return result[:, :frame_count, :row_count, :col_count, :]


def on_device(
    query,
    key_states,
    value_states,
    latent,
    sigma,
    head_weight,
    latent_scale,
    latent_shift,
    frame_tail,
    conv_weight,
    conv_bias,
):
    features = query.shape[4]
    q_all, k_all, v_all = (
        lax.all_to_all(query, "seq", split_axis=4, concat_axis=1, tiled=True),
        lax.all_to_all(key_states, "seq", split_axis=4, concat_axis=1, tiled=True),
        lax.all_to_all(value_states, "seq", split_axis=4, concat_axis=1, tiled=True),
    )
    token_count = q_all.shape[1] * q_all.shape[2] * q_all.shape[3]
    head_count = q_all.shape[4] // HD
    block_rows = 512
    query_blocks = q_all.reshape(token_count // block_rows, block_rows, head_count, HD)
    keys_all = k_all.reshape(token_count, head_count, HD)
    values_all = v_all.reshape(token_count, head_count, HD)
    attended = lax.map(
        partial(attend_block, keys_all=keys_all, values_all=values_all), query_blocks
    )
    attended = attended.reshape(token_count, head_count * HD)
    own_rows = lax.all_to_all(
        attended.reshape(q_all.shape), "seq", split_axis=1, concat_axis=4, tiled=True
    )
    own_flat = own_rows.reshape(-1, features)
    widened = own_flat.astype(jnp.float32)
    mean_sq = jnp.mean(widened * widened, axis=1)
    projected = jnp.dot(own_flat, head_weight, preferred_element_type=jnp.float32)
    velocity = projected / jnp.sqrt(mean_sq + norm_eps)[:, None]
    patch_ch = head_weight.shape[1]
    cleaned = latent.reshape(-1, patch_ch) - sigma[0] * velocity
    scaled = (cleaned.reshape(-1, 4, LAT_CH) * latent_scale + latent_shift).astype(jnp.bfloat16)
    row_local = latent.shape[1]
    frame_count = latent.shape[2]
    col_tokens = latent.shape[3]
    by_column = scaled.reshape(row_local, frame_count, col_tokens, 2, 2, LAT_CH).transpose(
        2, 4, 1, 0, 3, 5
    )
    by_column = by_column.reshape(1, 2 * col_tokens, frame_count * row_local * 2 * LAT_CH)
    tiles = lax.all_to_all(by_column, "grp", split_axis=1, concat_axis=0, tiled=True)
    video_count = tiles.shape[0]
    col_local = tiles.shape[1]
    image = tiles.reshape(video_count, col_local, frame_count, row_local, 2, LAT_CH).transpose(
        5, 0, 2, 3, 4, 1
    )
    image = image.reshape(LAT_CH, video_count, frame_count, 2 * row_local, col_local)
    cached = jnp.transpose(frame_tail, (4, 0, 1, 2, 3))
    window = jnp.concatenate([cached, image], axis=2)
    padded = with_halo(window, (("seq", 3), ("grp", 4)), 1)
    return decode_block(padded, conv_weight, conv_bias, frame_count, 2 * row_local, col_local)


def solution(mesh):
    return jax.shard_map(
        on_device,
        mesh=mesh,
        in_specs=(
            P("grp", "seq", None, None, None),
            P("grp", "seq", None, None, None),
            P("grp", "seq", None, None, None),
            P("grp", "seq", None, None, None),
            P("grp"),
            P(),
            P(),
            P(),
            P(None, None, "seq", "grp", None),
            P(),
            P(),
        ),
        out_specs=P(None, None, "seq", "grp", None),
        check_vma=False,
    )
```

profile of v0, /device:TPU:1, one launch (start us, length us, event | category | flops | bytes accessed | tf_op | source)
XLA Modules:
  0.0 238.1 jit_solution(7186794413638402468)
XLA Ops:
  0.0 6.1 %copy.87 = bf16[1,1,4,24,4096]{3,2,1,0,4:T(4,128)(2,1)} copy(bf16[1,1,4,24,4096]{4,3,2,1,0:T(8,128)(2,1)} %param.13) | data formatting | bytes 1572864 | tf_op args[0]
  6.1 11.7 %reshape.126 = bf16[32,2,6144]{2,1,0:T(2,128)(2,1)} reshape(bf16[4096,1,1,4,24]{4,3,2,1,0:T(4,128)(2,1)} %bitcast.95) | data formatting | bytes 1572864
  17.8 10.4 %all-to-all-start = ((bf16[32,2,6144]{2,1,0:T(2,128)(2,1)}), bf16[32,2,6144]{2,1,0:T(2,128)(2,1)S(1)}, u32[]{:S(2)}, u32[]{:S(2)}) async-start(bf16[32,2,6144]{2,1,0:T(2,128)(2,1)} %reshape.126), calls=%async_computation | async-start | bytes 1572864 | tf_op jit(solution)/shard_map/all_to_all | solution.py:86
  28.3 4.6 %copy.90 = bf16[1,1,4,24,4096]{3,2,1,0,4:T(4,128)(2,1)} copy(bf16[1,1,4,24,4096]{4,3,2,1,0:T(8,128)(2,1)S(1)} %copy-done.1) | data formatting | bytes 1572864 | tf_op args[1]
  32.9 11.7 %reshape.128 = bf16[32,2,6144]{2,1,0:T(2,128)(2,1)} reshape(bf16[4096,1,1,4,24]{4,3,2,1,0:T(4,128)(2,1)} %bitcast.96) | data formatting | bytes 1572864
  44.6 7.5 %all-to-all-start.1 = ((bf16[32,2,6144]{2,1,0:T(2,128)(2,1)}), bf16[32,2,6144]{2,1,0:T(2,128)(2,1)S(1)}, u32[]{:S(2)}, u32[]{:S(2)}) async-start(bf16[32,2,6144]{2,1,0:T(2,128)(2,1)} %reshape.128), calls=%async_computation.1 | async-start | bytes 1572864 | tf_op jit(solution)/shard_map/all_to_all | solution.py:87
  52.1 4.6 %copy.93 = bf16[1,1,4,24,4096]{3,2,1,0,4:T(4,128)(2,1)} copy(bf16[1,1,4,24,4096]{4,3,2,1,0:T(8,128)(2,1)S(1)} %copy-done.2) | data formatting | bytes 1572864 | tf_op args[2]
  56.7 11.6 %reshape.130 = bf16[32,2,6144]{2,1,0:T(2,128)(2,1)} reshape(bf16[4096,1,1,4,24]{4,3,2,1,0:T(4,128)(2,1)} %bitcast.97) | data formatting | bytes 1572864
  68.3 7.4 %all-to-all-start.2 = ((bf16[32,2,6144]{2,1,0:T(2,128)(2,1)}), bf16[32,2,6144]{2,1,0:T(2,128)(2,1)S(1)}, u32[]{:S(2)}, u32[]{:S(2)}) async-start(bf16[32,2,6144]{2,1,0:T(2,128)(2,1)} %reshape.130), calls=%async_computation.2 | async-start | bytes 1572864 | tf_op jit(solution)/shard_map/all_to_all | solution.py:88
  75.7 6.9 %reshape.127 = bf16[4096,1,1,4,24]{4,3,2,1,0:T(4,128)(2,1)} reshape(bf16[32,2,6144]{2,1,0:T(2,128)(2,1)S(1)} %all-to-all-done) | data formatting | bytes 1572864
  82.7 4.6 %copy.104 = bf16[1,1,4,24,32,128]{5,4,3,2,1,0:T(8,128)(2,1)S(1)} copy(bf16[1,1,4,24,32,128]{3,2,5,4,1,0:T(4,128)(2,1)} %bitcast.92) | data formatting | bytes 1572864 | tf_op jit(solution)/shard_map/all_to_all | solution.py:86
  87.3 1.2 copy.89
  88.5 6.9 %reshape.129 = bf16[4096,1,1,4,24]{4,3,2,1,0:T(4,128)(2,1)} reshape(bf16[32,2,6144]{2,1,0:T(2,128)(2,1)S(1)} %all-to-all-done.1) | data formatting | bytes 1572864
  95.4 4.6 %copy.105 = bf16[1,1,4,24,32,128]{5,4,3,2,1,0:T(8,128)(2,1)S(1)} copy(bf16[1,1,4,24,32,128]{3,2,5,4,1,0:T(4,128)(2,1)} %bitcast.93) | data formatting | bytes 1572864 | tf_op jit(solution)/shard_map/all_to_all | solution.py:87
  100.0 0.3 copy.92
  100.4 6.9 %reshape.131 = bf16[4096,1,1,4,24]{4,3,2,1,0:T(4,128)(2,1)} reshape(bf16[32,2,6144]{2,1,0:T(2,128)(2,1)S(1)} %all-to-all-done.2) | data formatting | bytes 1572864
  107.3 4.6 %copy.106 = bf16[1,1,4,24,32,128]{5,4,3,2,1,0:T(8,128)(2,1)S(1)} copy(bf16[1,1,4,24,32,128]{3,2,5,4,1,0:T(4,128)(2,1)} %bitcast.94) | data formatting | bytes 1572864 | tf_op jit(solution)/shard_map/all_to_all | solution.py:88
  112.2 29.8 %while.10 = (s32[]{:T(128)}, bf16[6,512,128]{2,1,0:T(8,128)(2,1)}, bf16[6,512,1,128]{3,1,2,0:T(8,128)(2,1)}, bf16[3072,1,128]{2,0,1:T(8,128)(2,1)S(1)}, bf16[3072,1,128]{2,0,1:T(8,128)(2,1)S(1)}, /*index=5*/s32[]{:T(128)}) while((s32[]{:T(128)}, bf16[6,512,128]{2,1,0:T(8,128)(2,1)}, bf16[6,512,1,128]{3,1,2,0:T(8,128)(2,1)}, ...), condition=%wide.region_3.4_spmd, body=%wide.region_0.3_spmd.sunk | while | flops 818019328 | bytes 20719700 | solution.py:96
  112.2 2.0 multiply_reduce_fusion.4
  114.2 1.2 fusion.44
  115.4 1.9 fusion.45
  117.2 2.0 multiply_reduce_fusion.4
  119.2 1.2 fusion.44
  120.4 1.8 fusion.45
  122.2 2.0 multiply_reduce_fusion.4
  124.1 1.2 fusion.44
  125.3 1.8 fusion.45
  127.1 2.0 multiply_reduce_fusion.4
  129.1 1.2 fusion.44
  130.3 1.8 fusion.45
  132.1 2.0 multiply_reduce_fusion.4
  134.0 1.2 fusion.44
  135.2 1.8 fusion.45
  137.0 2.0 multiply_reduce_fusion.4
  139.0 1.2 fusion.44
  140.2 1.8 fusion.45
  142.0 7.5 %all-to-all-start.3 = ((bf16[1,32,4,24,128]{4,3,2,0,1:T(8,128)(2,1)}), bf16[1,32,4,24,128]{4,3,2,0,1:T(8,128)(2,1)S(1)}, u32[]{:S(2)}, u32[]{:S(2)}) async-start(bf16[1,32,4,24,128]{4,3,2,0,1:T(8,128)(2,1)} %bitcast.110), calls=%async_computation.3 | async-start | bytes 1572864 | tf_op jit(solution)/shard_map/all_to_all | solution.py:100
  150.3 13.5 %all-to-all-done.3 = bf16[1,32,4,24,128]{4,3,2,0,1:T(8,128)(2,1)S(1)} async-done(((bf16[1,32,4,24,128]{4,3,2,0,1:T(8,128)(2,1)}), bf16[1,32,4,24,128]{4,3,2,0,1:T(8,128)(2,1)S(1)}, u32[]{:S(2)}, u32[]{:S(2)}) %all-to-all-start.3) | async-done | bytes 786464 | tf_op jit(solution)/shard_map/all_to_all | solution.py:100
  164.1 0.3 copy.97
  164.4 0.4 fusion.29
  165.4 0.5 broadcast.72
  165.9 0.7 reduce.7
  166.6 0.7 reshape.132
  167.3 12.9 %all-to-all-start.4 = ((bf16[16,2,192]{2,1,0:T(2,128)(2,1)}), bf16[16,2,192]{2,1,0:T(2,128)(2,1)S(1)}, u32[]{:S(2)}, u32[]{:S(2)}) async-start(bf16[16,2,192]{2,1,0:T(2,128)(2,1)} %reshape.132), calls=%async_computation.4 | async-start | bytes 32768 | tf_op jit(solution)/shard_map/all_to_all | solution.py:118
  180.3 11.3 %all-to-all-done.4 = bf16[16,2,192]{2,1,0:T(2,128)(2,1)S(1)} async-done(((bf16[16,2,192]{2,1,0:T(2,128)(2,1)}), bf16[16,2,192]{2,1,0:T(2,128)(2,1)S(1)}, u32[]{:S(2)}, u32[]{:S(2)}) %all-to-all-start.4) | async-done | bytes 12320 | tf_op jit(solution)/shard_map/all_to_all | solution.py:118
  192.2 4.0 %collective-permute-start = (bf16[16,16,6,1,3]{0,3,2,4,1:T(2,128)(2,1)S(1)}, bf16[16,16,6,1,3]{0,3,2,4,1:T(2,128)(2,1)S(1)}, u32[]{:S(2)}, u32[]{:S(2)}) collective-permute-start(bf16[16,16,6,1,3]{0,3,2,4,1:T(2,128)(2,1)S(1)} %get-tuple-element.103), channel_id=1, source_target_pairs={{0,16},{16,32},{32,48},{48,64},{64,80},{80,96},{96,112},{112,128},... | collective-permute-start | bytes 27656 | tf_op jit(solution)/shard_map/ppermute | solution.py:24
  196.3 2.1 collective-permute-start.1
  198.4 4.3 %collective-permute-done.1 = bf16[16,16,6,1,3]{0,3,2,4,1:T(2,128)(2,1)S(1)} collective-permute-done((bf16[16,16,6,1,3]{0,3,2,4,1:T(2,128)(2,1)S(1)}, bf16[16,16,6,1,3]{0,3,2,4,1:T(2,128)(2,1)S(1)}, u32[]{:S(2)}, u32[]{:S(2)}) %collective-permute-start.1) | collective-permute-done | bytes 9248 | tf_op jit(solution)/shard_map/ppermute | solution.py:26
  202.7 0.4 pad_maximum_fusion.5
  203.1 2.3 collective-permute-start.2
  205.4 1.3 collective-permute-start.3
  206.7 0.3 collective-permute-done.2
  207.0 3.7 %collective-permute-done.3 = bf16[16,16,6,4,1]{0,3,2,4,1:T(4,128)(2,1)S(1)} collective-permute-done((bf16[16,16,6,4,1]{0,3,2,4,1:T(4,128)(2,1)S(1)}, bf16[16,16,6,4,1]{0,3,2,4,1:T(4,128)(2,1)S(1)}, u32[]{:S(2)}, u32[]{:S(2)}) %collective-permute-start.3) | collective-permute-done | bytes 12320 | tf_op jit(solution)/shard_map/ppermute | solution.py:26
  210.8 0.7 pad_maximum_fusion
  211.7 0.3 reshape.122
  212.0 2.1 pad_slice_fusion.2
  214.1 2.5 %pad_slice_fusion.1 = (bf16[16,1920]{0,1:T(8,128)(2,1)}, bf16[16,1920]{0,1:T(8,128)(2,1)}, bf16[16,1920]{0,1:T(8,128)(2,1)}, bf16[16,1920]{0,1:T(8,128)(2,1)}, b...) fusion(bf16[16,1920]{0,1:T(8,128)(2,1)S(1)} %reshape.122), kind=kLoop, calls=%fused_computation.43 | loop fusion | bytes 614400 | tf_op jit(solution)/shard_map/slice | solution.py:57
  216.6 2.5 %pad_slice_fusion = (bf16[16,1920]{0,1:T(8,128)(2,1)}, bf16[16,1920]{0,1:T(8,128)(2,1)}, bf16[16,1920]{0,1:T(8,128)(2,1)}, bf16[16,1920]{0,1:T(8,128)(2,1)}, bf1...) fusion(bf16[16,1920]{0,1:T(8,128)(2,1)S(1)} %reshape.122), kind=kLoop, calls=%fused_computation.42 | loop fusion | bytes 614400 | tf_op jit(solution)/shard_map/slice | solution.py:57
  219.1 11.2 %concatenate.15 = bf16[432,1920]{0,1:T(8,128)(2,1)S(1)} concatenate(bf16[16,1920]{0,1:T(8,128)(2,1)S(1)} %reshape.122, bf16[16,1920]{0,1:T(8,128)(2,1)} %get-tuple-element.100, bf16[16,1920]{0,1:T(8,128)(2,1)} %get-tuple-element.76, bf16[16,1920]{0,1:T(8,128)(2,1)} %get-tuple-element.77, bf16[16,1920]{0,1:T(8,128)(2,1)} %get-tuple-element.78, ...), dimensions={0} | concatenate | bytes 3317760 | tf_op jit(solution)/shard_map/concatenate | solution.py:58
  230.4 2.3 multiply_reduce_fusion.1
  232.7 1.0 multiply_convert_fusion
  233.7 2.2 reshape.123
  235.8 1.3 slice.127
  237.1 1.0 copy.103
  (37 shorter events, 2.0 us)
Async XLA Ops:
  0.0 164.4 %copy-start = (bf16[4096,64]{0,1:T(8,128)(2,1)S(1)}, bf16[4096,64]{0,1:T(8,128)(2,1)}, u32[]{:S(2)}) copy-start(bf16[4096,64]{0,1:T(8,128)(2,1)} %param.18) | copy-start | bytes 1572868
  6.1 22.2 %copy-start.1 = (bf16[1,1,4,24,4096]{4,3,2,1,0:T(8,128)(2,1)S(1)}, bf16[1,1,4,24,4096]{4,3,2,1,0:T(8,128)(2,1)}, u32[]{:S(2)}) copy-start(bf16[1,1,4,24,4096]{4,3,2,1,0:T(8,128)(2,1)} %param.14) | copy-start | bytes 2359300
  17.8 26.8 %all-to-all-start = ((bf16[32,2,6144]{2,1,0:T(2,128)(2,1)}), bf16[32,2,6144]{2,1,0:T(2,128)(2,1)S(1)}, u32[]{:S(2)}, u32[]{:S(2)}) async-start(bf16[32,2,6144]{2,1,0:T(2,128)(2,1)} %reshape.126), calls=%async_computation | async-start | bytes 1572864 | tf_op jit(solution)/shard_map/all_to_all | solution.py:86
  32.9 19.2 %copy-start.2 = (bf16[1,1,4,24,4096]{4,3,2,1,0:T(8,128)(2,1)S(1)}, bf16[1,1,4,24,4096]{4,3,2,1,0:T(8,128)(2,1)}, u32[]{:S(2)}) copy-start(bf16[1,1,4,24,4096]{4,3,2,1,0:T(8,128)(2,1)} %param.15) | copy-start | bytes 2359300
  44.6 23.8 %all-to-all-start.1 = ((bf16[32,2,6144]{2,1,0:T(2,128)(2,1)}), bf16[32,2,6144]{2,1,0:T(2,128)(2,1)S(1)}, u32[]{:S(2)}, u32[]{:S(2)}) async-start(bf16[32,2,6144]{2,1,0:T(2,128)(2,1)} %reshape.128), calls=%async_computation.1 | async-start | bytes 1572864 | tf_op jit(solution)/shard_map/all_to_all | solution.py:87
  68.3 32.0 %all-to-all-start.2 = ((bf16[32,2,6144]{2,1,0:T(2,128)(2,1)}), bf16[32,2,6144]{2,1,0:T(2,128)(2,1)S(1)}, u32[]{:S(2)}, u32[]{:S(2)}) async-start(bf16[32,2,6144]{2,1,0:T(2,128)(2,1)} %reshape.130), calls=%async_computation.2 | async-start | bytes 1572864 | tf_op jit(solution)/shard_map/all_to_all | solution.py:88
  112.2 38.0 %copy-start.3 = (f32[1,1,4,24,64]{4,3,2,1,0:T(8,128)S(1)}, f32[1,1,4,24,64]{4,3,2,1,0:T(8,128)}, u32[]{:S(2)}) copy-start(f32[1,1,4,24,64]{4,3,2,1,0:T(8,128)} %param.16) | copy-start | bytes 73732
  142.0 23.0 %copy-start.5 = (f32[16]{0:T(128)S(1)}, f32[16]{0:T(128)}, u32[]{:S(2)}) copy-start(f32[16]{0:T(128)} %param.20) | copy-start | bytes 196
  142.0 23.0 %copy-start.6 = (f32[16]{0:T(128)S(1)}, f32[16]{0:T(128)}, u32[]{:S(2)}) copy-start(f32[16]{0:T(128)} %param.19) | copy-start | bytes 196
  142.0 38.2 %copy-start.4 = (bf16[16,2,2,3,16]{4,2,3,1,0:T(2,128)(2,1)S(1)}, bf16[16,2,2,3,16]{4,2,3,1,0:T(2,128)(2,1)}, u32[]{:S(2)}) copy-start(bf16[16,2,2,3,16]{4,2,3,1,0:T(2,128)(2,1)} %param.21) | copy-start | bytes 18436
  142.0 21.8 %all-to-all-start.3 = ((bf16[1,32,4,24,128]{4,3,2,0,1:T(8,128)(2,1)}), bf16[1,32,4,24,128]{4,3,2,0,1:T(8,128)(2,1)S(1)}, u32[]{:S(2)}, u32[]{:S(2)}) async-start(bf16[1,32,4,24,128]{4,3,2,0,1:T(8,128)(2,1)} %bitcast.110), calls=%async_computation.3 | async-start | bytes 1572864 | tf_op jit(solution)/shard_map/all_to_all | solution.py:100
  167.3 24.3 %all-to-all-start.4 = ((bf16[16,2,192]{2,1,0:T(2,128)(2,1)}), bf16[16,2,192]{2,1,0:T(2,128)(2,1)S(1)}, u32[]{:S(2)}, u32[]{:S(2)}) async-start(bf16[16,2,192]{2,1,0:T(2,128)(2,1)} %reshape.132), calls=%async_computation.4 | async-start | bytes 32768 | tf_op jit(solution)/shard_map/all_to_all | solution.py:118
  192.2 6.2 %collective-permute-start = (bf16[16,16,6,1,3]{0,3,2,4,1:T(2,128)(2,1)S(1)}, bf16[16,16,6,1,3]{0,3,2,4,1:T(2,128)(2,1)S(1)}, u32[]{:S(2)}, u32[]{:S(2)}) collective-permute-start(bf16[16,16,6,1,3]{0,3,2,4,1:T(2,128)(2,1)S(1)} %get-tuple-element.103), channel_id=1, source_target_pairs={{0,16},{16,32},{32,48},{48,64},{64,80},{80,96},{96,112},{112,128},... | collective-permute-start | bytes 27656 | tf_op jit(solution)/shard_map/ppermute | solution.py:24
  196.3 6.5 %collective-permute-start.1 = (bf16[16,16,6,1,3]{0,3,2,4,1:T(2,128)(2,1)S(1)}, bf16[16,16,6,1,3]{0,3,2,4,1:T(2,128)(2,1)S(1)}, u32[]{:S(2)}, u32[]{:S(2)}) collective-permute-start(bf16[16,16,6,1,3]{0,3,2,4,1:T(2,128)(2,1)S(1)} %get-tuple-element.104), channel_id=1, source_target_pairs={{16,0},{32,16},{48,32},{64,48},{80,64},{96,80},{112,96},{128,112},... | collective-permute-start | bytes 27656 | tf_op jit(solution)/shard_map/ppermute | solution.py:26
  203.1 3.9 %collective-permute-start.2 = (bf16[16,16,6,4,1]{0,3,2,4,1:T(4,128)(2,1)S(1)}, bf16[16,16,6,4,1]{0,3,2,4,1:T(4,128)(2,1)S(1)}, u32[]{:S(2)}, u32[]{:S(2)}) collective-permute-start(bf16[16,16,6,4,1]{0,3,2,4,1:T(4,128)(2,1)S(1)} %get-tuple-element.101), channel_id=1, source_target_pairs={{0,1},{1,2},{2,3},{3,4},{4,5},{5,6},{6,7},{7,8},{8,9},{9,10},{10,1... | collective-permute-start | bytes 36872 | tf_op jit(solution)/shard_map/ppermute | solution.py:24
  205.4 5.4 %collective-permute-start.3 = (bf16[16,16,6,4,1]{0,3,2,4,1:T(4,128)(2,1)S(1)}, bf16[16,16,6,4,1]{0,3,2,4,1:T(4,128)(2,1)S(1)}, u32[]{:S(2)}, u32[]{:S(2)}) collective-permute-start(bf16[16,16,6,4,1]{0,3,2,4,1:T(4,128)(2,1)S(1)} %get-tuple-element.102), channel_id=1, source_target_pairs={{1,0},{2,1},{3,2},{4,3},{5,4},{6,5},{7,6},{8,7},{9,8},{10,9},{11,1... | collective-permute-start | bytes 36872 | tf_op jit(solution)/shard_map/ppermute | solution.py:26
  219.1 11.3 %copy-start.7 = (f32[384]{0:T(512)S(1)}, f32[384]{0:T(512)}, u32[]{:S(2)}) copy-start(f32[384]{0:T(512)} %param.23) | copy-start | bytes 4612
where the time goes:
time: 240 us; the launch traced here: 238 us
  local copies, waits for them, and re-layouts  112 us (47%)
  starting transfers between devices  55.5 us (23%)
  waiting for transfers between devices  33.2 us (14%)
  matrix products  25.5 us (11%)
  other arithmetic  10.5 us (4%)
    unnamed x29, local copies, waits for them, and re-layouts  72.5 us
    all_to_all x1, waiting for transfers between devices, on_device(): lax.all_to_all(attended.reshape(q_all.shape), 'seq', split_axis=1, concat...  13.5 us
    all_to_all x1, starting transfers between devices, on_device(): lax.all_to_all(by_column, 'grp', split_axis=1, concat_axis=0, tiled=True)  12.9 us
    dot_general x6, matrix products, attend_block(): jnp.einsum('qhd,khd->hqk', query_rows, keys_all, preferred_element_type=j...  11.8 us
    all_to_all x1, waiting for transfers between devices, on_device(): lax.all_to_all(by_column, 'grp', split_axis=1, concat_axis=0, tiled=True)  11.3 us
    concatenate x1, local copies, waits for them, and re-layouts, decode_block(): stacked = jnp.concatenate(pieces, axis=0)  11.2 us
    dot_general x6, matrix products, attend_block(): jnp.einsum('hqk,khd->qhd', weights, values_all, preferred_element_type=jn...  11 us
    all_to_all x1, starting transfers between devices, on_device(): lax.all_to_all(query, 'seq', split_axis=4, concat_axis=1, tiled=True)  10.4 us
  transfers between devices with their start and end apart: 9, of which 5 were waited for; matrix products, arithmetic and copies ran while one was open for 24% of the time, Pallas kernels for 0%

commit v1 on v0

v1 whole, which is shorter than its diff:
```python
import functools
import math

import jax
import jax.numpy as jnp
import numpy as np
from jax import lax
from jax.experimental import pallas as pl
from jax.experimental.pallas import tpu as pltpu
from jax.sharding import PartitionSpec as P

HD = 128
LAT_CH = 16
NORM_EPS = 1e-06
F32 = jnp.float32
BF16 = jnp.bfloat16
VMEM = pltpu.VMEM
SIDE = 2 * LAT_CH


def dot_nt(a, b):
    return lax.dot_general(a, b, (((1,), (1,)), ((), ())), preferred_element_type=F32)


def dot_nn(a, b):
    return jnp.dot(a, b, preferred_element_type=F32)


def pack_kernel(q_ref, k_ref, v_ref, o_ref):
    rows = q_ref.shape[0]
    for place, ref in enumerate((q_ref, k_ref, v_ref)):
        for head in range(o_ref.shape[0]):
            o_ref[head, place * rows : (place + 1) * rows, :] = ref[:, head * HD : (head + 1) * HD]


def pack_heads(query, keys, values, heads, steps=4):
    rows, features = query.shape
    width = features // steps
    spec = pl.BlockSpec((rows, width), lambda i: (0, i))
    return pl.pallas_call(
        pack_kernel,
        grid=(steps,),
        in_specs=[spec] * 3,
        out_specs=pl.BlockSpec((heads // steps, 3 * rows, HD), lambda i: (i, 0, 0)),
        out_shape=jax.ShapeDtypeStruct((heads, 3 * rows, HD), BF16),
        name="pack_heads",
    )(query, keys, values)


def attend_kernel(block_tr, x_ref, w_ref, o_ref, kt, vx, s_even, s_odd, mx_even, mx_odd, vel, ssq):
    tr, rows3, _ = x_ref.shape
    rows = rows3 // 3
    tokens = tr * rows
    block = block_tr * rows
    steps = tr // block_tr
    factor = math.log2(math.e) / math.sqrt(HD)
    for r in range(tr):
        at = slice(r * rows, (r + 1) * rows)
        vx[at, :HD] = x_ref[r, 2 * rows :, :]
        vx[at, HD:] = jnp.ones((rows, HD), BF16)
    for c in range(0, tr, 4):
        keys = x_ref[c : c + 4, rows : 2 * rows, :].reshape(4 * rows, HD)
        flipped = keys.astype(F32).T.astype(BF16)
        at = slice(c * rows, (c + 4) * rows)
        kt[:HD, at] = flipped
        kt[HD:, at] = flipped
    ssq[...] = jnp.zeros_like(ssq)

    chunk = 512

    def score(step, s_ref, mx_ref):
        q = x_ref[pl.ds(step * block_tr, block_tr), :rows, :].reshape(block, HD)
        q = q.astype(F32) * factor
        high = q.astype(BF16)
        low = (q - high.astype(F32)).astype(BF16)
        both = jnp.concatenate([high, low], axis=1)
        peak = None
        for c in range(0, tokens, chunk):
            s = dot_nn(both, kt[:, c : c + chunk])
            s_ref[:, c : c + chunk] = s
            for l in range(0, chunk, HD):
                part = s[:, l : l + HD]
                peak = part if peak is None else jnp.maximum(peak, part)
        mx_ref[...] = jnp.broadcast_to(jnp.max(peak, axis=1, keepdims=True), mx_ref.shape)

    def mix(step, s_ref, mx_ref):
        peak = mx_ref[...]
        weights = jnp.concatenate(
            [
                jnp.exp2(s_ref[:, l : l + HD] - peak).astype(BF16)
                for l in range(0, tokens, HD)
            ],
            axis=1,
        )
        mixed = dot_nn(weights, vx[...])
        att = (mixed[:, :HD] / mixed[:, HD:]).astype(BF16)
        vel[pl.ds(pl.multiple_of(step * block, block), block), :] = dot_nn(att, w_ref[...])
        wide = att.astype(F32)
        squares = (wide * wide).astype(BF16)
        ones = jnp.ones((16, HD), BF16)
        for r in range(block_tr):
            total = dot_nt(ones, squares[r * rows : (r + 1) * rows, :])
            ssq[step * block_tr + r, :, :rows] = total

    score(0, s_even, mx_even)

    @pl.loop(0, steps // 2 - 1)
    def _(i):
        score(2 * i + 1, s_odd, mx_odd)
        mix(2 * i, s_even, mx_even)
        score(2 * i + 2, s_even, mx_even)
        mix(2 * i + 1, s_odd, mx_odd)

    score(steps - 1, s_odd, mx_odd)
    mix(steps - 2, s_even, mx_even)
    mix(steps - 1, s_odd, mx_odd)

    lane = lax.broadcasted_iota(jnp.int32, (rows, HD), 1)
    line = lax.broadcasted_iota(jnp.int32, (16, HD), 0)
    for r in range(tr):
        up, down = (r - 1) % tr, (r + 1) % tr
        piece = [vel[t * rows : (t + 1) * rows, :] for t in (up, r, down)]
        merged = jnp.where(lane < SIDE, piece[0], jnp.where(lane < 3 * SIDE, piece[1], piece[2]))
        o_ref[r, :rows, :] = merged.astype(BF16)
        merged = jnp.where(line == 0, ssq[up], jnp.where(line == 1, ssq[r], ssq[down]))
        o_ref[r, rows:, :] = merged.astype(BF16)


def attend(x, w, block_tr=4):
    tr, rows3, _ = x.shape
    rows = rows3 // 3
    tokens, block = tr * rows, block_tr * rows
    return pl.pallas_call(
        functools.partial(attend_kernel, block_tr),
        in_specs=[pl.BlockSpec(memory_space=VMEM)] * 2,
        out_specs=pl.BlockSpec(memory_space=VMEM),
        out_shape=jax.ShapeDtypeStruct((tr, rows + 16, HD), BF16),
        scratch_shapes=[
            VMEM((2 * HD, tokens), BF16),
            VMEM((tokens, 2 * HD), BF16),
            VMEM((block, tokens), F32),
            VMEM((block, tokens), F32),
            VMEM((block, HD), F32),
            VMEM((block, HD), F32),
            VMEM((tokens, HD), F32),
            VMEM((tr, 16, HD), F32),
        ],
        compiler_params=pltpu.CompilerParams(vmem_limit_bytes=48 << 20),
        cost_estimate=pl.CostEstimate(
            flops=8 * tokens * tokens * HD, bytes_accessed=4 << 20, transcendentals=tokens * tokens
        ),
        name="attend",
    )(x, w)


def update_kernel(features, bands, index_ref, sigma_ref, y_ref, lat_ref, gain_ref, shift_ref, o_ref):
    heads, lines, _ = y_ref.shape
    rows = lines - 16
    frames = 4
    cols = rows // frames
    total = y_ref[0].astype(F32)
    for h in range(1, heads):
        total = total + y_ref[h].astype(F32)
    velocity = total[:rows]
    sums = jnp.concatenate([total[rows:], jnp.zeros((HD - 16, HD), F32)], axis=0).T
    lane = lax.broadcasted_iota(jnp.int32, (rows, HD), 1)
    up, own, down = (jnp.broadcast_to(sums[:rows, i : i + 1], (rows, HD)) for i in range(3))
    square = jnp.where(lane < SIDE, up, jnp.where(lane < 3 * SIDE, own, down))
    velocity = velocity / jnp.sqrt(square * (1.0 / features) + NORM_EPS)
    cleaned = lat_ref[...] - sigma_ref[0] * velocity
    scaled = cleaned * gain_ref[...] + shift_ref[...]
    first, last = index_ref[0] == 0, index_ref[0] == heads - 1
    drop = ((lane < SIDE) & first) | ((lane >= 3 * SIDE) & last)
    scaled = jnp.where(drop, 0.0, scaled).astype(BF16)
    count = bands * 4 * frames
    at = lax.broadcasted_iota(jnp.int32, (count, rows), 0)
    source = lax.broadcasted_iota(jnp.int32, (count, rows), 1)
    band, frame, t = at // (4 * frames), (at // 4) % frames, at % 4
    column = (3 * band + 1) // 2 - 1 + t
    hit = (source == frame * cols + column) & (column >= 0) & (column < cols)
    chosen = jnp.where(hit, 1.0, 0.0).astype(BF16)
    o_ref[...] = dot_nn(chosen, scaled).astype(BF16).reshape(o_ref.shape)


def update(index, sigma, y, lat, gain, shift, features, bands):
    smem = pl.BlockSpec(memory_space=pltpu.SMEM)
    vmem = pl.BlockSpec(memory_space=VMEM)
    return pl.pallas_call(
        functools.partial(update_kernel, features, bands),
        in_specs=[smem, smem] + [vmem] * 4,
        out_specs=vmem,
        out_shape=jax.ShapeDtypeStruct((bands, 16, HD), BF16),
        compiler_params=pltpu.CompilerParams(vmem_limit_bytes=16 << 20),
        name="update",
    )(index, sigma, y, lat, gain, shift)


STARTS = (((0, 1), (1, 0), (1, 1)), ((0, 0), (0, 1), (1, 0)))


def taps_kernel(w_ref, o_ref):
    out = w_ref.shape[1]
    o_ref[...] = jnp.zeros_like(o_ref)
    for kind, start in enumerate(STARTS):
        for tf in range(3):
            for ti in range(3):
                for tj, (token, b) in enumerate(start):
                    tap = ((tf * 3 + ti) * 3 + tj) * LAT_CH
                    piece = w_ref[tap : tap + LAT_CH, :]
                    for i in range(2):
                        at = tf * 2 * HD + token * HD + (i + ti) * SIDE + b * LAT_CH
                        o_ref[kind, at : at + LAT_CH, i * out : (i + 1) * out] = piece


def spread_taps(conv_weight):
    out = conv_weight.shape[1]
    return pl.pallas_call(
        taps_kernel,
        in_specs=[pl.BlockSpec(memory_space=VMEM)],
        out_specs=pl.BlockSpec(memory_space=VMEM),
        out_shape=jax.ShapeDtypeStruct((2, 6 * HD, 2 * out), BF16),
        compiler_params=pltpu.CompilerParams(vmem_limit_bytes=16 << 20),
        name="spread_taps",
    )(conv_weight)


def conv_kernel(index_ref, z_ref, cached_ref, taps_ref, bias_ref, o_ref):
    videos, lines, _ = z_ref.shape
    frames = lines // 4
    out = bias_ref.shape[1]
    odd = index_ref[0] % 2
    count = videos * frames
    at = lax.broadcasted_iota(jnp.int32, (3 * count, videos * lines), 0)
    source = lax.broadcasted_iota(jnp.int32, (3 * count, videos * lines), 1)
    t, frame, video = at // count, (at // videos) % frames, at % videos
    chosen = jnp.where(source == video * lines + frame * 4 + t, 1.0, 0.0).astype(BF16)
    image = dot_nn(chosen, z_ref[...].reshape(videos * lines, HD)).astype(BF16)
    token = [
        jnp.concatenate([cached_ref[t], image[t * count : (t + 1) * count]], axis=0)
        for t in range(3)
    ]

    def windows(first, second):
        wide = jnp.concatenate([first, second], axis=1)
        return jnp.concatenate([wide[tf * videos : tf * videos + count] for tf in range(3)], axis=1)

    middle = jnp.where(odd == 1, windows(token[0], token[1]), windows(token[1], token[2]))
    outer = jnp.concatenate([windows(token[0], token[1]), windows(token[1], token[2])], axis=0)
    outer = dot_nn(outer, taps_ref[odd])
    inner = dot_nn(middle, taps_ref[1 - odd])
    for i in range(2):
        done = []
        for part in (outer[:count], inner, outer[count:]):
            conv = part[:, i * out : (i + 1) * out] + bias_ref[...]
            mean_sq = jnp.mean(conv * conv, axis=1, keepdims=True)
            normed = conv / jnp.sqrt(mean_sq + NORM_EPS)
            done.append(normed / (1.0 + jnp.exp(-normed)))
        for f in range(frames):
            at = slice(f * videos, (f + 1) * videos)
            tile = jnp.concatenate([d[at][:, None, :] for d in done], axis=1)
            o_ref[:, f, i] = tile.astype(BF16)


def convolve(index, z, cached, taps, bias):
    videos, lines, _ = z.shape
    out = bias.shape[1]
    vmem = pl.BlockSpec(memory_space=VMEM)
    return pl.pallas_call(
        conv_kernel,
        in_specs=[pl.BlockSpec(memory_space=pltpu.SMEM)] + [vmem] * 4,
        out_specs=vmem,
        out_shape=jax.ShapeDtypeStruct((videos, lines // 4, 2, 3, out), BF16),
        compiler_params=pltpu.CompilerParams(vmem_limit_bytes=32 << 20),
        name="convolve",
    )(index, z, cached, taps, bias)


def neighbours(head, tail, axis):
    count = lax.axis_size(axis)
    before = lax.ppermute(tail, axis, [(i, i + 1) for i in range(count - 1)])
    after = lax.ppermute(head, axis, [(i + 1, i) for i in range(count - 1)])
    return before, after


def on_device(
    query,
    key_states,
    value_states,
    latent,
    sigma,
    head_weight,
    latent_scale,
    latent_shift,
    frame_tail,
    conv_weight,
    conv_bias,
):
    features = query.shape[4]
    heads = features // HD
    frames, cols = latent.shape[2], latent.shape[3]
    rows = frames * cols
    bands = lax.axis_size("grp")
    seq_at, grp_at = lax.axis_index("seq"), lax.axis_index("grp")
    videos, tail_frames = frame_tail.shape[0], frame_tail.shape[1]

    sent = pack_heads(
        query.reshape(rows, features),
        key_states.reshape(rows, features),
        value_states.reshape(rows, features),
        heads,
    )
    mine = lax.all_to_all(sent, "seq", 0, 0, tiled=True)

    lat = latent.reshape(rows, 4 * LAT_CH)
    cached = jnp.transpose(frame_tail, (0, 1, 3, 2, 4))
    flat = (videos * tail_frames * frame_tail.shape[3] * LAT_CH // SIDE, SIDE)
    top = jnp.concatenate([lat[:, :SIDE], cached[:, :, :, 0].astype(F32).reshape(flat)], axis=0)
    low = jnp.concatenate([lat[:, SIDE:], cached[:, :, :, -1].astype(F32).reshape(flat)], axis=0)
    above, below = neighbours(top, low, "seq")
    lat = jnp.concatenate([above[:rows], lat, below[:rows]], axis=1)
    above, below = (
        side[rows:].astype(BF16).reshape(cached[:, :, :, :1].shape) for side in (above, below)
    )
    cached = jnp.concatenate([above, cached, below], axis=3)
    left, right = neighbours(cached[:, :, :1], cached[:, :, -1:], "grp")
    cached = jnp.concatenate([left, cached, right], axis=2)
    none = jnp.zeros_like(left)
    cached = jnp.where(
        grp_at % 2 == 0,
        jnp.concatenate([none, cached], axis=2),
        jnp.concatenate([cached, none], axis=2),
    )
    cached = cached.reshape(videos, tail_frames, 3, 2, 4, LAT_CH).transpose(2, 1, 0, 4, 3, 5)
    cached = cached.reshape(3, tail_frames * videos, HD)

    taps = spread_taps(conv_weight)
    w = lax.dynamic_slice_in_dim(head_weight, seq_at * HD, HD, axis=0)
    w = jnp.concatenate([w[:, SIDE:], w, w[:, :SIDE]], axis=1)
    gain = jnp.tile(latent_scale, HD // LAT_CH).reshape(1, HD)
    shift = jnp.tile(latent_shift, HD // LAT_CH).reshape(1, HD)

    parts = lax.all_to_all(attend(mine, w), "seq", 0, 0, tiled=True)
    bands_out = update(seq_at.reshape(1), sigma, parts, lat, gain, shift, features, bands)
    tiles = lax.all_to_all(bands_out, "grp", 0, 0, tiled=True)
    return convolve(grp_at.reshape(1), tiles, cached, taps, conv_bias.reshape(1, -1))


def solution(mesh):
    return jax.shard_map(
        on_device,
        mesh=mesh,
        in_specs=(
            P("grp", "seq", None, None, None),
            P("grp", "seq", None, None, None),
            P("grp", "seq", None, None, None),
            P("grp", "seq", None, None, None),
            P("grp"),
            P(),
            P(),
            P(),
            P(None, None, "seq", "grp", None),
            P(),
            P(),
        ),
        out_specs=P(None, None, "seq", "grp", None),
        check_vma=False,
    )
```

time: 240 us -> 118 us (0.49)
  local copies, waits for them, and re-layouts: 112 us -> 3.07 us
  Pallas kernels: 0 us -> 27.5 us
  matrix products: 25.5 us -> 0 us
  starting transfers between devices: 55.5 us -> 41.3 us
  waiting for transfers between devices: 33.2 us -> 42.4 us
  other arithmetic: 10.5 us -> 1.98 us
    unnamed x29 -> x17, local copies, waits for them, and re-layouts: 72.5 us -> 1.06 us
    pallas_call x0 -> x5, Pallas kernels: none -> 27.5 us  [the longest x1 20.7 us: attend(): pl.pallas_call(functools.partial(attend_kernel, block_tr), in_specs=[pl.B...]
    dot_general x14 -> x0, matrix products: 25.5 us -> none  [the longest x6 11.8 us: attend_block(): jnp.einsum('qhd,khd->hqk', query_rows, keys_all, preferred_element_type=j...]
    all_to_all x5 -> x3, starting transfers between devices: 45.8 us -> 29.7 us  [the longest x1 12.8 us: on_device(): tiles = lax.all_to_all(bands_out, 'grp', 0, 0, tiled=True)]
    all_to_all x8 -> x0, local copies, waits for them, and re-layouts: 16 us -> none  [the longest x2 5.81 us: on_device(): lax.all_to_all(query, 'seq', split_axis=4, concat_axis=1, tiled=True)]
    concatenate x2 -> x0, local copies, waits for them, and re-layouts: 11.4 us -> none  [the longest x1 11.2 us: decode_block(): stacked = jnp.concatenate(pieces, axis=0)]
    all_to_all x5 -> x3, waiting for transfers between devices: 24.8 us -> 36.1 us  [the longest x1 30.4 us: on_device(): mine = lax.all_to_all(sent, 'seq', 0, 0, tiled=True)]
    slice x5 -> x6, local copies, waits for them, and re-layouts: 9.37 us -> 0.18 us  [the longest x1 0.09 us: on_device(): w = jnp.concatenate([w[:, SIDE:], w, w[:, :SIDE]], axis=1)]
  transfers between devices with their start and end apart: 9 -> 7, of which waited for: 5 -> 5; matrix products, arithmetic and copies ran while one was open for 24% -> 3% of each run, Pallas kernels for 0% -> 0%
where the time goes in v1:
time: 118 us; the launch traced here: 117 us
  waiting for transfers between devices  42.4 us (36%)
  starting transfers between devices  41.3 us (35%)
  Pallas kernels  27.5 us (23%)
  local copies, waits for them, and re-layouts  3.07 us (3%)
  other arithmetic  1.98 us (2%)
    all_to_all x1, waiting for transfers between devices, on_device(): mine = lax.all_to_all(sent, 'seq', 0, 0, tiled=True)  30.4 us
    pallas_call x1, Pallas kernels, attend(): pl.pallas_call(functools.partial(attend_kernel, block_tr), in_specs=[pl.B...  20.7 us
    all_to_all x1, starting transfers between devices, on_device(): tiles = lax.all_to_all(bands_out, 'grp', 0, 0, tiled=True)  12.8 us
    all_to_all x1, starting transfers between devices, on_device(): mine = lax.all_to_all(sent, 'seq', 0, 0, tiled=True)  10.6 us
    ppermute x2, starting transfers between devices, neighbours(): before = lax.ppermute(tail, axis, [(i, i + 1) for i in range(count - 1)])  8.08 us
    all_to_all x1, starting transfers between devices, on_device(): parts = lax.all_to_all(attend(mine, w), 'seq', 0, 0, tiled=True)  6.33 us
    ppermute x2, waiting for transfers between devices, neighbours(): after = lax.ppermute(head, axis, [(i + 1, i) for i in range(count - 1)])  6.14 us
    pallas_call x1, Pallas kernels, pack_heads(): pl.pallas_call(pack_kernel, grid=(steps,), in_specs=[spec] * 3, out_specs...  4.12 us
  transfers between devices with their start and end apart: 7, of which 5 were waited for; matrix products, arithmetic and copies ran while one was open for 3% of the time, Pallas kernels for 0%

profile of v1, /device:TPU:1, one launch (start us, length us, event | category | flops | bytes accessed | tf_op | source)
XLA Modules:
  0.0 117.2 jit_solution(7045642790281927878)
XLA Ops:
  0.0 0.0 copy-start
  0.0 4.1 %pack_heads.1 = bf16[32,288,128]{2,1,0:T(8,128)(2,1)} custom-call(bf16[96,4096]{1,0:T(8,128)(2,1)} %bitcast.11, bf16[96,4096]{1,0:T(8,128)(2,1)} %bitcast.12, bf16[96,4096]{1,0:T(8,128)(2,1)} %bitcast.13), custom_call_target="tpu_custom_call" | custom-call | tf_op jit(solution)/shard_map/pack_heads/pallas_call | solution.py:40
  4.1 10.6 %all-to-all-start = ((bf16[32,288,128]{2,1,0:T(8,128)(2,1)}), bf16[32,288,128]{2,1,0:T(8,128)(2,1)S(1)}, u32[]{:S(2)}, u32[]{:S(2)}) async-start(bf16[32,288,128]{2,1,0:T(8,128)(2,1)} %pack_heads.1), calls=%async_computation | async-start | bytes 4718592 | tf_op jit(solution)/shard_map/all_to_all | solution.py:312
  14.7 0.0 copy-done
  14.8 0.1 copy.38
  14.9 0.1 fusion.3
  15.0 0.1 pad_maximum_fusion.6.w_ref
  15.1 0.0 copy-start.3
  15.1 0.0 copy-start.4
  15.1 30.4 %all-to-all-done.x_ref = bf16[32,288,128]{2,1,0:T(8,128)(2,1)S(1)} async-done(((bf16[32,288,128]{2,1,0:T(8,128)(2,1)}), bf16[32,288,128]{2,1,0:T(8,128)(2,1)S(1)}, u32[]{:S(2)}, u32[]{:S(2)}) %all-to-all-start) | async-done | bytes 2359328 | tf_op jit(solution)/shard_map/all_to_all | solution.py:312
  45.5 20.7 %attend.1 = bf16[32,112,128]{2,1,0:T(8,128)(2,1)S(1)} custom-call(bf16[32,288,128]{2,1,0:T(8,128)(2,1)S(1)} %all-to-all-done.x_ref, bf16[128,128]{1,0:T(8,128)(2,1)S(1)} %pad_maximum_fusion.6.w_ref), custom_call_target="tpu_custom_call" | custom-call | flops 9663676416 | bytes 4194304 | tf_op jit(solution)/shard_map/attend/pallas_call | solution.py:133
  66.2 0.0 copy-start.1
  66.2 0.9 copy-done.1
  67.2 0.0 copy-start.6
  67.2 0.0 copy-start.7
  67.2 0.0 copy-start.2
  67.2 6.3 %all-to-all-start.1 = ((bf16[32,112,128]{2,1,0:T(8,128)(2,1)}), bf16[32,112,128]{2,1,0:T(8,128)(2,1)S(1)}, u32[]{:S(2)}, u32[]{:S(2)}) async-start(bf16[32,112,128]{2,1,0:T(8,128)(2,1)} %copy-done.1), calls=%async_computation.1 | async-start | bytes 1835008 | tf_op jit(solution)/shard_map/all_to_all | solution.py:342
  73.5 0.0 copy-done.3
  73.5 0.3 fusion.1
  73.8 0.1 reshape.56
  73.9 0.0 copy-done.4
  73.9 0.1 fusion.2
  74.0 2.3 %collective-permute-start.1 = (f32[144,32]{1,0:T(8,128)S(1)}, f32[144,32]{1,0:T(8,128)S(1)}, u32[]{:S(2)}, u32[]{:S(2)}) collective-permute-start(f32[144,32]{1,0:T(8,128)S(1)} %pad_maximum_fusion.1), channel_id=1, source_target_pairs={{16,0},{32,16},{48,32},{64,48},{80,64},{96,80},{112,96},{128,112},... | collective-permute-start | bytes 55304 | tf_op jit(solution)/shard_map/ppermute | solution.py:281
  76.3 0.1 reshape.55
  76.4 0.0 copy-start.5
  76.4 3.5 %collective-permute-start = (f32[144,32]{1,0:T(8,128)S(1)}, f32[144,32]{1,0:T(8,128)S(1)}, u32[]{:S(2)}, u32[]{:S(2)}) collective-permute-start(f32[144,32]{1,0:T(8,128)S(1)} %pad_maximum_fusion), channel_id=1, source_target_pairs={{0,16},{16,32},{32,48},{48,64},{64,80},{80,96},{96,112},{112,128},... | collective-permute-start | bytes 55304 | tf_op jit(solution)/shard_map/ppermute | solution.py:280
  80.5 0.0 copy-done.6
  80.5 0.1 reshape_tile.6.gain_ref
  80.6 0.0 copy-done.7
  80.6 0.1 reshape_tile.7.shift_ref
  80.7 6.1 %collective-permute-done.1 = f32[144,32]{1,0:T(8,128)S(1)} collective-permute-done((f32[144,32]{1,0:T(8,128)S(1)}, f32[144,32]{1,0:T(8,128)S(1)}, u32[]{:S(2)}, u32[]{:S(2)}) %collective-permute-start.1) | collective-permute-done | bytes 18464 | tf_op jit(solution)/shard_map/ppermute | solution.py:281
  86.9 0.0 collective-permute-done
  86.9 0.1 pad_maximum_fusion.2.lat_ref
  87.0 2.4 %all-to-all-done.1.y_ref = bf16[32,112,128]{2,1,0:T(8,128)(2,1)S(1)} async-done(((bf16[32,112,128]{2,1,0:T(8,128)(2,1)}), bf16[32,112,128]{2,1,0:T(8,128)(2,1)S(1)}, u32[]{:S(2)}, u32[]{:S(2)}) %all-to-all-start.1) | async-done | bytes 917536 | tf_op jit(solution)/shard_map/all_to_all | solution.py:342
  89.4 1.1 update.1
  90.5 12.8 %all-to-all-start.2 = ((bf16[16,16,128]{2,1,0:T(8,128)(2,1)}), bf16[16,16,128]{2,1,0:T(8,128)(2,1)S(1)}, u32[]{:S(2)}, u32[]{:S(2)}) async-start(bf16[16,16,128]{2,1,0:T(8,128)(2,1)} %update.1), calls=%async_computation.2 | async-start | bytes 131072 | tf_op jit(solution)/shard_map/all_to_all | solution.py:344
  103.3 0.1 reshape.58
  103.4 0.1 reshape.57
  103.5 0.1 pad_maximum_fusion.5
  103.7 1.3 %collective-permute-start.3 = (bf16[16,2,1,4,16]{4,3,2,1,0:T(4,128)(2,1)S(1)}, bf16[16,2,1,4,16]{4,3,2,1,0:T(4,128)(2,1)S(1)}, u32[]{:S(2)}, u32[]{:S(2)}) collective-permute-start(bf16[16,2,1,4,16]{4,3,2,1,0:T(4,128)(2,1)S(1)} %get-tuple-element.8), channel_id=1, source_target_pairs={{1,0},{2,1},{3,2},{4,3},{5,4},{6,5},{7,6},{8,7},{9,8},{10,9},{11,1... | collective-permute-start | bytes 12296 | tf_op jit(solution)/shard_map/ppermute | solution.py:281
  105.0 4.6 %collective-permute-start.2 = (bf16[16,2,1,4,16]{4,3,2,1,0:T(4,128)(2,1)S(1)}, bf16[16,2,1,4,16]{4,3,2,1,0:T(4,128)(2,1)}, u32[]{:S(2)}, u32[]{:S(2)}) collective-permute-start(bf16[16,2,1,4,16]{4,3,2,1,0:T(4,128)(2,1)S(1)} %get-tuple-element.7), channel_id=1, source_target_pairs={{0,1},{1,2},{2,3},{3,4},{4,5},{5,6},{6,7},{7,8},{8,9},{9,10},{10,1... | collective-permute-start | bytes 12296 | tf_op jit(solution)/shard_map/ppermute | solution.py:280
  109.6 0.0 copy-done.2
  109.6 0.2 spread_taps.1.taps_ref
  109.8 0.0 copy-done.5
  109.8 0.0 collective-permute-done.3
  109.8 0.1 collective-permute-done.2
  110.0 1.3 %maximum_select_fusion = bf16[16,2,6,4,16]{4,3,2,1,0:T(4,128)(2,1)S(1)} fusion(bf16[16,2,1,4,16]{4,3,2,1,0:T(4,128)(2,1)S(1)} %collective-permute-done.3, bf16[16,2,3,1,16]{4,3,2,1,0:T(2,128)(2,1)S(1)} %reshape.58, bf16[16,2,3,2,16]{4,3,2,1,0:T(2,128)(2,1)S(1)} %bitcast.18, bf16[16,2,3,1,16]{4,3,2,1,0:T(2,128)(2,1)S(1)} %reshape.57, ...), kind=kLoop, calls=%fused_computation | loop fusion | flops 307200 | bytes 49153 | tf_op jit(solution)/shard_map/jit(_where)/select_n | solution.py:328
  111.3 0.2 copy.40
  111.5 0.2 reshape.53.cached_ref
  111.6 3.3 %all-to-all-done.2.z_ref = bf16[16,16,128]{2,1,0:T(8,128)(2,1)S(1)} async-done(((bf16[16,16,128]{2,1,0:T(8,128)(2,1)}), bf16[16,16,128]{2,1,0:T(8,128)(2,1)S(1)}, u32[]{:S(2)}, u32[]{:S(2)}) %all-to-all-start.2) | async-done | bytes 65568 | tf_op jit(solution)/shard_map/all_to_all | solution.py:344
  114.9 1.3 %convolve.1 = bf16[16,4,2,3,384]{4,3,2,1,0:T(4,128)(2,1)S(1)} custom-call(s32[1]{0:T(128)} %bitcast.index_ref, bf16[16,16,128]{2,1,0:T(8,128)(2,1)S(1)} %all-to-all-done.2.z_ref, bf16[3,32,128]{2,1,0:T(8,128)(2,1)S(1)} %reshape.53.cached_ref, bf16[2,768,768]{2,1,0:T(8,128)(2,1)S(1)} %spread_taps.1.taps_ref, f32[1,384]{1,0:T(1,128)S(1)} %reshape.54.bias_ref), custom_call_target="tpu_custom_call" | custom-call | tf_op jit(solution)/shard_map/convolve/pallas_call | solution.py:268
  116.2 1.0 copy.37
  (11 shorter events, 0.1 us)
Async XLA Ops:
  0.0 14.7 %copy-start = (bf16[4096,64]{0,1:T(8,128)(2,1)S(1)}, bf16[4096,64]{0,1:T(8,128)(2,1)}, u32[]{:S(2)}) copy-start(bf16[4096,64]{0,1:T(8,128)(2,1)} %param.16) | copy-start | bytes 1572868
  4.1 41.4 %all-to-all-start = ((bf16[32,288,128]{2,1,0:T(8,128)(2,1)}), bf16[32,288,128]{2,1,0:T(8,128)(2,1)S(1)}, u32[]{:S(2)}, u32[]{:S(2)}) async-start(bf16[32,288,128]{2,1,0:T(8,128)(2,1)} %pack_heads.1), calls=%async_computation | async-start | bytes 4718592 | tf_op jit(solution)/shard_map/all_to_all | solution.py:312
  15.1 58.4 %copy-start.3 = (bf16[16,2,2,3,16]{4,2,3,1,0:T(2,128)(2,1)S(1)}, bf16[16,2,2,3,16]{4,2,3,1,0:T(2,128)(2,1)}, u32[]{:S(2)}) copy-start(bf16[16,2,2,3,16]{4,2,3,1,0:T(2,128)(2,1)} %param.19) | copy-start | bytes 18436
  15.1 58.8 %copy-start.4 = (f32[1,1,4,24,64]{4,3,2,1,0:T(8,128)S(1)}, f32[1,1,4,24,64]{4,3,2,1,0:T(8,128)}, u32[]{:S(2)}) copy-start(f32[1,1,4,24,64]{4,3,2,1,0:T(8,128)} %param.14) | copy-start | bytes 73732
  66.2 0.9 copy-start.1
  67.2 13.4 %copy-start.6 = (f32[16]{0:T(128)S(1)}, f32[16]{0:T(128)}, u32[]{:S(2)}) copy-start(f32[16]{0:T(128)} %param.17) | copy-start | bytes 196
  67.2 13.5 %copy-start.7 = (f32[16]{0:T(128)S(1)}, f32[16]{0:T(128)}, u32[]{:S(2)}) copy-start(f32[16]{0:T(128)} %param.18) | copy-start | bytes 196
  67.2 42.4 %copy-start.2 = (bf16[432,384]{1,0:T(8,128)(2,1)S(1)}, bf16[432,384]{1,0:T(8,128)(2,1)}, u32[]{:S(2)}) copy-start(bf16[432,384]{1,0:T(8,128)(2,1)} %w_ref.1) | copy-start | bytes 995332
  67.2 22.2 %all-to-all-start.1 = ((bf16[32,112,128]{2,1,0:T(8,128)(2,1)}), bf16[32,112,128]{2,1,0:T(8,128)(2,1)S(1)}, u32[]{:S(2)}, u32[]{:S(2)}) async-start(bf16[32,112,128]{2,1,0:T(8,128)(2,1)} %copy-done.1), calls=%async_computation.1 | async-start | bytes 1835008 | tf_op jit(solution)/shard_map/all_to_all | solution.py:342
  74.0 12.8 %collective-permute-start.1 = (f32[144,32]{1,0:T(8,128)S(1)}, f32[144,32]{1,0:T(8,128)S(1)}, u32[]{:S(2)}, u32[]{:S(2)}) collective-permute-start(f32[144,32]{1,0:T(8,128)S(1)} %pad_maximum_fusion.1), channel_id=1, source_target_pairs={{16,0},{32,16},{48,32},{64,48},{80,64},{96,80},{112,96},{128,112},... | collective-permute-start | bytes 55304 | tf_op jit(solution)/shard_map/ppermute | solution.py:281
  76.4 33.4 %copy-start.5 = (f32[384]{0:T(512)S(1)}, f32[384]{0:T(512)}, u32[]{:S(2)}) copy-start(f32[384]{0:T(512)} %param.21) | copy-start | bytes 4612
  76.4 10.5 %collective-permute-start = (f32[144,32]{1,0:T(8,128)S(1)}, f32[144,32]{1,0:T(8,128)S(1)}, u32[]{:S(2)}, u32[]{:S(2)}) collective-permute-start(f32[144,32]{1,0:T(8,128)S(1)} %pad_maximum_fusion), channel_id=1, source_target_pairs={{0,16},{16,32},{32,48},{48,64},{64,80},{80,96},{96,112},{112,128},... | collective-permute-start | bytes 55304 | tf_op jit(solution)/shard_map/ppermute | solution.py:280
  90.5 24.4 %all-to-all-start.2 = ((bf16[16,16,128]{2,1,0:T(8,128)(2,1)}), bf16[16,16,128]{2,1,0:T(8,128)(2,1)S(1)}, u32[]{:S(2)}, u32[]{:S(2)}) async-start(bf16[16,16,128]{2,1,0:T(8,128)(2,1)} %update.1), calls=%async_computation.2 | async-start | bytes 131072 | tf_op jit(solution)/shard_map/all_to_all | solution.py:344
  103.7 6.2 %collective-permute-start.3 = (bf16[16,2,1,4,16]{4,3,2,1,0:T(4,128)(2,1)S(1)}, bf16[16,2,1,4,16]{4,3,2,1,0:T(4,128)(2,1)S(1)}, u32[]{:S(2)}, u32[]{:S(2)}) collective-permute-start(bf16[16,2,1,4,16]{4,3,2,1,0:T(4,128)(2,1)S(1)} %get-tuple-element.8), channel_id=1, source_target_pairs={{1,0},{2,1},{3,2},{4,3},{5,4},{6,5},{7,6},{8,7},{9,8},{10,9},{11,1... | collective-permute-start | bytes 12296 | tf_op jit(solution)/shard_map/ppermute | solution.py:281
  105.0 5.0 %collective-permute-start.2 = (bf16[16,2,1,4,16]{4,3,2,1,0:T(4,128)(2,1)S(1)}, bf16[16,2,1,4,16]{4,3,2,1,0:T(4,128)(2,1)}, u32[]{:S(2)}, u32[]{:S(2)}) collective-permute-start(bf16[16,2,1,4,16]{4,3,2,1,0:T(4,128)(2,1)S(1)} %get-tuple-element.7), channel_id=1, source_target_pairs={{0,1},{1,2},{2,3},{3,4},{4,5},{5,6},{6,7},{7,8},{8,9},{9,10},{10,1... | collective-permute-start | bytes 12296 | tf_op jit(solution)/shard_map/ppermute | solution.py:280

commit v2 on v1

--- a/solution.py
+++ b/solution.py
@@ -33,7 +33,7 @@
             o_ref[head, place * rows : (place + 1) * rows, :] = ref[:, head * HD : (head + 1) * HD]
 
 
-def pack_heads(query, keys, values, heads, steps=4):
+def pack_heads(query, keys, values, heads, steps=2):
     rows, features = query.shape
     width = features // steps
     spec = pl.BlockSpec((rows, width), lambda i: (0, i))
@@ -47,44 +47,44 @@
     )(query, keys, values)
 
 
-def attend_kernel(block_tr, x_ref, w_ref, o_ref, kt, vx, s_even, s_odd, mx_even, mx_odd, vel, ssq):
+def attend_kernel(block, x_ref, w_ref, o_ref, qq, kk, vx, att, ssq, *buffers):
     tr, rows3, _ = x_ref.shape
     rows = rows3 // 3
     tokens = tr * rows
-    block = block_tr * rows
-    steps = tr // block_tr
+    steps = tokens // block
     factor = math.log2(math.e) / math.sqrt(HD)
     for r in range(tr):
         at = slice(r * rows, (r + 1) * rows)
+        q = x_ref[r, :rows, :].astype(F32) * factor
+        high = q.astype(BF16)
+        qq[at, :HD] = high
+        qq[at, HD:] = (q - high.astype(F32)).astype(BF16)
         vx[at, :HD] = x_ref[r, 2 * rows :, :]
         vx[at, HD:] = jnp.ones((rows, HD), BF16)
     for c in range(0, tr, 4):
         keys = x_ref[c : c + 4, rows : 2 * rows, :].reshape(4 * rows, HD)
         flipped = keys.astype(F32).T.astype(BF16)
         at = slice(c * rows, (c + 4) * rows)
-        kt[:HD, at] = flipped
-        kt[HD:, at] = flipped
-    ssq[...] = jnp.zeros_like(ssq)
+        kk[:HD, at] = flipped
+        kk[HD:, at] = flipped
 
     chunk = 512
 
-    def score(step, s_ref, mx_ref):
-        q = x_ref[pl.ds(step * block_tr, block_tr), :rows, :].reshape(block, HD)
-        q = q.astype(F32) * factor
-        high = q.astype(BF16)
-        low = (q - high.astype(F32)).astype(BF16)
-        both = jnp.concatenate([high, low], axis=1)
+    def score(step):
+        s_ref, peak_ref = buffers[step % 2], buffers[2 + step % 2]
+        q = qq[step * block : (step + 1) * block, :]
         peak = None
         for c in range(0, tokens, chunk):
-            s = dot_nn(both, kt[:, c : c + chunk])
+            s = dot_nn(q, kk[:, c : c + chunk])
             s_ref[:, c : c + chunk] = s
             for l in range(0, chunk, HD):
                 part = s[:, l : l + HD]
                 peak = part if peak is None else jnp.maximum(peak, part)
-        mx_ref[...] = jnp.broadcast_to(jnp.max(peak, axis=1, keepdims=True), mx_ref.shape)
-
-    def mix(step, s_ref, mx_ref):
-        peak = mx_ref[...]
+        peak_ref[...] = jnp.broadcast_to(jnp.max(peak, axis=1, keepdims=True), peak_ref.shape)
+
+    def mix(step):
+        s_ref, peak_ref = buffers[step % 2], buffers[2 + step % 2]
+        peak = peak_ref[...]
         weights = jnp.concatenate(
             [
                 jnp.exp2(s_ref[:, l : l + HD] - peak).astype(BF16)
@@ -93,59 +93,52 @@
             axis=1,
         )
         mixed = dot_nn(weights, vx[...])
-        att = (mixed[:, :HD] / mixed[:, HD:]).astype(BF16)
-        vel[pl.ds(pl.multiple_of(step * block, block), block), :] = dot_nn(att, w_ref[...])
-        wide = att.astype(F32)
-        squares = (wide * wide).astype(BF16)
-        ones = jnp.ones((16, HD), BF16)
-        for r in range(block_tr):
-            total = dot_nt(ones, squares[r * rows : (r + 1) * rows, :])
-            ssq[step * block_tr + r, :, :rows] = total
-
-    score(0, s_even, mx_even)
-
-    @pl.loop(0, steps // 2 - 1)
-    def _(i):
-        score(2 * i + 1, s_odd, mx_odd)
-        mix(2 * i, s_even, mx_even)
-        score(2 * i + 2, s_even, mx_even)
-        mix(2 * i + 1, s_odd, mx_odd)
-
-    score(steps - 1, s_odd, mx_odd)
-    mix(steps - 2, s_even, mx_even)
-    mix(steps - 1, s_odd, mx_odd)
-
+        att[step * block : (step + 1) * block, :] = (mixed[:, :HD] / mixed[:, HD:]).astype(BF16)
+
+    score(0)
+    for step in range(1, steps):
+        score(step)
+        mix(step - 1)
+    mix(steps - 1)
+
+    ssq[...] = jnp.zeros_like(ssq)
+    ones = jnp.ones((16, HD), BF16)
+    velocity = dot_nn(att[...], w_ref[...])
+    for r in range(tr):
+        wide = att[r * rows : (r + 1) * rows, :].astype(F32)
+        ssq[r, :, :rows] = dot_nt(ones, (wide * wide).astype(BF16))
     lane = lax.broadcasted_iota(jnp.int32, (rows, HD), 1)
     line = lax.broadcasted_iota(jnp.int32, (16, HD), 0)
     for r in range(tr):
         up, down = (r - 1) % tr, (r + 1) % tr
-        piece = [vel[t * rows : (t + 1) * rows, :] for t in (up, r, down)]
+        piece = [velocity[t * rows : (t + 1) * rows, :] for t in (up, r, down)]
         merged = jnp.where(lane < SIDE, piece[0], jnp.where(lane < 3 * SIDE, piece[1], piece[2]))
         o_ref[r, :rows, :] = merged.astype(BF16)
         merged = jnp.where(line == 0, ssq[up], jnp.where(line == 1, ssq[r], ssq[down]))
         o_ref[r, rows:, :] = merged.astype(BF16)
 
 
-def attend(x, w, block_tr=4):
+def attend(x, w, block=384):
     tr, rows3, _ = x.shape
     rows = rows3 // 3
-    tokens, block = tr * rows, block_tr * rows
-    return pl.pallas_call(
-        functools.partial(attend_kernel, block_tr),
+    tokens = tr * rows
+    return pl.pallas_call(
+        functools.partial(attend_kernel, block),
         in_specs=[pl.BlockSpec(memory_space=VMEM)] * 2,
         out_specs=pl.BlockSpec(memory_space=VMEM),
         out_shape=jax.ShapeDtypeStruct((tr, rows + 16, HD), BF16),
         scratch_shapes=[
+            VMEM((tokens, 2 * HD), BF16),
             VMEM((2 * HD, tokens), BF16),
             VMEM((tokens, 2 * HD), BF16),
+            VMEM((tokens, HD), BF16),
+            VMEM((tr, 16, HD), F32),
             VMEM((block, tokens), F32),
             VMEM((block, tokens), F32),
             VMEM((block, HD), F32),
             VMEM((block, HD), F32),
-            VMEM((tokens, HD), F32),
-            VMEM((tr, 16, HD), F32),
         ],
-        compiler_params=pltpu.CompilerParams(vmem_limit_bytes=48 << 20),
+        compiler_params=pltpu.CompilerParams(vmem_limit_bytes=44 << 20),
         cost_estimate=pl.CostEstimate(
             flops=8 * tokens * tokens * HD, bytes_accessed=4 << 20, transcendentals=tokens * tokens
         ),
@@ -248,9 +241,9 @@
     outer = jnp.concatenate([windows(token[0], token[1]), windows(token[1], token[2])], axis=0)
     outer = dot_nn(outer, taps_ref[odd])
     inner = dot_nn(middle, taps_ref[1 - odd])
-    for i in range(2):
+    for j, part in enumerate((outer[:count], inner, outer[count:])):
         done = []
-        for part in (outer[:count], inner, outer[count:]):
+        for i in range(2):
             conv = part[:, i * out : (i + 1) * out] + bias_ref[...]
             mean_sq = jnp.mean(conv * conv, axis=1, keepdims=True)
             normed = conv / jnp.sqrt(mean_sq + NORM_EPS)
@@ -258,7 +251,7 @@
         for f in range(frames):
             at = slice(f * videos, (f + 1) * videos)
             tile = jnp.concatenate([d[at][:, None, :] for d in done], axis=1)
-            o_ref[:, f, i] = tile.astype(BF16)
+            o_ref[:, f, j] = tile.astype(BF16)
 
 
 def convolve(index, z, cached, taps, bias):
@@ -269,10 +262,10 @@
         conv_kernel,
         in_specs=[pl.BlockSpec(memory_space=pltpu.SMEM)] + [vmem] * 4,
         out_specs=vmem,
-        out_shape=jax.ShapeDtypeStruct((videos, lines // 4, 2, 3, out), BF16),
+        out_shape=jax.ShapeDtypeStruct((videos, lines // 4, 3, 2, out), BF16),
         compiler_params=pltpu.CompilerParams(vmem_limit_bytes=32 << 20),
         name="convolve",
-    )(index, z, cached, taps, bias)
+    )(index, z, cached, taps, bias).transpose(0, 1, 3, 2, 4)
 
 
 def neighbours(head, tail, axis):
@@ -339,10 +332,16 @@
     gain = jnp.tile(latent_scale, HD // LAT_CH).reshape(1, HD)
     shift = jnp.tile(latent_shift, HD // LAT_CH).reshape(1, HD)
 
+    bias = conv_bias.reshape(1, -1)
+    seq_at, grp_at = seq_at.reshape(1), grp_at.reshape(1)
+    mine, w, lat, cached, taps, gain, shift, bias, sigma, seq_at, grp_at = lax.optimization_barrier(
+        (mine, w, lat, cached, taps, gain, shift, bias, sigma, seq_at, grp_at)
+    )
+
     parts = lax.all_to_all(attend(mine, w), "seq", 0, 0, tiled=True)
-    bands_out = update(seq_at.reshape(1), sigma, parts, lat, gain, shift, features, bands)
+    bands_out = update(seq_at, sigma, parts, lat, gain, shift, features, bands)
     tiles = lax.all_to_all(bands_out, "grp", 0, 0, tiled=True)
-    return convolve(grp_at.reshape(1), tiles, cached, taps, conv_bias.reshape(1, -1))
+    return convolve(grp_at, tiles, cached, taps, bias)
 
 
 def solution(mesh):

time: 118 us -> 122 us (1.034)
  blocking collectives: 0 us -> 26 us
  starting transfers between devices: 41.3 us -> 29.7 us
  Pallas kernels: 27.5 us -> 20.3 us
  waiting for transfers between devices: 42.4 us -> 37.7 us
  local copies, waits for them, and re-layouts: 3.07 us -> 5.25 us
    all_to_all x1, waiting for transfers between devices: 30.4 us -> 0.01 us  [on_device(): mine = lax.all_to_all(sent, 'seq', 0, 0, tiled=True)]
    all_to_all x0 -> x1, blocking collectives: none -> 26 us  [on_device(): tiles = lax.all_to_all(bands_out, 'grp', 0, 0, tiled=True)]
    ppermute x2, waiting for transfers between devices: 0.13 us -> 19.9 us  [neighbours(): before = lax.ppermute(tail, axis, [(i, i + 1) for i in range(count - 1)])]
    all_to_all x1 -> x0, starting transfers between devices: 12.8 us -> none  [on_device(): tiles = lax.all_to_all(bands_out, 'grp', 0, 0, tiled=True)]
    all_to_all x1, waiting for transfers between devices: 2.4 us -> 15.2 us  [on_device(): parts = lax.all_to_all(attend(mine, w), 'seq', 0, 0, tiled=True)]
    pallas_call x1, Pallas kernels: 20.7 us -> 13.5 us  [attend(): pl.pallas_call(functools.partial(attend_kernel, block), in_specs=[pl.Bloc...]
    all_to_all x1, starting transfers between devices: 6.33 us -> 10.2 us  [on_device(): parts = lax.all_to_all(attend(mine, w), 'seq', 0, 0, tiled=True)]
    ppermute x2, waiting for transfers between devices: 6.14 us -> 2.59 us  [neighbours(): after = lax.ppermute(head, axis, [(i + 1, i) for i in range(count - 1)])]
  transfers between devices with their start and end apart: 7 -> 6, of which waited for: 5 -> 4; matrix products, arithmetic and copies ran while one was open for 3% -> 4% of each run, Pallas kernels for 0% -> 0%
where the time goes in v2:
time: 122 us; the launch traced here: 121 us
  waiting for transfers between devices  37.7 us (31%)
  starting transfers between devices  29.7 us (24%)
  blocking collectives  26 us (21%)
  Pallas kernels  20.3 us (17%)
  local copies, waits for them, and re-layouts  5.25 us (4%)
    all_to_all x1, blocking collectives, on_device(): tiles = lax.all_to_all(bands_out, 'grp', 0, 0, tiled=True)  26 us
    ppermute x2, waiting for transfers between devices, neighbours(): before = lax.ppermute(tail, axis, [(i, i + 1) for i in range(count - 1)])  19.9 us
    all_to_all x1, waiting for transfers between devices, on_device(): parts = lax.all_to_all(attend(mine, w), 'seq', 0, 0, tiled=True)  15.2 us
    pallas_call x1, Pallas kernels, attend(): pl.pallas_call(functools.partial(attend_kernel, block), in_specs=[pl.Bloc...  13.5 us
    all_to_all x1, starting transfers between devices, on_device(): mine = lax.all_to_all(sent, 'seq', 0, 0, tiled=True)  11.4 us
    all_to_all x1, starting transfers between devices, on_device(): parts = lax.all_to_all(attend(mine, w), 'seq', 0, 0, tiled=True)  10.2 us
    ppermute x2, starting transfers between devices, neighbours(): before = lax.ppermute(tail, axis, [(i, i + 1) for i in range(count - 1)])  4.84 us
    ppermute x2, starting transfers between devices, neighbours(): after = lax.ppermute(head, axis, [(i + 1, i) for i in range(count - 1)])  3.21 us
  transfers between devices with their start and end apart: 6, of which 4 were waited for; matrix products, arithmetic and copies ran while one was open for 4% of the time, Pallas kernels for 0%

profile of v2, /device:TPU:1, one launch (start us, length us, event | category | flops | bytes accessed | tf_op | source)
XLA Modules:
  0.0 120.9 jit_solution(14223257850274844143)
XLA Ops:
  0.0 0.0 copy-start
  0.0 2.9 %pack_heads.1 = bf16[32,288,128]{2,1,0:T(8,128)(2,1)} custom-call(bf16[96,4096]{1,0:T(8,128)(2,1)} %bitcast.12, bf16[96,4096]{1,0:T(8,128)(2,1)} %bitcast.13, bf16[96,4096]{1,0:T(8,128)(2,1)} %bitcast.14), custom_call_target="tpu_custom_call" | custom-call | tf_op jit(solution)/shard_map/pack_heads/pallas_call | solution.py:40
  2.9 0.0 copy-start.3
  2.9 0.0 copy-start.4
  2.9 0.0 copy-start.2
  2.9 11.4 %all-to-all-start = ((bf16[32,288,128]{2,1,0:T(8,128)(2,1)}), bf16[32,288,128]{2,1,0:T(8,128)(2,1)}, u32[]{:S(2)}, u32[]{:S(2)}) async-start(bf16[32,288,128]{2,1,0:T(8,128)(2,1)} %pack_heads.1), calls=%async_computation | async-start | bytes 4718592 | tf_op jit(solution)/shard_map/all_to_all | solution.py:305
  14.3 0.0 copy-start.6
  14.3 0.0 copy-start.7
  14.3 0.0 copy-start.5
  14.4 0.0 copy-done.3
  14.4 0.3 fusion.1
  14.7 0.1 reshape.55
  14.8 0.0 copy-done.4
  14.8 0.1 fusion.2
  14.9 3.5 %collective-permute-start = (f32[144,32]{1,0:T(8,128)S(1)}, f32[144,32]{1,0:T(8,128)}, u32[]{:S(2)}, u32[]{:S(2)}) collective-permute-start(f32[144,32]{1,0:T(8,128)S(1)} %pad_maximum_fusion), channel_id=1, source_target_pairs={{0,16},{16,32},{32,48},{48,64},{64,80},{80,96},{96,112},{112,128},... | collective-permute-start | bytes 55304 | tf_op jit(solution)/shard_map/ppermute | solution.py:273
  18.4 0.1 reshape.56
  18.5 1.9 %collective-permute-start.1 = (f32[144,32]{1,0:T(8,128)S(1)}, f32[144,32]{1,0:T(8,128)}, u32[]{:S(2)}, u32[]{:S(2)}) collective-permute-start(f32[144,32]{1,0:T(8,128)S(1)} %pad_maximum_fusion.1), channel_id=1, source_target_pairs={{16,0},{32,16},{48,32},{64,48},{80,64},{96,80},{112,96},{128,112},... | collective-permute-start | bytes 55304 | tf_op jit(solution)/shard_map/ppermute | solution.py:274
  20.5 0.0 copy-done
  20.5 0.1 copy.34
  20.6 0.1 fusion.3
  20.7 0.1 pad_maximum_fusion.6.w_ref
  20.8 0.0 copy-done.2
  20.8 0.2 spread_taps.1.taps_ref
  21.1 0.0 copy-done.6
  21.1 0.1 reshape_tile.6.gain_ref
  21.2 0.0 copy-done.7
  21.2 0.1 reshape_tile.7.shift_ref
  21.3 0.0 copy-done.5
  21.3 19.9 %collective-permute-done = f32[144,32]{1,0:T(8,128)} collective-permute-done((f32[144,32]{1,0:T(8,128)S(1)}, f32[144,32]{1,0:T(8,128)}, u32[]{:S(2)}, u32[]{:S(2)}) %collective-permute-start) | collective-permute-done | bytes 18464 | tf_op jit(solution)/shard_map/ppermute | solution.py:273
  41.2 0.7 slice.69
  41.9 0.1 reshape.57
  42.0 0.9 collective-permute-done.1
  43.0 0.7 slice.68
  43.7 0.1 reshape.58
  43.8 0.1 pad_maximum_fusion.5
  43.9 1.3 %collective-permute-start.2 = (bf16[16,2,1,4,16]{4,3,2,1,0:T(4,128)(2,1)S(1)}, bf16[16,2,1,4,16]{4,3,2,1,0:T(4,128)(2,1)S(1)}, u32[]{:S(2)}, u32[]{:S(2)}) collective-permute-start(bf16[16,2,1,4,16]{4,3,2,1,0:T(4,128)(2,1)S(1)} %get-tuple-element.29), channel_id=1, source_target_pairs={{0,1},{1,2},{2,3},{3,4},{4,5},{5,6},{6,7},{7,8},{8,9},{9,10},{10,1... | collective-permute-start | bytes 12296 | tf_op jit(solution)/shard_map/ppermute | solution.py:273
  45.2 1.3 %collective-permute-start.3 = (bf16[16,2,1,4,16]{4,3,2,1,0:T(4,128)(2,1)S(1)}, bf16[16,2,1,4,16]{4,3,2,1,0:T(4,128)(2,1)S(1)}, u32[]{:S(2)}, u32[]{:S(2)}) collective-permute-start(bf16[16,2,1,4,16]{4,3,2,1,0:T(4,128)(2,1)S(1)} %get-tuple-element.30), channel_id=1, source_target_pairs={{1,0},{2,1},{3,2},{4,3},{5,4},{6,5},{7,6},{8,7},{9,8},{10,9},{11,1... | collective-permute-start | bytes 12296 | tf_op jit(solution)/shard_map/ppermute | solution.py:274
  46.5 0.8 slice.54
  47.4 0.8 slice.57
  48.2 0.1 pad_maximum_fusion.2.lat_ref
  48.2 0.0 collective-permute-done.2
  48.3 1.6 %collective-permute-done.3 = bf16[16,2,1,4,16]{4,3,2,1,0:T(4,128)(2,1)S(1)} collective-permute-done((bf16[16,2,1,4,16]{4,3,2,1,0:T(4,128)(2,1)S(1)}, bf16[16,2,1,4,16]{4,3,2,1,0:T(4,128)(2,1)S(1)}, u32[]{:S(2)}, u32[]{:S(2)}) %collective-permute-start.3) | collective-permute-done | bytes 4128 | tf_op jit(solution)/shard_map/ppermute | solution.py:274
  49.9 0.5 maximum_select_fusion
  50.4 0.2 copy.36
  50.6 0.2 reshape.51.cached_ref
  50.7 0.0 all-to-all-done.x_ref
  50.7 13.5 %attend.1 = bf16[32,112,128]{2,1,0:T(8,128)(2,1)S(1)} custom-call(bf16[32,288,128]{2,1,0:T(8,128)(2,1)} %all-to-all-done.x_ref, bf16[128,128]{1,0:T(8,128)(2,1)S(1)} %pad_maximum_fusion.6.w_ref), custom_call_target="tpu_custom_call" | custom-call | flops 9663676416 | bytes 4194304 | tf_op jit(solution)/shard_map/attend/pallas_call | solution.py:125
  64.2 0.0 copy-start.1
  64.2 1.0 copy-done.1
  65.2 10.2 %all-to-all-start.1 = ((bf16[32,112,128]{2,1,0:T(8,128)(2,1)}), bf16[32,112,128]{2,1,0:T(8,128)(2,1)}, u32[]{:S(2)}, u32[]{:S(2)}) async-start(bf16[32,112,128]{2,1,0:T(8,128)(2,1)} %copy-done.1), calls=%async_computation.1 | async-start | bytes 1835008 | tf_op jit(solution)/shard_map/all_to_all | solution.py:341
  76.1 15.2 %all-to-all-done.1.y_ref = bf16[32,112,128]{2,1,0:T(8,128)(2,1)} async-done(((bf16[32,112,128]{2,1,0:T(8,128)(2,1)}), bf16[32,112,128]{2,1,0:T(8,128)(2,1)}, u32[]{:S(2)}, u32[]{:S(2)}) %all-to-all-start.1) | async-done | bytes 917536 | tf_op jit(solution)/shard_map/all_to_all | solution.py:341
  91.3 1.7 %update.1 = bf16[16,16,128]{2,1,0:T(8,128)(2,1)S(1)} custom-call(s32[1]{0:T(128)} %bitcast.7.index_ref, f32[1]{0:T(128)S(6)} %copy.37.sigma_ref, bf16[32,112,128]{2,1,0:T(8,128)(2,1)} %all-to-all-done.1.y_ref, f32[96,128]{1,0:T(8,128)S(1)} %pad_maximum_fusion.2.lat_ref, f32[1,128]{1,0:T(1,128)S(1)} %reshape_tile.6.gain_ref, f32[1,128]{1,0:T(1,128)S(1)} %reshape_tile.7.shift_ref), custom_call_target="tpu_custom_call" | custom-call | tf_op jit(solution)/shard_map/update/pallas_call | solution.py:181
  92.9 26.0 %all_to_all.15.z_ref = bf16[16,16,128]{2,1,0:T(8,128)(2,1)S(1)} all-to-all(bf16[16,16,128]{2,1,0:T(8,128)(2,1)S(1)} %update.1), channel_id=1, replica_groups=mesh['seq'=32,'grp'=16] {'grp'}, dimensions={0} | all-to-all | bytes 131072 | tf_op jit(solution)/shard_map/all_to_all | solution.py:343
  118.9 2.0 %convolve.1 = bf16[16,4,3,2,384]{4,3,2,1,0:T(2,128)(2,1)} custom-call(s32[1]{0:T(128)} %bitcast.8.index_ref, bf16[16,16,128]{2,1,0:T(8,128)(2,1)S(1)} %all_to_all.15.z_ref, bf16[3,32,128]{2,1,0:T(8,128)(2,1)S(1)} %reshape.51.cached_ref, bf16[2,768,768]{2,1,0:T(8,128)(2,1)S(1)} %spread_taps.1.taps_ref, f32[1,384]{1,0:T(1,128)S(1)} %reshape.52.bias_ref), custom_call_target="tpu_custom_call" | custom-call | tf_op jit(solution)/shard_map/convolve/pallas_call | solution.py:261
  (7 shorter events, 0.1 us)
Async XLA Ops:
  0.0 20.5 %copy-start = (bf16[4096,64]{0,1:T(8,128)(2,1)S(1)}, bf16[4096,64]{0,1:T(8,128)(2,1)}, u32[]{:S(2)}) copy-start(bf16[4096,64]{0,1:T(8,128)(2,1)} %param.16) | copy-start | bytes 1572868
  2.9 11.4 %copy-start.3 = (bf16[16,2,2,3,16]{4,2,3,1,0:T(2,128)(2,1)S(1)}, bf16[16,2,2,3,16]{4,2,3,1,0:T(2,128)(2,1)}, u32[]{:S(2)}) copy-start(bf16[16,2,2,3,16]{4,2,3,1,0:T(2,128)(2,1)} %param.19) | copy-start | bytes 18436
  2.9 11.9 %copy-start.4 = (f32[1,1,4,24,64]{4,3,2,1,0:T(8,128)S(1)}, f32[1,1,4,24,64]{4,3,2,1,0:T(8,128)}, u32[]{:S(2)}) copy-start(f32[1,1,4,24,64]{4,3,2,1,0:T(8,128)} %param.14) | copy-start | bytes 73732
  2.9 17.9 %copy-start.2 = (bf16[432,384]{1,0:T(8,128)(2,1)S(1)}, bf16[432,384]{1,0:T(8,128)(2,1)}, u32[]{:S(2)}) copy-start(bf16[432,384]{1,0:T(8,128)(2,1)} %w_ref.1) | copy-start | bytes 995332
  2.9 47.8 %all-to-all-start = ((bf16[32,288,128]{2,1,0:T(8,128)(2,1)}), bf16[32,288,128]{2,1,0:T(8,128)(2,1)}, u32[]{:S(2)}, u32[]{:S(2)}) async-start(bf16[32,288,128]{2,1,0:T(8,128)(2,1)} %pack_heads.1), calls=%async_computation | async-start | bytes 4718592 | tf_op jit(solution)/shard_map/all_to_all | solution.py:305
  14.3 6.7 %copy-start.6 = (f32[16]{0:T(128)S(1)}, f32[16]{0:T(128)}, u32[]{:S(2)}) copy-start(f32[16]{0:T(128)} %param.17) | copy-start | bytes 196
  14.3 6.8 %copy-start.7 = (f32[16]{0:T(128)S(1)}, f32[16]{0:T(128)}, u32[]{:S(2)}) copy-start(f32[16]{0:T(128)} %param.18) | copy-start | bytes 196
  14.3 6.9 %copy-start.5 = (f32[384]{0:T(512)S(1)}, f32[384]{0:T(512)}, u32[]{:S(2)}) copy-start(f32[384]{0:T(512)} %param.21) | copy-start | bytes 4612
  14.9 26.3 %collective-permute-start = (f32[144,32]{1,0:T(8,128)S(1)}, f32[144,32]{1,0:T(8,128)}, u32[]{:S(2)}, u32[]{:S(2)}) collective-permute-start(f32[144,32]{1,0:T(8,128)S(1)} %pad_maximum_fusion), channel_id=1, source_target_pairs={{0,16},{16,32},{32,48},{48,64},{64,80},{80,96},{96,112},{112,128},... | collective-permute-start | bytes 55304 | tf_op jit(solution)/shard_map/ppermute | solution.py:273
  18.5 24.4 %collective-permute-start.1 = (f32[144,32]{1,0:T(8,128)S(1)}, f32[144,32]{1,0:T(8,128)}, u32[]{:S(2)}, u32[]{:S(2)}) collective-permute-start(f32[144,32]{1,0:T(8,128)S(1)} %pad_maximum_fusion.1), channel_id=1, source_target_pairs={{16,0},{32,16},{48,32},{64,48},{80,64},{96,80},{112,96},{128,112},... | collective-permute-start | bytes 55304 | tf_op jit(solution)/shard_map/ppermute | solution.py:274
  43.9 4.3 %collective-permute-start.2 = (bf16[16,2,1,4,16]{4,3,2,1,0:T(4,128)(2,1)S(1)}, bf16[16,2,1,4,16]{4,3,2,1,0:T(4,128)(2,1)S(1)}, u32[]{:S(2)}, u32[]{:S(2)}) collective-permute-start(bf16[16,2,1,4,16]{4,3,2,1,0:T(4,128)(2,1)S(1)} %get-tuple-element.29), channel_id=1, source_target_pairs={{0,1},{1,2},{2,3},{3,4},{4,5},{5,6},{6,7},{7,8},{8,9},{9,10},{10,1... | collective-permute-start | bytes 12296 | tf_op jit(solution)/shard_map/ppermute | solution.py:273
  45.2 4.7 %collective-permute-start.3 = (bf16[16,2,1,4,16]{4,3,2,1,0:T(4,128)(2,1)S(1)}, bf16[16,2,1,4,16]{4,3,2,1,0:T(4,128)(2,1)S(1)}, u32[]{:S(2)}, u32[]{:S(2)}) collective-permute-start(bf16[16,2,1,4,16]{4,3,2,1,0:T(4,128)(2,1)S(1)} %get-tuple-element.30), channel_id=1, source_target_pairs={{1,0},{2,1},{3,2},{4,3},{5,4},{6,5},{7,6},{8,7},{9,8},{10,9},{11,1... | collective-permute-start | bytes 12296 | tf_op jit(solution)/shard_map/ppermute | solution.py:274
  64.2 1.0 copy-start.1
  65.2 26.0 %all-to-all-start.1 = ((bf16[32,112,128]{2,1,0:T(8,128)(2,1)}), bf16[32,112,128]{2,1,0:T(8,128)(2,1)}, u32[]{:S(2)}, u32[]{:S(2)}) async-start(bf16[32,112,128]{2,1,0:T(8,128)(2,1)} %copy-done.1), calls=%async_computation.1 | async-start | bytes 1835008 | tf_op jit(solution)/shard_map/all_to_all | solution.py:341

commit v3 on v2

--- a/solution.py
+++ b/solution.py
@@ -47,36 +47,31 @@
     )(query, keys, values)
 
 
-def attend_kernel(block, x_ref, w_ref, o_ref, qq, kk, vx, att, ssq, *buffers):
+def attend_kernel(block_tr, x_ref, w_ref, o_ref, kk, vx, held, vel, ssq, msg, sem, *buffers):
     tr, rows3, _ = x_ref.shape
     rows = rows3 // 3
-    tokens = tr * rows
-    steps = tokens // block
+    tokens, block = tr * rows, block_tr * rows
+    steps = tr // block_tr
     factor = math.log2(math.e) / math.sqrt(HD)
-    for r in range(tr):
-        at = slice(r * rows, (r + 1) * rows)
-        q = x_ref[r, :rows, :].astype(F32) * factor
-        high = q.astype(BF16)
-        qq[at, :HD] = high
-        qq[at, HD:] = (q - high.astype(F32)).astype(BF16)
-        vx[at, :HD] = x_ref[r, 2 * rows :, :]
-        vx[at, HD:] = jnp.ones((rows, HD), BF16)
-    for c in range(0, tr, 4):
-        keys = x_ref[c : c + 4, rows : 2 * rows, :].reshape(4 * rows, HD)
-        flipped = keys.astype(F32).T.astype(BF16)
-        at = slice(c * rows, (c + 4) * rows)
-        kk[:HD, at] = flipped
-        kk[HD:, at] = flipped
-
-    chunk = 512
+    chunk_tr = 8
+    chunk = chunk_tr * rows
 
     def score(step):
         s_ref, peak_ref = buffers[step % 2], buffers[2 + step % 2]
-        q = qq[step * block : (step + 1) * block, :]
+        q = x_ref[step * block_tr : (step + 1) * block_tr, :rows, :].reshape(block, HD)
+        q = q.astype(F32) * factor
+        high = q.astype(BF16)
+        q = jnp.concatenate([high, (q - high.astype(F32)).astype(BF16)], axis=1)
         peak = None
-        for c in range(0, tokens, chunk):
-            s = dot_nn(q, kk[:, c : c + chunk])
-            s_ref[:, c : c + chunk] = s
+        for c in range(tr // chunk_tr):
+            at = slice(c * chunk, (c + 1) * chunk)
+            if step == 0:
+                keys = x_ref[c * chunk_tr : (c + 1) * chunk_tr, rows : 2 * rows, :]
+                flipped = keys.reshape(chunk, HD).astype(F32).T.astype(BF16)
+                kk[:HD, at] = flipped
+                kk[HD:, at] = flipped
+            s = dot_nn(q, kk[:, at])
+            s_ref[:, at] = s
             for l in range(0, chunk, HD):
                 part = s[:, l : l + HD]
                 peak = part if peak is None else jnp.maximum(peak, part)
@@ -93,46 +88,56 @@
             axis=1,
         )
         mixed = dot_nn(weights, vx[...])
-        att[step * block : (step + 1) * block, :] = (mixed[:, :HD] / mixed[:, HD:]).astype(BF16)
-
-    score(0)
-    for step in range(1, steps):
-        score(step)
-        mix(step - 1)
-    mix(steps - 1)
-
-    ssq[...] = jnp.zeros_like(ssq)
-    ones = jnp.ones((16, HD), BF16)
-    velocity = dot_nn(att[...], w_ref[...])
-    for r in range(tr):
-        wide = att[r * rows : (r + 1) * rows, :].astype(F32)
-        ssq[r, :, :rows] = dot_nt(ones, (wide * wide).astype(BF16))
+        held[step * block : (step + 1) * block, :] = (mixed[:, :HD] / mixed[:, HD:]).astype(BF16)
+
     lane = lax.broadcasted_iota(jnp.int32, (rows, HD), 1)
     line = lax.broadcasted_iota(jnp.int32, (16, HD), 0)
+
+    def send(r):
+        up, down = (r - 1) % tr, (r + 1) % tr
+        piece = [vel[t * rows : (t + 1) * rows, :] for t in (up, r, down)]
+        merged = jnp.where(lane < SIDE, piece[0], jnp.where(lane < 3 * SIDE, piece[1], piece[2]))
+        msg[r, :rows, :] = merged.astype(BF16)
+        merged = jnp.where(line == 0, ssq[up], jnp.where(line == 1, ssq[r], ssq[down]))
+        msg[r, rows:, :] = merged.astype(BF16)
+        pltpu.make_async_copy(msg.at[r], o_ref.at[r], sem).start()
+
+    ssq[...] = jnp.zeros_like(ssq)
+    score(0)
     for r in range(tr):
-        up, down = (r - 1) % tr, (r + 1) % tr
-        piece = [velocity[t * rows : (t + 1) * rows, :] for t in (up, r, down)]
-        merged = jnp.where(lane < SIDE, piece[0], jnp.where(lane < 3 * SIDE, piece[1], piece[2]))
-        o_ref[r, :rows, :] = merged.astype(BF16)
-        merged = jnp.where(line == 0, ssq[up], jnp.where(line == 1, ssq[r], ssq[down]))
-        o_ref[r, rows:, :] = merged.astype(BF16)
-
-
-def attend(x, w, block=384):
+        at = slice(r * rows, (r + 1) * rows)
+        vx[at, :HD] = x_ref[r, 2 * rows :, :]
+        vx[at, HD:] = jnp.ones((rows, HD), BF16)
+    for step in range(steps):
+        if step + 1 < steps:
+            score(step + 1)
+        mix(step)
+    vel[...] = dot_nn(held[...], w_ref[...])
+    for r in range(tr):
+        wide = held[r * rows : (r + 1) * rows, :].astype(F32)
+        ssq[r, :, :rows] = dot_nt(jnp.ones((16, HD), BF16), (wide * wide).astype(BF16))
+    for r in range(tr):
+        send(r)
+    pltpu.make_async_copy(msg, o_ref, sem).wait()
+
+
+def attend(x, w, block_tr=4):
     tr, rows3, _ = x.shape
     rows = rows3 // 3
-    tokens = tr * rows
-    return pl.pallas_call(
-        functools.partial(attend_kernel, block),
+    tokens, block = tr * rows, block_tr * rows
+    return pl.pallas_call(
+        functools.partial(attend_kernel, block_tr),
         in_specs=[pl.BlockSpec(memory_space=VMEM)] * 2,
-        out_specs=pl.BlockSpec(memory_space=VMEM),
+        out_specs=pl.BlockSpec(memory_space=pl.ANY),
         out_shape=jax.ShapeDtypeStruct((tr, rows + 16, HD), BF16),
         scratch_shapes=[
-            VMEM((tokens, 2 * HD), BF16),
             VMEM((2 * HD, tokens), BF16),
             VMEM((tokens, 2 * HD), BF16),
             VMEM((tokens, HD), BF16),
+            VMEM((tokens, HD), F32),
             VMEM((tr, 16, HD), F32),
+            VMEM((tr, rows + 16, HD), BF16),
+            pltpu.SemaphoreType.DMA,
             VMEM((block, tokens), F32),
             VMEM((block, tokens), F32),
             VMEM((block, HD), F32),
@@ -146,7 +151,9 @@
     )(x, w)
 
 
-def update_kernel(features, bands, index_ref, sigma_ref, y_ref, lat_ref, gain_ref, shift_ref, o_ref):
+def update_kernel(
+    features, bands, index_ref, sigma_ref, y_ref, lat_ref, above_ref, below_ref, gain_ref, shift_ref, o_ref
+):
     heads, lines, _ = y_ref.shape
     rows = lines - 16
     frames = 4
@@ -160,7 +167,12 @@
     up, own, down = (jnp.broadcast_to(sums[:rows, i : i + 1], (rows, HD)) for i in range(3))
     square = jnp.where(lane < SIDE, up, jnp.where(lane < 3 * SIDE, own, down))
     velocity = velocity / jnp.sqrt(square * (1.0 / features) + NORM_EPS)
-    cleaned = lat_ref[...] - sigma_ref[0] * velocity
+    above = above_ref[above_ref.shape[0] - rows :, :].astype(F32)
+    below = below_ref[below_ref.shape[0] - rows :, :].astype(F32)
+    above = above + pltpu.roll(above, HD - SIDE, 1) + pltpu.roll(above, HD - 2 * SIDE, 1)
+    below = pltpu.roll(below, 3 * SIDE, 1) + pltpu.roll(below, 2 * SIDE, 1) + pltpu.roll(below, SIDE, 1)
+    lat = jnp.where(lane < SIDE, above, jnp.where(lane < 3 * SIDE, lat_ref[...], below))
+    cleaned = lat - sigma_ref[0] * velocity
     scaled = cleaned * gain_ref[...] + shift_ref[...]
     first, last = index_ref[0] == 0, index_ref[0] == heads - 1
     drop = ((lane < SIDE) & first) | ((lane >= 3 * SIDE) & last)
@@ -175,17 +187,83 @@
     o_ref[...] = dot_nn(chosen, scaled).astype(BF16).reshape(o_ref.shape)
 
 
-def update(index, sigma, y, lat, gain, shift, features, bands):
+def update(index, sigma, y, lat, above, below, gain, shift, features, bands):
     smem = pl.BlockSpec(memory_space=pltpu.SMEM)
     vmem = pl.BlockSpec(memory_space=VMEM)
     return pl.pallas_call(
         functools.partial(update_kernel, features, bands),
-        in_specs=[smem, smem] + [vmem] * 4,
+        in_specs=[smem, smem] + [vmem] * 6,
         out_specs=vmem,
         out_shape=jax.ShapeDtypeStruct((bands, 16, HD), BF16),
         compiler_params=pltpu.CompilerParams(vmem_limit_bytes=16 << 20),
         name="update",
-    )(index, sigma, y, lat, gain, shift)
+    )(index, sigma, y, lat, above, below, gain, shift)
+
+
+AROUND = ((1, 0), (-1, 0), (0, 1), (0, -1), (1, 1), (1, -1), (-1, 1), (-1, -1))
+
+
+def edges_kernel(index_ref, tail_ref, lat_ref, own_ref, *out_refs):
+    count, width = tail_ref.shape
+    odd = index_ref[0] % 2
+    shape = (width, 3 * HD)
+    k = lax.broadcasted_iota(jnp.int32, shape, 0)
+    n = lax.broadcasted_iota(jnp.int32, shape, 1)
+    pixel = k // LAT_CH
+    i = jnp.where(pixel >= 3, 1, 0)
+    j = pixel - 3 * i
+    same = (k % LAT_CH) == (n % LAT_CH)
+    slot = 2 * (n // HD) + (n % SIDE) // LAT_CH
+    row = (n % HD) // SIDE
+    for (dr, dz), out_ref in zip(((0, 0),) + AROUND, (own_ref,) + out_refs):
+        shift = 1 - odd if dz == 0 else odd
+        hit = same & (row == i + (1 - 2 * dr)) & (slot == j + (1 - 3 * dz) + shift)
+        if dz:
+            hit = hit & (j == (2 if dz == 1 else 0))
+        placed = dot_nn(tail_ref[...], jnp.where(hit, 1.0, 0.0).astype(BF16)).astype(BF16)
+        for t in range(3):
+            out_ref[t * count : (t + 1) * count, :] = placed[:, t * HD : (t + 1) * HD]
+    lat = lat_ref[...]
+    high = lat.astype(BF16).astype(F32)
+    rest = lat - high
+    mid = rest.astype(BF16).astype(F32)
+    low = rest - mid
+    lane = lax.broadcasted_iota(jnp.int32, lat.shape, 1)
+    for out_ref, start in zip(out_refs[:2], (2 * SIDE, SIDE)):
+        parts = []
+        for place, part in enumerate((high, mid, low)):
+            turn = (place * SIDE - start) % HD
+            parts.append(pltpu.roll(part, turn, 1) if turn else part)
+        merged = jnp.where(lane < 2 * SIDE, parts[1], jnp.where(lane < 3 * SIDE, parts[2], 0.0))
+        merged = jnp.where(lane < SIDE, parts[0], merged)
+        out_ref[3 * count :, :] = merged.astype(BF16)
+
+
+def edges(index, tail, lat):
+    count = 3 * tail.shape[0]
+    shapes = [count] + [count + lat.shape[0]] * 2 + [count] * 6
+    vmem = pl.BlockSpec(memory_space=VMEM)
+    return pl.pallas_call(
+        edges_kernel,
+        in_specs=[pl.BlockSpec(memory_space=pltpu.SMEM), vmem, vmem],
+        out_specs=[vmem] * 9,
+        out_shape=[jax.ShapeDtypeStruct((lines, HD), BF16) for lines in shapes],
+        compiler_params=pltpu.CompilerParams(vmem_limit_bytes=16 << 20),
+        name="edges",
+    )(index, tail, lat)
+
+
+def to_around(arrays):
+    rows, bands = lax.axis_size("seq"), lax.axis_size("grp")
+    arrived = []
+    for (dr, dz), array in zip(AROUND, arrays):
+        pairs = [
+            (r * bands + z, (r + dr) * bands + z + dz)
+            for r in range(max(-dr, 0), rows - max(dr, 0))
+            for z in range(max(-dz, 0), bands - max(dz, 0))
+        ]
+        arrived.append(lax.ppermute(array, ("seq", "grp"), pairs))
+    return arrived
 
 
 STARTS = (((0, 1), (1, 0), (1, 1)), ((0, 0), (0, 1), (1, 0)))
@@ -217,7 +295,8 @@
     )(conv_weight)
 
 
-def conv_kernel(index_ref, z_ref, cached_ref, taps_ref, bias_ref, o_ref):
+def conv_kernel(index_ref, z_ref, taps_ref, bias_ref, *refs):
+    *cached_refs, o_ref = refs
     videos, lines, _ = z_ref.shape
     frames = lines // 4
     out = bias_ref.shape[1]
@@ -228,8 +307,12 @@
     t, frame, video = at // count, (at // videos) % frames, at % videos
     chosen = jnp.where(source == video * lines + frame * 4 + t, 1.0, 0.0).astype(BF16)
     image = dot_nn(chosen, z_ref[...].reshape(videos * lines, HD)).astype(BF16)
+    held = cached_refs[0].shape[0] // 3
+    cached = sum(ref[: 3 * held, :].astype(F32) for ref in cached_refs).astype(BF16)
     token = [
-        jnp.concatenate([cached_ref[t], image[t * count : (t + 1) * count]], axis=0)
+        jnp.concatenate(
+            [cached[t * held : (t + 1) * held], image[t * count : (t + 1) * count]], axis=0
+        )
         for t in range(3)
     ]
 
@@ -260,19 +343,12 @@
     vmem = pl.BlockSpec(memory_space=VMEM)
     return pl.pallas_call(
         conv_kernel,
-        in_specs=[pl.BlockSpec(memory_space=pltpu.SMEM)] + [vmem] * 4,
+        in_specs=[pl.BlockSpec(memory_space=pltpu.SMEM)] + [vmem] * (3 + len(cached)),
         out_specs=vmem,
         out_shape=jax.ShapeDtypeStruct((videos, lines // 4, 3, 2, out), BF16),
         compiler_params=pltpu.CompilerParams(vmem_limit_bytes=32 << 20),
         name="convolve",
-    )(index, z, cached, taps, bias).transpose(0, 1, 3, 2, 4)
-
-
-def neighbours(head, tail, axis):
-    count = lax.axis_size(axis)
-    before = lax.ppermute(tail, axis, [(i, i + 1) for i in range(count - 1)])
-    after = lax.ppermute(head, axis, [(i + 1, i) for i in range(count - 1)])
-    return before, after
+    )(index, z, taps, bias, *cached).transpose(0, 1, 3, 2, 4)
 
 
 def on_device(
@@ -304,44 +380,29 @@
     )
     mine = lax.all_to_all(sent, "seq", 0, 0, tiled=True)
 
-    lat = latent.reshape(rows, 4 * LAT_CH)
-    cached = jnp.transpose(frame_tail, (0, 1, 3, 2, 4))
-    flat = (videos * tail_frames * frame_tail.shape[3] * LAT_CH // SIDE, SIDE)
-    top = jnp.concatenate([lat[:, :SIDE], cached[:, :, :, 0].astype(F32).reshape(flat)], axis=0)
-    low = jnp.concatenate([lat[:, SIDE:], cached[:, :, :, -1].astype(F32).reshape(flat)], axis=0)
-    above, below = neighbours(top, low, "seq")
-    lat = jnp.concatenate([above[:rows], lat, below[:rows]], axis=1)
-    above, below = (
-        side[rows:].astype(BF16).reshape(cached[:, :, :, :1].shape) for side in (above, below)
-    )
-    cached = jnp.concatenate([above, cached, below], axis=3)
-    left, right = neighbours(cached[:, :, :1], cached[:, :, -1:], "grp")
-    cached = jnp.concatenate([left, cached, right], axis=2)
-    none = jnp.zeros_like(left)
-    cached = jnp.where(
-        grp_at % 2 == 0,
-        jnp.concatenate([none, cached], axis=2),
-        jnp.concatenate([cached, none], axis=2),
-    )
-    cached = cached.reshape(videos, tail_frames, 3, 2, 4, LAT_CH).transpose(2, 1, 0, 4, 3, 5)
-    cached = cached.reshape(3, tail_frames * videos, HD)
+    seq_at, grp_at = seq_at.reshape(1), grp_at.reshape(1)
+    lat = jnp.pad(latent.reshape(rows, 4 * LAT_CH), ((0, 0), (SIDE, SIDE)))
+    tail = jnp.transpose(frame_tail, (1, 0, 2, 3, 4)).reshape(videos * tail_frames, -1)
+    own, *sides = edges(grp_at, tail, lat)
+    sides = to_around(sides)
 
     taps = spread_taps(conv_weight)
-    w = lax.dynamic_slice_in_dim(head_weight, seq_at * HD, HD, axis=0)
+    w = lax.dynamic_slice_in_dim(head_weight, seq_at[0] * HD, HD, axis=0)
     w = jnp.concatenate([w[:, SIDE:], w, w[:, :SIDE]], axis=1)
     gain = jnp.tile(latent_scale, HD // LAT_CH).reshape(1, HD)
     shift = jnp.tile(latent_shift, HD // LAT_CH).reshape(1, HD)
 
     bias = conv_bias.reshape(1, -1)
-    seq_at, grp_at = seq_at.reshape(1), grp_at.reshape(1)
-    mine, w, lat, cached, taps, gain, shift, bias, sigma, seq_at, grp_at = lax.optimization_barrier(
-        (mine, w, lat, cached, taps, gain, shift, bias, sigma, seq_at, grp_at)
+    mine, w, lat, own, sides, taps, gain, shift, bias, sigma = lax.optimization_barrier(
+        (mine, w, lat, own, sides, taps, gain, shift, bias, sigma)
     )
 
     parts = lax.all_to_all(attend(mine, w), "seq", 0, 0, tiled=True)
-    bands_out = update(seq_at, sigma, parts, lat, gain, shift, features, bands)
+    bands_out = update(
+        seq_at, sigma, parts, lat, sides[0], sides[1], gain, shift, features, bands
+    )
     tiles = lax.all_to_all(bands_out, "grp", 0, 0, tiled=True)
-    return convolve(grp_at, tiles, cached, taps, bias)
+    return convolve(grp_at, tiles, [own] + sides, taps, bias)
 
 
 def solution(mesh):

time: 122 us -> 118 us (0.967)
  waiting for transfers between devices: 37.7 us -> 23.7 us
  starting transfers between devices: 29.7 us -> 39.8 us
  local copies, waits for them, and re-layouts: 5.25 us -> 1.58 us
  Pallas kernels: 20.3 us -> 23.4 us
  blocking collectives: 26 us -> 27.4 us
    ppermute x4 -> x8, waiting for transfers between devices: 22.5 us -> 5.85 us  [to_around(): arrived.append(lax.ppermute(array, ('seq', 'grp'), pairs))]
    ppermute x4 -> x8, starting transfers between devices: 8.05 us -> 20.6 us  [to_around(): arrived.append(lax.ppermute(array, ('seq', 'grp'), pairs))]
    slice x5 -> x0, local copies, waits for them, and re-layouts: 3.16 us -> none  [the longest x2 1.6 us: on_device(): lat = jnp.concatenate([above[:rows], lat, below[:rows]], axis=1)]
    all_to_all x1, waiting for transfers between devices: 0.01 us -> 2.67 us  [on_device(): mine = lax.all_to_all(sent, 'seq', 0, 0, tiled=True)]
    all_to_all x1, starting transfers between devices: 10.2 us -> 7.74 us  [on_device(): parts = lax.all_to_all(attend(mine, w), 'seq', 0, 0, tiled=True)]
    pallas_call x1 -> x2, Pallas kernels: 13.5 us -> 15.8 us  [the longest x1 14.9 us: attend(): pl.pallas_call(functools.partial(attend_kernel, block_tr), in_specs=[pl.B...]
    all_to_all x1, blocking collectives: 26 us -> 27.4 us  [on_device(): tiles = lax.all_to_all(bands_out, 'grp', 0, 0, tiled=True)]
  transfers between devices with their start and end apart: 6 -> 10, of which waited for: 4 -> 4; matrix products, arithmetic and copies ran while one was open for 4% -> 1% of each run, Pallas kernels for 0% -> 1%
where the time goes in v3:
time: 118 us; the launch traced here: 117 us
  starting transfers between devices  39.8 us (34%)
  blocking collectives  27.4 us (23%)
  waiting for transfers between devices  23.7 us (20%)
  Pallas kernels  23.4 us (20%)
  local copies, waits for them, and re-layouts  1.58 us (1%)
    all_to_all x1, blocking collectives, on_device(): tiles = lax.all_to_all(bands_out, 'grp', 0, 0, tiled=True)  27.4 us
    ppermute x8, starting transfers between devices, to_around(): arrived.append(lax.ppermute(array, ('seq', 'grp'), pairs))  20.6 us
    all_to_all x1, waiting for transfers between devices, on_device(): parts = lax.all_to_all(attend(mine, w), 'seq', 0, 0, tiled=True)  15.2 us
    pallas_call x1, Pallas kernels, attend(): pl.pallas_call(functools.partial(attend_kernel, block_tr), in_specs=[pl.B...  14.9 us
    all_to_all x1, starting transfers between devices, on_device(): mine = lax.all_to_all(sent, 'seq', 0, 0, tiled=True)  11.4 us
    all_to_all x1, starting transfers between devices, on_device(): parts = lax.all_to_all(attend(mine, w), 'seq', 0, 0, tiled=True)  7.74 us
    ppermute x8, waiting for transfers between devices, to_around(): arrived.append(lax.ppermute(array, ('seq', 'grp'), pairs))  5.85 us
    pallas_call x1, Pallas kernels, pack_heads(): pl.pallas_call(pack_kernel, grid=(steps,), in_specs=[spec] * 3, out_specs...  2.93 us
  transfers between devices with their start and end apart: 10, of which 4 were waited for; matrix products, arithmetic and copies ran while one was open for 1% of the time, Pallas kernels for 1%

profile of v3, /device:TPU:1, one launch (start us, length us, event | category | flops | bytes accessed | tf_op | source)
XLA Modules:
  0.0 116.8 jit_solution(3613531081041422815)
XLA Ops:
  0.0 0.0 copy-start
  0.0 2.9 %pack_heads.1 = bf16[32,288,128]{2,1,0:T(8,128)(2,1)} custom-call(bf16[96,4096]{1,0:T(8,128)(2,1)} %bitcast.8, bf16[96,4096]{1,0:T(8,128)(2,1)} %bitcast.9, bf16[96,4096]{1,0:T(8,128)(2,1)} %bitcast.10), custom_call_target="tpu_custom_call" | custom-call | tf_op jit(solution)/shard_map/pack_heads/pallas_call | solution.py:40
  2.9 0.0 copy-start.3
  2.9 0.0 copy-start.4
  2.9 0.0 copy-start.2
  2.9 11.4 %all-to-all-start = ((bf16[32,288,128]{2,1,0:T(8,128)(2,1)}), bf16[32,288,128]{2,1,0:T(8,128)(2,1)}, u32[]{:S(2)}, u32[]{:S(2)}) async-start(bf16[32,288,128]{2,1,0:T(8,128)(2,1)} %pack_heads.1), calls=%async_computation | async-start | bytes 4718592 | tf_op jit(solution)/shard_map/all_to_all | solution.py:381
  14.4 0.0 copy-start.6
  14.4 0.0 copy-start.7
  14.4 0.0 copy-start.5
  14.4 0.0 copy-done.3
  14.4 0.1 reshape.34.tail_ref
  14.5 0.0 copy-done.4
  14.6 0.1 pad.4.lat_ref
  14.6 0.9 edges.1
  15.6 3.5 %collective-permute-start = (bf16[192,128]{1,0:T(8,128)(2,1)}, bf16[192,128]{1,0:T(8,128)(2,1)S(1)}, u32[]{:S(2)}, u32[]{:S(2)}) collective-permute-start(bf16[192,128]{1,0:T(8,128)(2,1)} %get-tuple-element.32), channel_id=1, source_target_pairs={{0,16},{1,17},{2,18},{3,19},{4,20},{5,21},{6,22},{7,23},{8,24},{9,... | collective-permute-start | bytes 147464 | tf_op jit(solution)/shard_map/ppermute | solution.py:265
  19.1 1.9 %collective-permute-start.1 = (bf16[192,128]{1,0:T(8,128)(2,1)}, bf16[192,128]{1,0:T(8,128)(2,1)S(1)}, u32[]{:S(2)}, u32[]{:S(2)}) collective-permute-start(bf16[192,128]{1,0:T(8,128)(2,1)} %get-tuple-element.33), channel_id=1, source_target_pairs={{16,0},{17,1},{18,2},{19,3},{20,4},{21,5},{22,6},{23,7},{24,8},{25... | collective-permute-start | bytes 147464 | tf_op jit(solution)/shard_map/ppermute | solution.py:265
  21.0 1.3 %collective-permute-start.2 = (bf16[96,128]{1,0:T(8,128)(2,1)S(1)}, bf16[96,128]{1,0:T(8,128)(2,1)S(1)}, u32[]{:S(2)}, u32[]{:S(2)}) collective-permute-start(bf16[96,128]{1,0:T(8,128)(2,1)S(1)} %get-tuple-element.34), channel_id=1, source_target_pairs={{0,1},{1,2},{2,3},{3,4},{4,5},{5,6},{6,7},{7,8},{8,9},{9,10},{10,1... | collective-permute-start | bytes 73736 | tf_op jit(solution)/shard_map/ppermute | solution.py:265
  22.3 1.3 %collective-permute-start.3 = (bf16[96,128]{1,0:T(8,128)(2,1)S(1)}, bf16[96,128]{1,0:T(8,128)(2,1)S(1)}, u32[]{:S(2)}, u32[]{:S(2)}) collective-permute-start(bf16[96,128]{1,0:T(8,128)(2,1)S(1)} %get-tuple-element.35), channel_id=1, source_target_pairs={{1,0},{2,1},{3,2},{4,3},{5,4},{6,5},{7,6},{8,7},{9,8},{10,9},{11,1... | collective-permute-start | bytes 73736 | tf_op jit(solution)/shard_map/ppermute | solution.py:265
  23.6 5.7 %collective-permute-start.4 = (bf16[96,128]{1,0:T(8,128)(2,1)S(1)}, bf16[96,128]{1,0:T(8,128)(2,1)S(1)}, u32[]{:S(2)}, u32[]{:S(2)}) collective-permute-start(bf16[96,128]{1,0:T(8,128)(2,1)S(1)} %get-tuple-element.36), channel_id=1, source_target_pairs={{0,17},{1,18},{2,19},{3,20},{4,21},{5,22},{6,23},{7,24},{8,25},{9,... | collective-permute-start | bytes 73736 | tf_op jit(solution)/shard_map/ppermute | solution.py:265
  29.4 0.0 copy-done
  29.4 0.1 copy.19
  29.5 0.1 fusion
  29.6 0.0 collective-permute-done.2.refs_3_
  29.6 1.3 %collective-permute-start.5 = (bf16[96,128]{1,0:T(8,128)(2,1)}, bf16[96,128]{1,0:T(8,128)(2,1)S(1)}, u32[]{:S(2)}, u32[]{:S(2)}) collective-permute-start(bf16[96,128]{1,0:T(8,128)(2,1)} %get-tuple-element.37), channel_id=1, source_target_pairs={{1,16},{2,17},{3,18},{4,19},{5,20},{6,21},{7,22},{8,23},{9,24},{10... | collective-permute-start | bytes 73736 | tf_op jit(solution)/shard_map/ppermute | solution.py:265
  30.9 0.0 collective-permute-done.3.refs_4_
  30.9 4.3 %collective-permute-start.6 = (bf16[96,128]{1,0:T(8,128)(2,1)}, bf16[96,128]{1,0:T(8,128)(2,1)S(1)}, u32[]{:S(2)}, u32[]{:S(2)}) collective-permute-start(bf16[96,128]{1,0:T(8,128)(2,1)} %get-tuple-element.38), channel_id=1, source_target_pairs={{16,1},{17,2},{18,3},{19,4},{20,5},{21,6},{22,7},{23,8},{24,9},{25... | collective-permute-start | bytes 73736 | tf_op jit(solution)/shard_map/ppermute | solution.py:265
  35.2 0.0 collective-permute-done.4.refs_5_
  35.2 1.3 %collective-permute-start.7 = (bf16[96,128]{1,0:T(8,128)(2,1)}, bf16[96,128]{1,0:T(8,128)(2,1)}, u32[]{:S(2)}, u32[]{:S(2)}) collective-permute-start(bf16[96,128]{1,0:T(8,128)(2,1)} %get-tuple-element.39), channel_id=1, source_target_pairs={{17,0},{18,1},{19,2},{20,3},{21,4},{22,5},{23,6},{24,7},{25,8},{26... | collective-permute-start | bytes 73736 | tf_op jit(solution)/shard_map/ppermute | solution.py:265
  36.5 0.1 pad_maximum_fusion.w_ref
  36.6 0.0 copy-done.2
  36.6 0.2 spread_taps.1.taps_ref
  36.9 0.0 copy-done.6
  36.9 0.1 reshape_tile.6.gain_ref
  37.0 0.0 copy-done.7
  37.0 0.1 reshape_tile.7.shift_ref
  37.0 0.0 copy-done.5
  37.1 0.0 collective-permute-done.5.refs_6_
  37.1 0.0 collective-permute-done.6.refs_7_
  37.1 5.7 %collective-permute-done.7.refs_8_ = bf16[96,128]{1,0:T(8,128)(2,1)} collective-permute-done((bf16[96,128]{1,0:T(8,128)(2,1)}, bf16[96,128]{1,0:T(8,128)(2,1)}, u32[]{:S(2)}, u32[]{:S(2)}) %collective-permute-start.7) | collective-permute-done | bytes 24608 | tf_op jit(solution)/shard_map/ppermute | solution.py:265
  42.8 0.0 collective-permute-done.above_ref.refs_1_
  42.8 0.1 collective-permute-done.1.below_ref.refs_2_
  42.9 2.7 %all-to-all-done.x_ref = bf16[32,288,128]{2,1,0:T(8,128)(2,1)} async-done(((bf16[32,288,128]{2,1,0:T(8,128)(2,1)}), bf16[32,288,128]{2,1,0:T(8,128)(2,1)}, u32[]{:S(2)}, u32[]{:S(2)}) %all-to-all-start) | async-done | bytes 2359328 | tf_op jit(solution)/shard_map/all_to_all | solution.py:381
  45.6 14.9 %attend.1 = bf16[32,112,128]{2,1,0:T(8,128)(2,1)S(1)} custom-call(bf16[32,288,128]{2,1,0:T(8,128)(2,1)} %all-to-all-done.x_ref, bf16[128,128]{1,0:T(8,128)(2,1)S(1)} %pad_maximum_fusion.w_ref), custom_call_target="tpu_custom_call" | custom-call | flops 9663676416 | bytes 4194304 | tf_op jit(solution)/shard_map/attend/pallas_call | solution.py:128
  60.5 0.0 copy-start.1
  60.5 1.0 copy-done.1
  61.4 7.7 %all-to-all-start.1 = ((bf16[32,112,128]{2,1,0:T(8,128)(2,1)}), bf16[32,112,128]{2,1,0:T(8,128)(2,1)}, u32[]{:S(2)}, u32[]{:S(2)}) async-start(bf16[32,112,128]{2,1,0:T(8,128)(2,1)} %copy-done.1), calls=%async_computation.1 | async-start | bytes 1835008 | tf_op jit(solution)/shard_map/all_to_all | solution.py:400
  69.8 15.2 %all-to-all-done.1.y_ref = bf16[32,112,128]{2,1,0:T(8,128)(2,1)} async-done(((bf16[32,112,128]{2,1,0:T(8,128)(2,1)}), bf16[32,112,128]{2,1,0:T(8,128)(2,1)}, u32[]{:S(2)}, u32[]{:S(2)}) %all-to-all-start.1) | async-done | bytes 917536 | tf_op jit(solution)/shard_map/all_to_all | solution.py:400
  85.0 1.7 %update.1 = bf16[16,16,128]{2,1,0:T(8,128)(2,1)S(1)} custom-call(s32[1]{0:T(128)} %bitcast.1.index_ref, f32[1]{0:T(128)S(6)} %copy.20.sigma_ref, bf16[32,112,128]{2,1,0:T(8,128)(2,1)} %all-to-all-done.1.y_ref, f32[96,128]{1,0:T(8,128)S(1)} %pad.4.lat_ref, bf16[192,128]{1,0:T(8,128)(2,1)S(1)} %collective-permute-done.above_ref.refs_1_, ...), custom_call_target="tpu_custom_call" | custom-call | tf_op jit(solution)/shard_map/update/pallas_call | solution.py:193
  86.7 27.4 %all_to_all.15.z_ref = bf16[16,16,128]{2,1,0:T(8,128)(2,1)S(1)} all-to-all(bf16[16,16,128]{2,1,0:T(8,128)(2,1)S(1)} %update.1), channel_id=1, replica_groups=mesh['seq'=32,'grp'=16] {'grp'}, dimensions={0} | all-to-all | bytes 131072 | tf_op jit(solution)/shard_map/all_to_all | solution.py:404
  114.1 2.7 %convolve.1 = bf16[16,4,3,2,384]{4,3,2,1,0:T(2,128)(2,1)} custom-call(s32[1]{0:T(128)} %bitcast.index_ref, bf16[16,16,128]{2,1,0:T(8,128)(2,1)S(1)} %all_to_all.15.z_ref, bf16[2,768,768]{2,1,0:T(8,128)(2,1)S(1)} %spread_taps.1.taps_ref, f32[1,384]{1,0:T(1,128)S(1)} %reshape.33.bias_ref, bf16[96,128]{1,0:T(8,128)(2,1)S(1)} %get-tuple-element.50.refs_0_, ...), custom_call_target="tpu_custom_call" | custom-call | tf_op jit(solution)/shard_map/convolve/pallas_call | solution.py:344
  (5 shorter events, 0.0 us)
Async XLA Ops:
  0.0 29.4 %copy-start = (bf16[4096,64]{0,1:T(8,128)(2,1)S(1)}, bf16[4096,64]{0,1:T(8,128)(2,1)}, u32[]{:S(2)}) copy-start(bf16[4096,64]{0,1:T(8,128)(2,1)} %param.16) | copy-start | bytes 1572868
  2.9 11.5 %copy-start.3 = (bf16[16,2,2,3,16]{4,2,3,1,0:T(2,128)(2,1)S(1)}, bf16[16,2,2,3,16]{4,2,3,1,0:T(2,128)(2,1)}, u32[]{:S(2)}) copy-start(bf16[16,2,2,3,16]{4,2,3,1,0:T(2,128)(2,1)} %param.19) | copy-start | bytes 18436
  2.9 11.6 %copy-start.4 = (f32[1,1,4,24,64]{4,3,2,1,0:T(8,128)S(1)}, f32[1,1,4,24,64]{4,3,2,1,0:T(8,128)}, u32[]{:S(2)}) copy-start(f32[1,1,4,24,64]{4,3,2,1,0:T(8,128)} %param.14) | copy-start | bytes 73732
  2.9 33.7 %copy-start.2 = (bf16[432,384]{1,0:T(8,128)(2,1)S(1)}, bf16[432,384]{1,0:T(8,128)(2,1)}, u32[]{:S(2)}) copy-start(bf16[432,384]{1,0:T(8,128)(2,1)} %w_ref.1) | copy-start | bytes 995332
  2.9 42.6 %all-to-all-start = ((bf16[32,288,128]{2,1,0:T(8,128)(2,1)}), bf16[32,288,128]{2,1,0:T(8,128)(2,1)}, u32[]{:S(2)}, u32[]{:S(2)}) async-start(bf16[32,288,128]{2,1,0:T(8,128)(2,1)} %pack_heads.1), calls=%async_computation | async-start | bytes 4718592 | tf_op jit(solution)/shard_map/all_to_all | solution.py:381
  14.4 22.5 %copy-start.6 = (f32[16]{0:T(128)S(1)}, f32[16]{0:T(128)}, u32[]{:S(2)}) copy-start(f32[16]{0:T(128)} %param.17) | copy-start | bytes 196
  14.4 22.6 %copy-start.7 = (f32[16]{0:T(128)S(1)}, f32[16]{0:T(128)}, u32[]{:S(2)}) copy-start(f32[16]{0:T(128)} %param.18) | copy-start | bytes 196
  14.4 22.7 %copy-start.5 = (f32[384]{0:T(512)S(1)}, f32[384]{0:T(512)}, u32[]{:S(2)}) copy-start(f32[384]{0:T(512)} %param.21) | copy-start | bytes 4612
  15.6 27.2 %collective-permute-start = (bf16[192,128]{1,0:T(8,128)(2,1)}, bf16[192,128]{1,0:T(8,128)(2,1)S(1)}, u32[]{:S(2)}, u32[]{:S(2)}) collective-permute-start(bf16[192,128]{1,0:T(8,128)(2,1)} %get-tuple-element.32), channel_id=1, source_target_pairs={{0,16},{1,17},{2,18},{3,19},{4,20},{5,21},{6,22},{7,23},{8,24},{9,... | collective-permute-start | bytes 147464 | tf_op jit(solution)/shard_map/ppermute | solution.py:265
  19.1 23.8 %collective-permute-start.1 = (bf16[192,128]{1,0:T(8,128)(2,1)}, bf16[192,128]{1,0:T(8,128)(2,1)S(1)}, u32[]{:S(2)}, u32[]{:S(2)}) collective-permute-start(bf16[192,128]{1,0:T(8,128)(2,1)} %get-tuple-element.33), channel_id=1, source_target_pairs={{16,0},{17,1},{18,2},{19,3},{20,4},{21,5},{22,6},{23,7},{24,8},{25... | collective-permute-start | bytes 147464 | tf_op jit(solution)/shard_map/ppermute | solution.py:265
  21.0 8.6 %collective-permute-start.2 = (bf16[96,128]{1,0:T(8,128)(2,1)S(1)}, bf16[96,128]{1,0:T(8,128)(2,1)S(1)}, u32[]{:S(2)}, u32[]{:S(2)}) collective-permute-start(bf16[96,128]{1,0:T(8,128)(2,1)S(1)} %get-tuple-element.34), channel_id=1, source_target_pairs={{0,1},{1,2},{2,3},{3,4},{4,5},{5,6},{6,7},{7,8},{8,9},{9,10},{10,1... | collective-permute-start | bytes 73736 | tf_op jit(solution)/shard_map/ppermute | solution.py:265
  22.3 8.6 %collective-permute-start.3 = (bf16[96,128]{1,0:T(8,128)(2,1)S(1)}, bf16[96,128]{1,0:T(8,128)(2,1)S(1)}, u32[]{:S(2)}, u32[]{:S(2)}) collective-permute-start(bf16[96,128]{1,0:T(8,128)(2,1)S(1)} %get-tuple-element.35), channel_id=1, source_target_pairs={{1,0},{2,1},{3,2},{4,3},{5,4},{6,5},{7,6},{8,7},{9,8},{10,9},{11,1... | collective-permute-start | bytes 73736 | tf_op jit(solution)/shard_map/ppermute | solution.py:265
  23.6 11.6 %collective-permute-start.4 = (bf16[96,128]{1,0:T(8,128)(2,1)S(1)}, bf16[96,128]{1,0:T(8,128)(2,1)S(1)}, u32[]{:S(2)}, u32[]{:S(2)}) collective-permute-start(bf16[96,128]{1,0:T(8,128)(2,1)S(1)} %get-tuple-element.36), channel_id=1, source_target_pairs={{0,17},{1,18},{2,19},{3,20},{4,21},{5,22},{6,23},{7,24},{8,25},{9,... | collective-permute-start | bytes 73736 | tf_op jit(solution)/shard_map/ppermute | solution.py:265
  29.6 7.4 %collective-permute-start.5 = (bf16[96,128]{1,0:T(8,128)(2,1)}, bf16[96,128]{1,0:T(8,128)(2,1)S(1)}, u32[]{:S(2)}, u32[]{:S(2)}) collective-permute-start(bf16[96,128]{1,0:T(8,128)(2,1)} %get-tuple-element.37), channel_id=1, source_target_pairs={{1,16},{2,17},{3,18},{4,19},{5,20},{6,21},{7,22},{8,23},{9,24},{10... | collective-permute-start | bytes 73736 | tf_op jit(solution)/shard_map/ppermute | solution.py:265
  30.9 6.1 %collective-permute-start.6 = (bf16[96,128]{1,0:T(8,128)(2,1)}, bf16[96,128]{1,0:T(8,128)(2,1)S(1)}, u32[]{:S(2)}, u32[]{:S(2)}) collective-permute-start(bf16[96,128]{1,0:T(8,128)(2,1)} %get-tuple-element.38), channel_id=1, source_target_pairs={{16,1},{17,2},{18,3},{19,4},{20,5},{21,6},{22,7},{23,8},{24,9},{25... | collective-permute-start | bytes 73736 | tf_op jit(solution)/shard_map/ppermute | solution.py:265
  35.2 7.6 %collective-permute-start.7 = (bf16[96,128]{1,0:T(8,128)(2,1)}, bf16[96,128]{1,0:T(8,128)(2,1)}, u32[]{:S(2)}, u32[]{:S(2)}) collective-permute-start(bf16[96,128]{1,0:T(8,128)(2,1)} %get-tuple-element.39), channel_id=1, source_target_pairs={{17,0},{18,1},{19,2},{20,3},{21,4},{22,5},{23,6},{24,7},{25,8},{26... | collective-permute-start | bytes 73736 | tf_op jit(solution)/shard_map/ppermute | solution.py:265
  60.5 1.0 copy-start.1
  61.4 23.6 %all-to-all-start.1 = ((bf16[32,112,128]{2,1,0:T(8,128)(2,1)}), bf16[32,112,128]{2,1,0:T(8,128)(2,1)}, u32[]{:S(2)}, u32[]{:S(2)}) async-start(bf16[32,112,128]{2,1,0:T(8,128)(2,1)} %copy-done.1), calls=%async_computation.1 | async-start | bytes 1835008 | tf_op jit(solution)/shard_map/all_to_all | solution.py:400

commit v4 on v3

--- a/solution.py
+++ b/solution.py
@@ -47,9 +47,18 @@
     )(query, keys, values)
 
 
-def attend_kernel(block_tr, x_ref, w_ref, o_ref, kk, vx, held, vel, ssq, msg, sem, *buffers):
+def attend_kernel(
+    block_tr, x_ref, w_ref, o_ref, queries, keys, kk, vx, held, vel, ssq, msg, sems, *buffers
+):
     tr, rows3, _ = x_ref.shape
     rows = rows3 // 3
+    into = (queries, keys, vx.at[:, :, :HD])
+    fetches = [
+        pltpu.make_async_copy(x_ref.at[:, n * rows : (n + 1) * rows, :], into[n], sems.at[n])
+        for n in range(3)
+    ]
+    for n in (1, 0, 2):
+        fetches[n].start()
     tokens, block = tr * rows, block_tr * rows
     steps = tr // block_tr
     factor = math.log2(math.e) / math.sqrt(HD)
@@ -58,7 +67,7 @@
 
     def score(step):
         s_ref, peak_ref = buffers[step % 2], buffers[2 + step % 2]
-        q = x_ref[step * block_tr : (step + 1) * block_tr, :rows, :].reshape(block, HD)
+        q = queries[step * block_tr : (step + 1) * block_tr].reshape(block, HD)
         q = q.astype(F32) * factor
         high = q.astype(BF16)
         q = jnp.concatenate([high, (q - high.astype(F32)).astype(BF16)], axis=1)
@@ -66,8 +75,8 @@
         for c in range(tr // chunk_tr):
             at = slice(c * chunk, (c + 1) * chunk)
             if step == 0:
-                keys = x_ref[c * chunk_tr : (c + 1) * chunk_tr, rows : 2 * rows, :]
-                flipped = keys.reshape(chunk, HD).astype(F32).T.astype(BF16)
+                piece = keys[c * chunk_tr : (c + 1) * chunk_tr]
+                flipped = piece.reshape(chunk, HD).astype(F32).T.astype(BF16)
                 kk[:HD, at] = flipped
                 kk[HD:, at] = flipped
             s = dot_nn(q, kk[:, at])
@@ -87,7 +96,7 @@
             ],
             axis=1,
         )
-        mixed = dot_nn(weights, vx[...])
+        mixed = dot_nn(weights, vx[...].reshape(tokens, 2 * HD))
         held[step * block : (step + 1) * block, :] = (mixed[:, :HD] / mixed[:, HD:]).astype(BF16)
 
     lane = lax.broadcasted_iota(jnp.int32, (rows, HD), 1)
@@ -100,14 +109,14 @@
         msg[r, :rows, :] = merged.astype(BF16)
         merged = jnp.where(line == 0, ssq[up], jnp.where(line == 1, ssq[r], ssq[down]))
         msg[r, rows:, :] = merged.astype(BF16)
-        pltpu.make_async_copy(msg.at[r], o_ref.at[r], sem).start()
+        pltpu.make_async_copy(msg.at[r], o_ref.at[r], sems.at[3]).start()
 
     ssq[...] = jnp.zeros_like(ssq)
+    fetches[1].wait()
+    fetches[0].wait()
     score(0)
-    for r in range(tr):
-        at = slice(r * rows, (r + 1) * rows)
-        vx[at, :HD] = x_ref[r, 2 * rows :, :]
-        vx[at, HD:] = jnp.ones((rows, HD), BF16)
+    fetches[2].wait()
+    vx[:, :, HD:] = jnp.ones((tr, rows, HD), BF16)
     for step in range(steps):
         if step + 1 < steps:
             score(step + 1)
@@ -118,7 +127,7 @@
         ssq[r, :, :rows] = dot_nt(jnp.ones((16, HD), BF16), (wide * wide).astype(BF16))
     for r in range(tr):
         send(r)
-    pltpu.make_async_copy(msg, o_ref, sem).wait()
+    pltpu.make_async_copy(msg, o_ref, sems.at[3]).wait()
 
 
 def attend(x, w, block_tr=4):
@@ -127,23 +136,25 @@
     tokens, block = tr * rows, block_tr * rows
     return pl.pallas_call(
         functools.partial(attend_kernel, block_tr),
-        in_specs=[pl.BlockSpec(memory_space=VMEM)] * 2,
-        out_specs=pl.BlockSpec(memory_space=pl.ANY),
-        out_shape=jax.ShapeDtypeStruct((tr, rows + 16, HD), BF16),
+        in_specs=[pl.BlockSpec(memory_space=pl.ANY), pl.BlockSpec(memory_space=VMEM)],
+        out_specs=pl.BlockSpec(memory_space=pltpu.HBM),
+        out_shape=pltpu.HBM((tr, rows + 16, HD), BF16),
         scratch_shapes=[
+            VMEM((tr, rows, HD), BF16),
+            VMEM((tr, rows, HD), BF16),
             VMEM((2 * HD, tokens), BF16),
-            VMEM((tokens, 2 * HD), BF16),
+            VMEM((tr, rows, 2 * HD), BF16),
             VMEM((tokens, HD), BF16),
             VMEM((tokens, HD), F32),
             VMEM((tr, 16, HD), F32),
             VMEM((tr, rows + 16, HD), BF16),
-            pltpu.SemaphoreType.DMA,
+            pltpu.SemaphoreType.DMA((4,)),
             VMEM((block, tokens), F32),
             VMEM((block, tokens), F32),
             VMEM((block, HD), F32),
             VMEM((block, HD), F32),
         ],
-        compiler_params=pltpu.CompilerParams(vmem_limit_bytes=44 << 20),
+        compiler_params=pltpu.CompilerParams(vmem_limit_bytes=32 << 20),
         cost_estimate=pl.CostEstimate(
             flops=8 * tokens * tokens * HD, bytes_accessed=4 << 20, transcendentals=tokens * tokens
         ),
@@ -200,10 +211,7 @@
     )(index, sigma, y, lat, above, below, gain, shift)
 
 
-AROUND = ((1, 0), (-1, 0), (0, 1), (0, -1), (1, 1), (1, -1), (-1, 1), (-1, -1))
-
-
-def edges_kernel(index_ref, tail_ref, lat_ref, own_ref, *out_refs):
+def columns_kernel(index_ref, tail_ref, own_ref, right_ref, left_ref):
     count, width = tail_ref.shape
     odd = index_ref[0] % 2
     shape = (width, 3 * HD)
@@ -212,58 +220,74 @@
     pixel = k // LAT_CH
     i = jnp.where(pixel >= 3, 1, 0)
     j = pixel - 3 * i
-    same = (k % LAT_CH) == (n % LAT_CH)
+    same = ((k % LAT_CH) == (n % LAT_CH)) & ((n % HD) // SIDE == i + 1)
     slot = 2 * (n // HD) + (n % SIDE) // LAT_CH
-    row = (n % HD) // SIDE
-    for (dr, dz), out_ref in zip(((0, 0),) + AROUND, (own_ref,) + out_refs):
+    for dz, out_ref in ((0, own_ref), (1, right_ref), (-1, left_ref)):
         shift = 1 - odd if dz == 0 else odd
-        hit = same & (row == i + (1 - 2 * dr)) & (slot == j + (1 - 3 * dz) + shift)
+        hit = same & (slot == j + (1 - 3 * dz) + shift)
         if dz:
             hit = hit & (j == (2 if dz == 1 else 0))
         placed = dot_nn(tail_ref[...], jnp.where(hit, 1.0, 0.0).astype(BF16)).astype(BF16)
         for t in range(3):
             out_ref[t * count : (t + 1) * count, :] = placed[:, t * HD : (t + 1) * HD]
+
+
+def rows_kernel(own_ref, before_ref, after_ref, lat_ref, tile_ref, down_ref, up_ref):
+    tile = own_ref[...].astype(F32) + before_ref[...].astype(F32) + after_ref[...].astype(F32)
+    count = tile.shape[0]
+    tile_ref[...] = tile.astype(BF16)
+    lane = lax.broadcasted_iota(jnp.int32, tile.shape, 1)
+    turned = pltpu.roll(tile, 2 * SIDE, 1)
+    down_ref[:count, :] = jnp.where(lane < SIDE, turned, 0.0).astype(BF16)
+    up_ref[:count, :] = jnp.where(lane >= 3 * SIDE, turned, 0.0).astype(BF16)
     lat = lat_ref[...]
     high = lat.astype(BF16).astype(F32)
     rest = lat - high
     mid = rest.astype(BF16).astype(F32)
     low = rest - mid
     lane = lax.broadcasted_iota(jnp.int32, lat.shape, 1)
-    for out_ref, start in zip(out_refs[:2], (2 * SIDE, SIDE)):
+    for out_ref, start in ((down_ref, 2 * SIDE), (up_ref, SIDE)):
         parts = []
         for place, part in enumerate((high, mid, low)):
             turn = (place * SIDE - start) % HD
             parts.append(pltpu.roll(part, turn, 1) if turn else part)
         merged = jnp.where(lane < 2 * SIDE, parts[1], jnp.where(lane < 3 * SIDE, parts[2], 0.0))
         merged = jnp.where(lane < SIDE, parts[0], merged)
-        out_ref[3 * count :, :] = merged.astype(BF16)
+        out_ref[count:, :] = merged.astype(BF16)
 
 
 def edges(index, tail, lat):
-    count = 3 * tail.shape[0]
-    shapes = [count] + [count + lat.shape[0]] * 2 + [count] * 6
+    count, more = 3 * tail.shape[0], lat.shape[0]
     vmem = pl.BlockSpec(memory_space=VMEM)
-    return pl.pallas_call(
-        edges_kernel,
-        in_specs=[pl.BlockSpec(memory_space=pltpu.SMEM), vmem, vmem],
-        out_specs=[vmem] * 9,
-        out_shape=[jax.ShapeDtypeStruct((lines, HD), BF16) for lines in shapes],
-        compiler_params=pltpu.CompilerParams(vmem_limit_bytes=16 << 20),
-        name="edges",
-    )(index, tail, lat)
-
-
-def to_around(arrays):
-    rows, bands = lax.axis_size("seq"), lax.axis_size("grp")
-    arrived = []
-    for (dr, dz), array in zip(AROUND, arrays):
-        pairs = [
-            (r * bands + z, (r + dr) * bands + z + dz)
-            for r in range(max(-dr, 0), rows - max(dr, 0))
-            for z in range(max(-dz, 0), bands - max(dz, 0))
-        ]
-        arrived.append(lax.ppermute(array, ("seq", "grp"), pairs))
-    return arrived
+    tile = jax.ShapeDtypeStruct((count, HD), BF16)
+    both = jax.ShapeDtypeStruct((count + more, HD), BF16)
+    small = pltpu.CompilerParams(vmem_limit_bytes=8 << 20)
+    own, right, left = pl.pallas_call(
+        columns_kernel,
+        in_specs=[pl.BlockSpec(memory_space=pltpu.SMEM), vmem],
+        out_specs=[vmem] * 3,
+        out_shape=[tile] * 3,
+        compiler_params=small,
+        name="edge_columns",
+    )(index, tail)
+    before, after = to_next(right, "grp"), to_last(left, "grp")
+    own, down, up = pl.pallas_call(
+        rows_kernel,
+        in_specs=[vmem] * 4,
+        out_specs=[vmem] * 3,
+        out_shape=[tile, both, both],
+        compiler_params=small,
+        name="edge_rows",
+    )(own, before, after, lat)
+    return own, to_next(down, "seq"), to_last(up, "seq")
+
+
+def to_next(array, axis):
+    return lax.ppermute(array, axis, [(i, i + 1) for i in range(lax.axis_size(axis) - 1)])
+
+
+def to_last(array, axis):
+    return lax.ppermute(array, axis, [(i + 1, i) for i in range(lax.axis_size(axis) - 1)])
 
 
 STARTS = (((0, 1), (1, 0), (1, 1)), ((0, 0), (0, 1), (1, 0)))
@@ -290,13 +314,12 @@
         in_specs=[pl.BlockSpec(memory_space=VMEM)],
         out_specs=pl.BlockSpec(memory_space=VMEM),
         out_shape=jax.ShapeDtypeStruct((2, 6 * HD, 2 * out), BF16),
-        compiler_params=pltpu.CompilerParams(vmem_limit_bytes=16 << 20),
+        compiler_params=pltpu.CompilerParams(vmem_limit_bytes=8 << 20),
         name="spread_taps",
     )(conv_weight)
 
 
-def conv_kernel(index_ref, z_ref, taps_ref, bias_ref, *refs):
-    *cached_refs, o_ref = refs
+def conv_kernel(index_ref, z_ref, own_ref, above_ref, below_ref, taps_ref, bias_ref, o_ref):
     videos, lines, _ = z_ref.shape
     frames = lines // 4
     out = bias_ref.shape[1]
@@ -307,8 +330,11 @@
     t, frame, video = at // count, (at // videos) % frames, at % videos
     chosen = jnp.where(source == video * lines + frame * 4 + t, 1.0, 0.0).astype(BF16)
     image = dot_nn(chosen, z_ref[...].reshape(videos * lines, HD)).astype(BF16)
-    held = cached_refs[0].shape[0] // 3
-    cached = sum(ref[: 3 * held, :].astype(F32) for ref in cached_refs).astype(BF16)
+    cached = own_ref[...].astype(F32)
+    for ref in (above_ref, below_ref):
+        cached = cached + ref[: cached.shape[0], :].astype(F32)
+    cached = cached.astype(BF16)
+    held = cached.shape[0] // 3
     token = [
         jnp.concatenate(
             [cached[t * held : (t + 1) * held], image[t * count : (t + 1) * count]], axis=0
@@ -337,18 +363,18 @@
             o_ref[:, f, j] = tile.astype(BF16)
 
 
-def convolve(index, z, cached, taps, bias):
+def convolve(index, z, own, above, below, taps, bias):
     videos, lines, _ = z.shape
     out = bias.shape[1]
     vmem = pl.BlockSpec(memory_space=VMEM)
     return pl.pallas_call(
         conv_kernel,
-        in_specs=[pl.BlockSpec(memory_space=pltpu.SMEM)] + [vmem] * (3 + len(cached)),
+        in_specs=[pl.BlockSpec(memory_space=pltpu.SMEM)] + [vmem] * 6,
         out_specs=vmem,
         out_shape=jax.ShapeDtypeStruct((videos, lines // 4, 3, 2, out), BF16),
-        compiler_params=pltpu.CompilerParams(vmem_limit_bytes=32 << 20),
+        compiler_params=pltpu.CompilerParams(vmem_limit_bytes=16 << 20),
         name="convolve",
-    )(index, z, taps, bias, *cached).transpose(0, 1, 3, 2, 4)
+    )(index, z, own, above, below, taps, bias).transpose(0, 1, 3, 2, 4)
 
 
 def on_device(
@@ -383,8 +409,7 @@
     seq_at, grp_at = seq_at.reshape(1), grp_at.reshape(1)
     lat = jnp.pad(latent.reshape(rows, 4 * LAT_CH), ((0, 0), (SIDE, SIDE)))
     tail = jnp.transpose(frame_tail, (1, 0, 2, 3, 4)).reshape(videos * tail_frames, -1)
-    own, *sides = edges(grp_at, tail, lat)
-    sides = to_around(sides)
+    own, above, below = edges(grp_at, tail, lat)
 
     taps = spread_taps(conv_weight)
     w = lax.dynamic_slice_in_dim(head_weight, seq_at[0] * HD, HD, axis=0)
@@ -393,16 +418,14 @@
     shift = jnp.tile(latent_shift, HD // LAT_CH).reshape(1, HD)
 
     bias = conv_bias.reshape(1, -1)
-    mine, w, lat, own, sides, taps, gain, shift, bias, sigma = lax.optimization_barrier(
-        (mine, w, lat, own, sides, taps, gain, shift, bias, sigma)
+    mine, w, lat, own, above, below, taps, gain, shift, bias, sigma = lax.optimization_barrier(
+        (mine, w, lat, own, above, below, taps, gain, shift, bias, sigma)
     )
 
     parts = lax.all_to_all(attend(mine, w), "seq", 0, 0, tiled=True)
-    bands_out = update(
-        seq_at, sigma, parts, lat, sides[0], sides[1], gain, shift, features, bands
-    )
+    bands_out = update(seq_at, sigma, parts, lat, above, below, gain, shift, features, bands)
     tiles = lax.all_to_all(bands_out, "grp", 0, 0, tiled=True)
-    return convolve(grp_at, tiles, [own] + sides, taps, bias)
+    return convolve(grp_at, tiles, own, above, below, taps, bias)
 
 
 def solution(mesh):

time: 118 us -> 110 us (0.932)
  starting transfers between devices: 39.8 us -> 27.1 us
  waiting for transfers between devices: 23.7 us -> 36 us
  blocking collectives: 27.4 us -> 23.6 us
  Pallas kernels: 23.4 us -> 21 us
    ppermute x8 -> x4, waiting for transfers between devices: 5.85 us -> 18.1 us  [the longest x2 13.1 us: to_next(): lax.ppermute(array, axis, [(i, i + 1) for i in range(lax.axis_size(axis)...]
    ppermute x8 -> x4, starting transfers between devices: 20.6 us -> 8.8 us  [the longest x2 5.59 us: to_next(): lax.ppermute(array, axis, [(i, i + 1) for i in range(lax.axis_size(axis)...]
    all_to_all x1, blocking collectives: 27.4 us -> 23.6 us  [on_device(): tiles = lax.all_to_all(bands_out, 'grp', 0, 0, tiled=True)]
  transfers between devices with their start and end apart: 10 -> 6, of which waited for: 4 -> 5; matrix products, arithmetic and copies ran while one was open for 1% -> 1% of each run, Pallas kernels for 1% -> 0%
where the time goes in v4:
time: 110 us; the launch traced here: 109 us
  waiting for transfers between devices  36 us (33%)
  starting transfers between devices  27.1 us (25%)
  blocking collectives  23.6 us (21%)
  Pallas kernels  21 us (19%)
    all_to_all x1, blocking collectives, on_device(): tiles = lax.all_to_all(bands_out, 'grp', 0, 0, tiled=True)  23.6 us
    all_to_all x1, waiting for transfers between devices, on_device(): parts = lax.all_to_all(attend(mine, w), 'seq', 0, 0, tiled=True)  15.3 us
    pallas_call x1, Pallas kernels, attend(): pl.pallas_call(functools.partial(attend_kernel, block_tr), in_specs=[pl.B...  13.9 us
    ppermute x2, waiting for transfers between devices, to_next(): lax.ppermute(array, axis, [(i, i + 1) for i in range(lax.axis_size(axis)...  13.1 us
    all_to_all x1, starting transfers between devices, on_device(): mine = lax.all_to_all(sent, 'seq', 0, 0, tiled=True)  11.4 us
    all_to_all x1, starting transfers between devices, on_device(): parts = lax.all_to_all(attend(mine, w), 'seq', 0, 0, tiled=True)  6.89 us
    ppermute x2, starting transfers between devices, to_next(): lax.ppermute(array, axis, [(i, i + 1) for i in range(lax.axis_size(axis)...  5.59 us
    ppermute x2, waiting for transfers between devices, to_last(): lax.ppermute(array, axis, [(i + 1, i) for i in range(lax.axis_size(axis)...  5.02 us
  transfers between devices with their start and end apart: 6, of which 5 were waited for; matrix products, arithmetic and copies ran while one was open for 1% of the time, Pallas kernels for 0%

profile of v4, /device:TPU:1, one launch (start us, length us, event | category | flops | bytes accessed | tf_op | source)
XLA Modules:
  0.0 109.3 jit_solution(15056587265364492390)
XLA Ops:
  0.0 0.0 copy-start
  0.0 2.9 %pack_heads.1 = bf16[32,288,128]{2,1,0:T(8,128)(2,1)} custom-call(bf16[96,4096]{1,0:T(8,128)(2,1)} %bitcast.8, bf16[96,4096]{1,0:T(8,128)(2,1)} %bitcast.9, bf16[96,4096]{1,0:T(8,128)(2,1)} %bitcast.10), custom_call_target="tpu_custom_call" | custom-call | tf_op jit(solution)/shard_map/pack_heads/pallas_call | solution.py:40
  2.9 0.0 copy-start.2
  2.9 0.0 copy-start.3
  2.9 0.0 copy-start.1
  2.9 11.4 %all-to-all-start = ((bf16[32,288,128]{2,1,0:T(8,128)(2,1)}), bf16[32,288,128]{2,1,0:T(8,128)(2,1)}, u32[]{:S(2)}, u32[]{:S(2)}) async-start(bf16[32,288,128]{2,1,0:T(8,128)(2,1)} %pack_heads.1), calls=%async_computation | async-start | bytes 4718592 | tf_op jit(solution)/shard_map/all_to_all | solution.py:407
  14.3 0.0 copy-start.5
  14.3 0.0 copy-start.6
  14.4 0.0 copy-start.4
  14.4 0.0 copy-done.2
  14.4 0.1 reshape.34.tail_ref
  14.5 0.2 edge_columns.1
  14.7 1.3 %collective-permute-start = (bf16[96,128]{1,0:T(8,128)(2,1)S(1)}, bf16[96,128]{1,0:T(8,128)(2,1)S(1)}, u32[]{:S(2)}, u32[]{:S(2)}) collective-permute-start(bf16[96,128]{1,0:T(8,128)(2,1)S(1)} %get-tuple-element.23), channel_id=1, source_target_pairs={{0,1},{1,2},{2,3},{3,4},{4,5},{5,6},{6,7},{7,8},{8,9},{9,10},{10,1... | collective-permute-start | bytes 73736 | tf_op jit(solution)/shard_map/ppermute | solution.py:286
  16.0 1.3 %collective-permute-start.1 = (bf16[96,128]{1,0:T(8,128)(2,1)S(1)}, bf16[96,128]{1,0:T(8,128)(2,1)S(1)}, u32[]{:S(2)}, u32[]{:S(2)}) collective-permute-start(bf16[96,128]{1,0:T(8,128)(2,1)S(1)} %get-tuple-element.24), channel_id=1, source_target_pairs={{1,0},{2,1},{3,2},{4,3},{5,4},{6,5},{7,6},{8,7},{9,8},{10,9},{11,1... | collective-permute-start | bytes 73736 | tf_op jit(solution)/shard_map/ppermute | solution.py:290
  17.3 0.0 copy-done
  17.4 0.1 copy.19
  17.5 0.1 fusion
  17.6 0.0 copy-done.3
  17.6 0.1 pad.4.lat_ref
  17.6 0.0 collective-permute-done.before_ref
  17.6 3.3 %collective-permute-done.1.after_ref = bf16[96,128]{1,0:T(8,128)(2,1)S(1)} collective-permute-done((bf16[96,128]{1,0:T(8,128)(2,1)S(1)}, bf16[96,128]{1,0:T(8,128)(2,1)S(1)}, u32[]{:S(2)}, u32[]{:S(2)}) %collective-permute-start.1) | collective-permute-done | bytes 24608 | tf_op jit(solution)/shard_map/ppermute | solution.py:290
  21.0 0.1 edge_rows.1
  21.1 4.3 %collective-permute-start.2 = (bf16[192,128]{1,0:T(8,128)(2,1)S(1)}, bf16[192,128]{1,0:T(8,128)(2,1)S(1)}, u32[]{:S(2)}, u32[]{:S(2)}) collective-permute-start(bf16[192,128]{1,0:T(8,128)(2,1)S(1)} %get-tuple-element.26), channel_id=1, source_target_pairs={{0,16},{16,32},{32,48},{48,64},{64,80},{80,96},{96,112},{112,128},... | collective-permute-start | bytes 147464 | tf_op jit(solution)/shard_map/ppermute | solution.py:286
  25.4 1.9 %collective-permute-start.3 = (bf16[192,128]{1,0:T(8,128)(2,1)S(1)}, bf16[192,128]{1,0:T(8,128)(2,1)S(1)}, u32[]{:S(2)}, u32[]{:S(2)}) collective-permute-start(bf16[192,128]{1,0:T(8,128)(2,1)S(1)} %get-tuple-element.27), channel_id=1, source_target_pairs={{16,0},{32,16},{48,32},{64,48},{80,64},{96,80},{112,96},{128,112},... | collective-permute-start | bytes 147464 | tf_op jit(solution)/shard_map/ppermute | solution.py:290
  27.3 0.1 pad_maximum_fusion.w_ref
  27.4 0.0 copy-done.1
  27.4 0.2 spread_taps.1.taps_ref
  27.7 0.0 copy-done.5
  27.7 0.1 reshape_tile.6.gain_ref
  27.8 0.0 copy-done.6
  27.8 0.1 reshape_tile.7.shift_ref
  27.9 0.0 copy-done.4
  27.9 13.1 %collective-permute-done.2.above_ref = bf16[192,128]{1,0:T(8,128)(2,1)S(1)} collective-permute-done((bf16[192,128]{1,0:T(8,128)(2,1)S(1)}, bf16[192,128]{1,0:T(8,128)(2,1)S(1)}, u32[]{:S(2)}, u32[]{:S(2)}) %collective-permute-start.2) | collective-permute-done | bytes 49184 | tf_op jit(solution)/shard_map/ppermute | solution.py:286
  41.0 1.7 %collective-permute-done.3.below_ref = bf16[192,128]{1,0:T(8,128)(2,1)S(1)} collective-permute-done((bf16[192,128]{1,0:T(8,128)(2,1)S(1)}, bf16[192,128]{1,0:T(8,128)(2,1)S(1)}, u32[]{:S(2)}, u32[]{:S(2)}) %collective-permute-start.3) | collective-permute-done | bytes 49184 | tf_op jit(solution)/shard_map/ppermute | solution.py:290
  42.6 2.6 %all-to-all-done.x_ref = bf16[32,288,128]{2,1,0:T(8,128)(2,1)} async-done(((bf16[32,288,128]{2,1,0:T(8,128)(2,1)}), bf16[32,288,128]{2,1,0:T(8,128)(2,1)}, u32[]{:S(2)}, u32[]{:S(2)}) %all-to-all-start) | async-done | bytes 2359328 | tf_op jit(solution)/shard_map/all_to_all | solution.py:407
  45.2 13.9 %attend.1 = bf16[32,112,128]{2,1,0:T(8,128)(2,1)} custom-call(bf16[32,288,128]{2,1,0:T(8,128)(2,1)} %all-to-all-done.x_ref, bf16[128,128]{1,0:T(8,128)(2,1)S(1)} %pad_maximum_fusion.w_ref), custom_call_target="tpu_custom_call" | custom-call | flops 9663676416 | bytes 4194304 | tf_op jit(solution)/shard_map/attend/pallas_call | solution.py:137
  59.1 6.9 %all-to-all-start.1 = ((bf16[32,112,128]{2,1,0:T(8,128)(2,1)}), bf16[32,112,128]{2,1,0:T(8,128)(2,1)}, u32[]{:S(2)}, u32[]{:S(2)}) async-start(bf16[32,112,128]{2,1,0:T(8,128)(2,1)} %attend.1), calls=%async_computation.1 | async-start | bytes 1835008 | tf_op jit(solution)/shard_map/all_to_all | solution.py:425
  66.7 15.3 %all-to-all-done.1.y_ref = bf16[32,112,128]{2,1,0:T(8,128)(2,1)} async-done(((bf16[32,112,128]{2,1,0:T(8,128)(2,1)}), bf16[32,112,128]{2,1,0:T(8,128)(2,1)}, u32[]{:S(2)}, u32[]{:S(2)}) %all-to-all-start.1) | async-done | bytes 917536 | tf_op jit(solution)/shard_map/all_to_all | solution.py:425
  82.0 1.7 %update.1 = bf16[16,16,128]{2,1,0:T(8,128)(2,1)S(1)} custom-call(s32[1]{0:T(128)} %bitcast.1.index_ref, f32[1]{0:T(128)S(6)} %copy.20.sigma_ref, bf16[32,112,128]{2,1,0:T(8,128)(2,1)} %all-to-all-done.1.y_ref, f32[96,128]{1,0:T(8,128)S(1)} %pad.4.lat_ref, bf16[192,128]{1,0:T(8,128)(2,1)S(1)} %collective-permute-done.2.above_ref, ...), custom_call_target="tpu_custom_call" | custom-call | tf_op jit(solution)/shard_map/update/pallas_call | solution.py:204
  83.7 23.6 %all_to_all.15.z_ref = bf16[16,16,128]{2,1,0:T(8,128)(2,1)S(1)} all-to-all(bf16[16,16,128]{2,1,0:T(8,128)(2,1)S(1)} %update.1), channel_id=1, replica_groups=mesh['seq'=32,'grp'=16] {'grp'}, dimensions={0} | all-to-all | bytes 131072 | tf_op jit(solution)/shard_map/all_to_all | solution.py:427
  107.2 2.0 %convolve.1 = bf16[16,4,3,2,384]{4,3,2,1,0:T(2,128)(2,1)} custom-call(s32[1]{0:T(128)} %bitcast.index_ref, bf16[16,16,128]{2,1,0:T(8,128)(2,1)S(1)} %all_to_all.15.z_ref, bf16[96,128]{1,0:T(8,128)(2,1)S(1)} %get-tuple-element.36.own_ref, bf16[192,128]{1,0:T(8,128)(2,1)S(1)} %collective-permute-done.2.above_ref, ...), custom_call_target="tpu_custom_call" | custom-call | tf_op jit(solution)/shard_map/convolve/pallas_call | solution.py:370
  (5 shorter events, 0.0 us)
Async XLA Ops:
  0.0 17.3 %copy-start = (bf16[4096,64]{0,1:T(8,128)(2,1)S(1)}, bf16[4096,64]{0,1:T(8,128)(2,1)}, u32[]{:S(2)}) copy-start(bf16[4096,64]{0,1:T(8,128)(2,1)} %param.16) | copy-start | bytes 1572868
  2.9 11.5 %copy-start.2 = (bf16[16,2,2,3,16]{4,2,3,1,0:T(2,128)(2,1)S(1)}, bf16[16,2,2,3,16]{4,2,3,1,0:T(2,128)(2,1)}, u32[]{:S(2)}) copy-start(bf16[16,2,2,3,16]{4,2,3,1,0:T(2,128)(2,1)} %param.19) | copy-start | bytes 18436
  2.9 14.6 %copy-start.3 = (f32[1,1,4,24,64]{4,3,2,1,0:T(8,128)S(1)}, f32[1,1,4,24,64]{4,3,2,1,0:T(8,128)}, u32[]{:S(2)}) copy-start(f32[1,1,4,24,64]{4,3,2,1,0:T(8,128)} %param.14) | copy-start | bytes 73732
  2.9 24.5 %copy-start.1 = (bf16[432,384]{1,0:T(8,128)(2,1)S(1)}, bf16[432,384]{1,0:T(8,128)(2,1)}, u32[]{:S(2)}) copy-start(bf16[432,384]{1,0:T(8,128)(2,1)} %w_ref.1) | copy-start | bytes 995332
  2.9 42.3 %all-to-all-start = ((bf16[32,288,128]{2,1,0:T(8,128)(2,1)}), bf16[32,288,128]{2,1,0:T(8,128)(2,1)}, u32[]{:S(2)}, u32[]{:S(2)}) async-start(bf16[32,288,128]{2,1,0:T(8,128)(2,1)} %pack_heads.1), calls=%async_computation | async-start | bytes 4718592 | tf_op jit(solution)/shard_map/all_to_all | solution.py:407
  14.3 13.4 %copy-start.5 = (f32[16]{0:T(128)S(1)}, f32[16]{0:T(128)}, u32[]{:S(2)}) copy-start(f32[16]{0:T(128)} %param.17) | copy-start | bytes 196
  14.3 13.4 %copy-start.6 = (f32[16]{0:T(128)S(1)}, f32[16]{0:T(128)}, u32[]{:S(2)}) copy-start(f32[16]{0:T(128)} %param.18) | copy-start | bytes 196
  14.4 13.5 %copy-start.4 = (f32[384]{0:T(512)S(1)}, f32[384]{0:T(512)}, u32[]{:S(2)}) copy-start(f32[384]{0:T(512)} %param.21) | copy-start | bytes 4612
  14.7 2.9 %collective-permute-start = (bf16[96,128]{1,0:T(8,128)(2,1)S(1)}, bf16[96,128]{1,0:T(8,128)(2,1)S(1)}, u32[]{:S(2)}, u32[]{:S(2)}) collective-permute-start(bf16[96,128]{1,0:T(8,128)(2,1)S(1)} %get-tuple-element.23), channel_id=1, source_target_pairs={{0,1},{1,2},{2,3},{3,4},{4,5},{5,6},{6,7},{7,8},{8,9},{9,10},{10,1... | collective-permute-start | bytes 73736 | tf_op jit(solution)/shard_map/ppermute | solution.py:286
  16.0 5.0 %collective-permute-start.1 = (bf16[96,128]{1,0:T(8,128)(2,1)S(1)}, bf16[96,128]{1,0:T(8,128)(2,1)S(1)}, u32[]{:S(2)}, u32[]{:S(2)}) collective-permute-start(bf16[96,128]{1,0:T(8,128)(2,1)S(1)} %get-tuple-element.24), channel_id=1, source_target_pairs={{1,0},{2,1},{3,2},{4,3},{5,4},{6,5},{7,6},{8,7},{9,8},{10,9},{11,1... | collective-permute-start | bytes 73736 | tf_op jit(solution)/shard_map/ppermute | solution.py:290
  21.1 19.8 %collective-permute-start.2 = (bf16[192,128]{1,0:T(8,128)(2,1)S(1)}, bf16[192,128]{1,0:T(8,128)(2,1)S(1)}, u32[]{:S(2)}, u32[]{:S(2)}) collective-permute-start(bf16[192,128]{1,0:T(8,128)(2,1)S(1)} %get-tuple-element.26), channel_id=1, source_target_pairs={{0,16},{16,32},{32,48},{48,64},{64,80},{80,96},{96,112},{112,128},... | collective-permute-start | bytes 147464 | tf_op jit(solution)/shard_map/ppermute | solution.py:286
  25.4 17.2 %collective-permute-start.3 = (bf16[192,128]{1,0:T(8,128)(2,1)S(1)}, bf16[192,128]{1,0:T(8,128)(2,1)S(1)}, u32[]{:S(2)}, u32[]{:S(2)}) collective-permute-start(bf16[192,128]{1,0:T(8,128)(2,1)S(1)} %get-tuple-element.27), channel_id=1, source_target_pairs={{16,0},{32,16},{48,32},{64,48},{80,64},{96,80},{112,96},{128,112},... | collective-permute-start | bytes 147464 | tf_op jit(solution)/shard_map/ppermute | solution.py:290
  59.1 22.8 %all-to-all-start.1 = ((bf16[32,112,128]{2,1,0:T(8,128)(2,1)}), bf16[32,112,128]{2,1,0:T(8,128)(2,1)}, u32[]{:S(2)}, u32[]{:S(2)}) async-start(bf16[32,112,128]{2,1,0:T(8,128)(2,1)} %attend.1), calls=%async_computation.1 | async-start | bytes 1835008 | tf_op jit(solution)/shard_map/all_to_all | solution.py:425

commit v5 on v4

--- a/solution.py
+++ b/solution.py
@@ -48,7 +48,7 @@
 
 
 def attend_kernel(
-    block_tr, x_ref, w_ref, o_ref, queries, keys, kk, vx, held, vel, ssq, msg, sems, *buffers
+    block_tr, x_ref, w_ref, o_ref, queries, keys, kk, vx, held, vel, ssq, sems, *buffers
 ):
     tr, rows3, _ = x_ref.shape
     rows = rows3 // 3
@@ -106,10 +106,9 @@
         up, down = (r - 1) % tr, (r + 1) % tr
         piece = [vel[t * rows : (t + 1) * rows, :] for t in (up, r, down)]
         merged = jnp.where(lane < SIDE, piece[0], jnp.where(lane < 3 * SIDE, piece[1], piece[2]))
-        msg[r, :rows, :] = merged.astype(BF16)
+        o_ref[r, :rows, :] = merged.astype(BF16)
         merged = jnp.where(line == 0, ssq[up], jnp.where(line == 1, ssq[r], ssq[down]))
-        msg[r, rows:, :] = merged.astype(BF16)
-        pltpu.make_async_copy(msg.at[r], o_ref.at[r], sems.at[3]).start()
+        o_ref[r, rows:, :] = merged.astype(BF16)
 
     ssq[...] = jnp.zeros_like(ssq)
     fetches[1].wait()
@@ -122,12 +121,12 @@
             score(step + 1)
         mix(step)
     vel[...] = dot_nn(held[...], w_ref[...])
+    wide = held[...].astype(F32)
+    total = dot_nt(jnp.ones((16, HD), BF16), (wide * wide).astype(BF16))
     for r in range(tr):
-        wide = held[r * rows : (r + 1) * rows, :].astype(F32)
-        ssq[r, :, :rows] = dot_nt(jnp.ones((16, HD), BF16), (wide * wide).astype(BF16))
+        ssq[r, :, :rows] = total[:, r * rows : (r + 1) * rows]
     for r in range(tr):
         send(r)
-    pltpu.make_async_copy(msg, o_ref, sems.at[3]).wait()
 
 
 def attend(x, w, block_tr=4):
@@ -137,8 +136,8 @@
     return pl.pallas_call(
         functools.partial(attend_kernel, block_tr),
         in_specs=[pl.BlockSpec(memory_space=pl.ANY), pl.BlockSpec(memory_space=VMEM)],
-        out_specs=pl.BlockSpec(memory_space=pltpu.HBM),
-        out_shape=pltpu.HBM((tr, rows + 16, HD), BF16),
+        out_specs=pl.BlockSpec(memory_space=VMEM),
+        out_shape=jax.ShapeDtypeStruct((tr, rows + 16, HD), BF16),
         scratch_shapes=[
             VMEM((tr, rows, HD), BF16),
             VMEM((tr, rows, HD), BF16),
@@ -147,8 +146,7 @@
             VMEM((tokens, HD), BF16),
             VMEM((tokens, HD), F32),
             VMEM((tr, 16, HD), F32),
-            VMEM((tr, rows + 16, HD), BF16),
-            pltpu.SemaphoreType.DMA((4,)),
+            pltpu.SemaphoreType.DMA((3,)),
             VMEM((block, tokens), F32),
             VMEM((block, tokens), F32),
             VMEM((block, HD), F32),
@@ -163,7 +161,7 @@
 
 
 def update_kernel(
-    features, bands, index_ref, sigma_ref, y_ref, lat_ref, above_ref, below_ref, gain_ref, shift_ref, o_ref
+    features, bands, index_ref, y_ref, lat_ref, above_ref, below_ref, sigma_ref, gain_ref, shift_ref, o_ref
 ):
     heads, lines, _ = y_ref.shape
     rows = lines - 16
@@ -183,7 +181,7 @@
     above = above + pltpu.roll(above, HD - SIDE, 1) + pltpu.roll(above, HD - 2 * SIDE, 1)
     below = pltpu.roll(below, 3 * SIDE, 1) + pltpu.roll(below, 2 * SIDE, 1) + pltpu.roll(below, SIDE, 1)
     lat = jnp.where(lane < SIDE, above, jnp.where(lane < 3 * SIDE, lat_ref[...], below))
-    cleaned = lat - sigma_ref[0] * velocity
+    cleaned = lat - sigma_ref[...] * velocity
     scaled = cleaned * gain_ref[...] + shift_ref[...]
     first, last = index_ref[0] == 0, index_ref[0] == heads - 1
     drop = ((lane < SIDE) & first) | ((lane >= 3 * SIDE) & last)
@@ -198,17 +196,17 @@
     o_ref[...] = dot_nn(chosen, scaled).astype(BF16).reshape(o_ref.shape)
 
 
-def update(index, sigma, y, lat, above, below, gain, shift, features, bands):
+def update(index, y, lat, above, below, sigma, gain, shift, features, bands):
     smem = pl.BlockSpec(memory_space=pltpu.SMEM)
     vmem = pl.BlockSpec(memory_space=VMEM)
     return pl.pallas_call(
         functools.partial(update_kernel, features, bands),
-        in_specs=[smem, smem] + [vmem] * 6,
+        in_specs=[smem] + [vmem] * 7,
         out_specs=vmem,
         out_shape=jax.ShapeDtypeStruct((bands, 16, HD), BF16),
         compiler_params=pltpu.CompilerParams(vmem_limit_bytes=16 << 20),
         name="update",
-    )(index, sigma, y, lat, above, below, gain, shift)
+    )(index, y, lat, above, below, sigma, gain, shift)
 
 
 def columns_kernel(index_ref, tail_ref, own_ref, right_ref, left_ref):
@@ -417,13 +415,14 @@
     gain = jnp.tile(latent_scale, HD // LAT_CH).reshape(1, HD)
     shift = jnp.tile(latent_shift, HD // LAT_CH).reshape(1, HD)
 
+    sigma = jnp.broadcast_to(sigma.reshape(1, 1), (1, HD))
     bias = conv_bias.reshape(1, -1)
     mine, w, lat, own, above, below, taps, gain, shift, bias, sigma = lax.optimization_barrier(
         (mine, w, lat, own, above, below, taps, gain, shift, bias, sigma)
     )
 
     parts = lax.all_to_all(attend(mine, w), "seq", 0, 0, tiled=True)
-    bands_out = update(seq_at, sigma, parts, lat, above, below, gain, shift, features, bands)
+    bands_out = update(seq_at, parts, lat, above, below, sigma, gain, shift, features, bands)
     tiles = lax.all_to_all(bands_out, "grp", 0, 0, tiled=True)
     return convolve(grp_at, tiles, own, above, below, taps, bias)
 

time: 110 us -> 106 us (0.964)
  blocking collectives: 23.6 us -> 44.8 us
  waiting for transfers between devices: 36 us -> 20.1 us
  starting transfers between devices: 27.1 us -> 20.2 us
  Pallas kernels: 21 us -> 18.8 us
    all_to_all x0 -> x1, blocking collectives: none -> 21.2 us  [on_device(): parts = lax.all_to_all(attend(mine, w), 'seq', 0, 0, tiled=True)]
    all_to_all x1 -> x0, waiting for transfers between devices: 15.3 us -> none  [on_device(): parts = lax.all_to_all(attend(mine, w), 'seq', 0, 0, tiled=True)]
    all_to_all x1 -> x0, starting transfers between devices: 6.89 us -> none  [on_device(): parts = lax.all_to_all(attend(mine, w), 'seq', 0, 0, tiled=True)]
    pallas_call x1, Pallas kernels: 1.7 us -> 0.53 us  [update(): pl.pallas_call(functools.partial(update_kernel, features, bands), in_spec...]
  transfers between devices with their start and end apart: 6 -> 5, of which waited for: 5 -> 4; matrix products, arithmetic and copies ran while one was open for 1% -> 1% of each run, Pallas kernels for 0% -> 1%
where the time goes in v5:
time: 106 us; the launch traced here: 105 us
  blocking collectives  44.8 us (42%)
  starting transfers between devices  20.2 us (19%)
  waiting for transfers between devices  20.1 us (19%)
  Pallas kernels  18.8 us (18%)
    all_to_all x1, blocking collectives, on_device(): tiles = lax.all_to_all(bands_out, 'grp', 0, 0, tiled=True)  23.6 us
    all_to_all x1, blocking collectives, on_device(): parts = lax.all_to_all(attend(mine, w), 'seq', 0, 0, tiled=True)  21.2 us
    pallas_call x1, Pallas kernels, attend(): pl.pallas_call(functools.partial(attend_kernel, block_tr), in_specs=[pl.B...  12.8 us
    ppermute x2, waiting for transfers between devices, to_next(): lax.ppermute(array, axis, [(i, i + 1) for i in range(lax.axis_size(axis)...  12.4 us
    all_to_all x1, starting transfers between devices, on_device(): mine = lax.all_to_all(sent, 'seq', 0, 0, tiled=True)  11.4 us
    ppermute x2, starting transfers between devices, to_next(): lax.ppermute(array, axis, [(i, i + 1) for i in range(lax.axis_size(axis)...  5.59 us
    ppermute x2, waiting for transfers between devices, to_last(): lax.ppermute(array, axis, [(i + 1, i) for i in range(lax.axis_size(axis)...  5.02 us
    ppermute x2, starting transfers between devices, to_last(): lax.ppermute(array, axis, [(i + 1, i) for i in range(lax.axis_size(axis)...  3.21 us
  transfers between devices with their start and end apart: 5, of which 4 were waited for; matrix products, arithmetic and copies ran while one was open for 1% of the time, Pallas kernels for 1%

profile of v5, /device:TPU:1, one launch (start us, length us, event | category | flops | bytes accessed | tf_op | source)
XLA Modules:
  0.0 105.4 jit_solution(14414279085834206478)
XLA Ops:
  0.0 0.0 copy-start
  0.0 2.9 %pack_heads.1 = bf16[32,288,128]{2,1,0:T(8,128)(2,1)} custom-call(bf16[96,4096]{1,0:T(8,128)(2,1)} %bitcast.10, bf16[96,4096]{1,0:T(8,128)(2,1)} %bitcast.11, bf16[96,4096]{1,0:T(8,128)(2,1)} %bitcast.12), custom_call_target="tpu_custom_call" | custom-call | tf_op jit(solution)/shard_map/pack_heads/pallas_call | solution.py:40
  2.9 0.0 copy-start.2
  2.9 0.0 copy-start.3
  2.9 0.0 copy-start.4
  2.9 0.0 copy-start.5
  2.9 0.0 copy-start.6
  3.0 0.0 copy-start.1
  3.0 11.4 %all-to-all-start = ((bf16[32,288,128]{2,1,0:T(8,128)(2,1)}), bf16[32,288,128]{2,1,0:T(8,128)(2,1)}, u32[]{:S(2)}, u32[]{:S(2)}) async-start(bf16[32,288,128]{2,1,0:T(8,128)(2,1)} %pack_heads.1), calls=%async_computation | async-start | bytes 4718592 | tf_op jit(solution)/shard_map/all_to_all | solution.py:405
  14.4 0.0 copy-done.2
  14.4 0.1 reshape.38.tail_ref
  14.5 0.2 edge_columns.1
  14.7 1.3 %collective-permute-start = (bf16[96,128]{1,0:T(8,128)(2,1)S(1)}, bf16[96,128]{1,0:T(8,128)(2,1)S(1)}, u32[]{:S(2)}, u32[]{:S(2)}) collective-permute-start(bf16[96,128]{1,0:T(8,128)(2,1)S(1)} %get-tuple-element.23), channel_id=1, source_target_pairs={{0,1},{1,2},{2,3},{3,4},{4,5},{5,6},{6,7},{7,8},{8,9},{9,10},{10,1... | collective-permute-start | bytes 73736 | tf_op jit(solution)/shard_map/ppermute | solution.py:284
  16.0 1.3 %collective-permute-start.1 = (bf16[96,128]{1,0:T(8,128)(2,1)S(1)}, bf16[96,128]{1,0:T(8,128)(2,1)S(1)}, u32[]{:S(2)}, u32[]{:S(2)}) collective-permute-start(bf16[96,128]{1,0:T(8,128)(2,1)S(1)} %get-tuple-element.24), channel_id=1, source_target_pairs={{1,0},{2,1},{3,2},{4,3},{5,4},{6,5},{7,6},{8,7},{9,8},{10,9},{11,1... | collective-permute-start | bytes 73736 | tf_op jit(solution)/shard_map/ppermute | solution.py:288
  17.3 0.0 copy-done
  17.4 0.1 copy.19
  17.5 0.1 fusion
  17.6 0.0 copy-done.3
  17.6 0.1 pad.4.lat_ref
  17.6 0.0 collective-permute-done.before_ref
  17.7 3.3 %collective-permute-done.1.after_ref = bf16[96,128]{1,0:T(8,128)(2,1)S(1)} collective-permute-done((bf16[96,128]{1,0:T(8,128)(2,1)S(1)}, bf16[96,128]{1,0:T(8,128)(2,1)S(1)}, u32[]{:S(2)}, u32[]{:S(2)}) %collective-permute-start.1) | collective-permute-done | bytes 24608 | tf_op jit(solution)/shard_map/ppermute | solution.py:288
  21.0 0.1 edge_rows.1
  21.1 4.3 %collective-permute-start.2 = (bf16[192,128]{1,0:T(8,128)(2,1)S(1)}, bf16[192,128]{1,0:T(8,128)(2,1)S(1)}, u32[]{:S(2)}, u32[]{:S(2)}) collective-permute-start(bf16[192,128]{1,0:T(8,128)(2,1)S(1)} %get-tuple-element.26), channel_id=1, source_target_pairs={{0,16},{16,32},{32,48},{48,64},{64,80},{80,96},{96,112},{112,128},... | collective-permute-start | bytes 147464 | tf_op jit(solution)/shard_map/ppermute | solution.py:284
  25.4 1.9 %collective-permute-start.3 = (bf16[192,128]{1,0:T(8,128)(2,1)S(1)}, bf16[192,128]{1,0:T(8,128)(2,1)S(1)}, u32[]{:S(2)}, u32[]{:S(2)}) collective-permute-start(bf16[192,128]{1,0:T(8,128)(2,1)S(1)} %get-tuple-element.27), channel_id=1, source_target_pairs={{16,0},{32,16},{48,32},{64,48},{80,64},{96,80},{112,96},{128,112},... | collective-permute-start | bytes 147464 | tf_op jit(solution)/shard_map/ppermute | solution.py:288
  27.3 0.1 pad_maximum_fusion.w_ref
  28.1 0.0 copy-done.4
  28.1 0.0 copy-done.5
  28.1 0.1 reshape_tile.6.gain_ref
  28.2 0.0 copy-done.6
  28.2 0.1 reshape_tile.7.shift_ref
  28.3 0.0 copy-done.1
  28.3 0.2 spread_taps.1.taps_ref
  28.5 12.4 %collective-permute-done.2.above_ref = bf16[192,128]{1,0:T(8,128)(2,1)S(1)} collective-permute-done((bf16[192,128]{1,0:T(8,128)(2,1)S(1)}, bf16[192,128]{1,0:T(8,128)(2,1)S(1)}, u32[]{:S(2)}, u32[]{:S(2)}) %collective-permute-start.2) | collective-permute-done | bytes 49184 | tf_op jit(solution)/shard_map/ppermute | solution.py:284
  41.0 1.7 %collective-permute-done.3.below_ref = bf16[192,128]{1,0:T(8,128)(2,1)S(1)} collective-permute-done((bf16[192,128]{1,0:T(8,128)(2,1)S(1)}, bf16[192,128]{1,0:T(8,128)(2,1)S(1)}, u32[]{:S(2)}, u32[]{:S(2)}) %collective-permute-start.3) | collective-permute-done | bytes 49184 | tf_op jit(solution)/shard_map/ppermute | solution.py:288
  42.7 2.6 %all-to-all-done.x_ref = bf16[32,288,128]{2,1,0:T(8,128)(2,1)} async-done(((bf16[32,288,128]{2,1,0:T(8,128)(2,1)}), bf16[32,288,128]{2,1,0:T(8,128)(2,1)}, u32[]{:S(2)}, u32[]{:S(2)}) %all-to-all-start) | async-done | bytes 2359328 | tf_op jit(solution)/shard_map/all_to_all | solution.py:405
  45.3 12.8 %attend.1 = bf16[32,112,128]{2,1,0:T(8,128)(2,1)S(1)} custom-call(bf16[32,288,128]{2,1,0:T(8,128)(2,1)} %all-to-all-done.x_ref, bf16[128,128]{1,0:T(8,128)(2,1)S(1)} %pad_maximum_fusion.w_ref), custom_call_target="tpu_custom_call" | custom-call | flops 9663676416 | bytes 4194304 | tf_op jit(solution)/shard_map/attend/pallas_call | solution.py:136
  58.1 21.2 %all_to_all.15.y_ref = bf16[32,112,128]{2,1,0:T(8,128)(2,1)S(1)} all-to-all(bf16[32,112,128]{2,1,0:T(8,128)(2,1)S(1)} %attend.1), channel_id=1, replica_groups=mesh['seq'=32,'grp'=16] {'seq'}, dimensions={0} | all-to-all | bytes 1835008 | tf_op jit(solution)/shard_map/all_to_all | solution.py:424
  79.3 0.5 update.1
  79.8 23.6 %all_to_all.16.z_ref = bf16[16,16,128]{2,1,0:T(8,128)(2,1)S(1)} all-to-all(bf16[16,16,128]{2,1,0:T(8,128)(2,1)S(1)} %update.1), channel_id=1, replica_groups=mesh['seq'=32,'grp'=16] {'grp'}, dimensions={0} | all-to-all | bytes 131072 | tf_op jit(solution)/shard_map/all_to_all | solution.py:426
  103.4 2.0 %convolve.1 = bf16[16,4,3,2,384]{4,3,2,1,0:T(2,128)(2,1)} custom-call(s32[1]{0:T(128)} %bitcast.index_ref, bf16[16,16,128]{2,1,0:T(8,128)(2,1)S(1)} %all_to_all.16.z_ref, bf16[96,128]{1,0:T(8,128)(2,1)S(1)} %get-tuple-element.36.own_ref, bf16[192,128]{1,0:T(8,128)(2,1)S(1)} %collective-permute-done.2.above_ref, ...), custom_call_target="tpu_custom_call" | custom-call | tf_op jit(solution)/shard_map/convolve/pallas_call | solution.py:368
  (6 shorter events, 0.0 us)
Async XLA Ops:
  0.0 17.3 %copy-start = (bf16[4096,64]{0,1:T(8,128)(2,1)S(1)}, bf16[4096,64]{0,1:T(8,128)(2,1)}, u32[]{:S(2)}) copy-start(bf16[4096,64]{0,1:T(8,128)(2,1)} %param.16) | copy-start | bytes 1572868
  2.9 11.5 %copy-start.2 = (bf16[16,2,2,3,16]{4,2,3,1,0:T(2,128)(2,1)S(1)}, bf16[16,2,2,3,16]{4,2,3,1,0:T(2,128)(2,1)}, u32[]{:S(2)}) copy-start(bf16[16,2,2,3,16]{4,2,3,1,0:T(2,128)(2,1)} %param.19) | copy-start | bytes 18436
  2.9 14.6 %copy-start.3 = (f32[1,1,4,24,64]{4,3,2,1,0:T(8,128)S(1)}, f32[1,1,4,24,64]{4,3,2,1,0:T(8,128)}, u32[]{:S(2)}) copy-start(f32[1,1,4,24,64]{4,3,2,1,0:T(8,128)} %param.14) | copy-start | bytes 73732
  2.9 25.2 %copy-start.4 = (f32[384]{0:T(512)S(1)}, f32[384]{0:T(512)}, u32[]{:S(2)}) copy-start(f32[384]{0:T(512)} %param.21) | copy-start | bytes 4612
  2.9 25.2 %copy-start.5 = (f32[16]{0:T(128)S(1)}, f32[16]{0:T(128)}, u32[]{:S(2)}) copy-start(f32[16]{0:T(128)} %param.17) | copy-start | bytes 196
  2.9 25.3 %copy-start.6 = (f32[16]{0:T(128)S(1)}, f32[16]{0:T(128)}, u32[]{:S(2)}) copy-start(f32[16]{0:T(128)} %param.18) | copy-start | bytes 196
  3.0 25.3 %copy-start.1 = (bf16[432,384]{1,0:T(8,128)(2,1)S(1)}, bf16[432,384]{1,0:T(8,128)(2,1)}, u32[]{:S(2)}) copy-start(bf16[432,384]{1,0:T(8,128)(2,1)} %w_ref.1) | copy-start | bytes 995332
  3.0 42.3 %all-to-all-start = ((bf16[32,288,128]{2,1,0:T(8,128)(2,1)}), bf16[32,288,128]{2,1,0:T(8,128)(2,1)}, u32[]{:S(2)}, u32[]{:S(2)}) async-start(bf16[32,288,128]{2,1,0:T(8,128)(2,1)} %pack_heads.1), calls=%async_computation | async-start | bytes 4718592 | tf_op jit(solution)/shard_map/all_to_all | solution.py:405
  14.7 2.9 %collective-permute-start = (bf16[96,128]{1,0:T(8,128)(2,1)S(1)}, bf16[96,128]{1,0:T(8,128)(2,1)S(1)}, u32[]{:S(2)}, u32[]{:S(2)}) collective-permute-start(bf16[96,128]{1,0:T(8,128)(2,1)S(1)} %get-tuple-element.23), channel_id=1, source_target_pairs={{0,1},{1,2},{2,3},{3,4},{4,5},{5,6},{6,7},{7,8},{8,9},{9,10},{10,1... | collective-permute-start | bytes 73736 | tf_op jit(solution)/shard_map/ppermute | solution.py:284
  16.0 5.0 %collective-permute-start.1 = (bf16[96,128]{1,0:T(8,128)(2,1)S(1)}, bf16[96,128]{1,0:T(8,128)(2,1)S(1)}, u32[]{:S(2)}, u32[]{:S(2)}) collective-permute-start(bf16[96,128]{1,0:T(8,128)(2,1)S(1)} %get-tuple-element.24), channel_id=1, source_target_pairs={{1,0},{2,1},{3,2},{4,3},{5,4},{6,5},{7,6},{8,7},{9,8},{10,9},{11,1... | collective-permute-start | bytes 73736 | tf_op jit(solution)/shard_map/ppermute | solution.py:288
  21.1 19.9 %collective-permute-start.2 = (bf16[192,128]{1,0:T(8,128)(2,1)S(1)}, bf16[192,128]{1,0:T(8,128)(2,1)S(1)}, u32[]{:S(2)}, u32[]{:S(2)}) collective-permute-start(bf16[192,128]{1,0:T(8,128)(2,1)S(1)} %get-tuple-element.26), channel_id=1, source_target_pairs={{0,16},{16,32},{32,48},{48,64},{64,80},{80,96},{96,112},{112,128},... | collective-permute-start | bytes 147464 | tf_op jit(solution)/shard_map/ppermute | solution.py:284
  25.4 17.3 %collective-permute-start.3 = (bf16[192,128]{1,0:T(8,128)(2,1)S(1)}, bf16[192,128]{1,0:T(8,128)(2,1)S(1)}, u32[]{:S(2)}, u32[]{:S(2)}) collective-permute-start(bf16[192,128]{1,0:T(8,128)(2,1)S(1)} %get-tuple-element.27), channel_id=1, source_target_pairs={{16,0},{32,16},{48,32},{64,48},{80,64},{96,80},{112,96},{128,112},... | collective-permute-start | bytes 147464 | tf_op jit(solution)/shard_map/ppermute | solution.py:288

commit v6 on v5

--- a/solution.py
+++ b/solution.py
@@ -176,8 +176,8 @@
     up, own, down = (jnp.broadcast_to(sums[:rows, i : i + 1], (rows, HD)) for i in range(3))
     square = jnp.where(lane < SIDE, up, jnp.where(lane < 3 * SIDE, own, down))
     velocity = velocity / jnp.sqrt(square * (1.0 / features) + NORM_EPS)
-    above = above_ref[above_ref.shape[0] - rows :, :].astype(F32)
-    below = below_ref[below_ref.shape[0] - rows :, :].astype(F32)
+    above = above_ref[...].astype(F32)
+    below = below_ref[...].astype(F32)
     above = above + pltpu.roll(above, HD - SIDE, 1) + pltpu.roll(above, HD - 2 * SIDE, 1)
     below = pltpu.roll(below, 3 * SIDE, 1) + pltpu.roll(below, 2 * SIDE, 1) + pltpu.roll(below, SIDE, 1)
     lat = jnp.where(lane < SIDE, above, jnp.where(lane < 3 * SIDE, lat_ref[...], below))
@@ -232,12 +232,7 @@
 
 def rows_kernel(own_ref, before_ref, after_ref, lat_ref, tile_ref, down_ref, up_ref):
     tile = own_ref[...].astype(F32) + before_ref[...].astype(F32) + after_ref[...].astype(F32)
-    count = tile.shape[0]
     tile_ref[...] = tile.astype(BF16)
-    lane = lax.broadcasted_iota(jnp.int32, tile.shape, 1)
-    turned = pltpu.roll(tile, 2 * SIDE, 1)
-    down_ref[:count, :] = jnp.where(lane < SIDE, turned, 0.0).astype(BF16)
-    up_ref[:count, :] = jnp.where(lane >= 3 * SIDE, turned, 0.0).astype(BF16)
     lat = lat_ref[...]
     high = lat.astype(BF16).astype(F32)
     rest = lat - high
@@ -246,19 +241,18 @@
     lane = lax.broadcasted_iota(jnp.int32, lat.shape, 1)
     for out_ref, start in ((down_ref, 2 * SIDE), (up_ref, SIDE)):
         parts = []
-        for place, part in enumerate((high, mid, low)):
+        for place, part in enumerate((high, mid, low, tile)):
             turn = (place * SIDE - start) % HD
             parts.append(pltpu.roll(part, turn, 1) if turn else part)
-        merged = jnp.where(lane < 2 * SIDE, parts[1], jnp.where(lane < 3 * SIDE, parts[2], 0.0))
-        merged = jnp.where(lane < SIDE, parts[0], merged)
-        out_ref[count:, :] = merged.astype(BF16)
+        merged = jnp.where(lane < 3 * SIDE, parts[2], parts[3])
+        merged = jnp.where(lane < SIDE, parts[0], jnp.where(lane < 2 * SIDE, parts[1], merged))
+        out_ref[...] = merged.astype(BF16)
 
 
 def edges(index, tail, lat):
-    count, more = 3 * tail.shape[0], lat.shape[0]
+    assert lat.shape[0] == 3 * tail.shape[0]
     vmem = pl.BlockSpec(memory_space=VMEM)
-    tile = jax.ShapeDtypeStruct((count, HD), BF16)
-    both = jax.ShapeDtypeStruct((count + more, HD), BF16)
+    tile = jax.ShapeDtypeStruct(lat.shape, BF16)
     small = pltpu.CompilerParams(vmem_limit_bytes=8 << 20)
     own, right, left = pl.pallas_call(
         columns_kernel,
@@ -273,7 +267,7 @@
         rows_kernel,
         in_specs=[vmem] * 4,
         out_specs=[vmem] * 3,
-        out_shape=[tile, both, both],
+        out_shape=[tile] * 3,
         compiler_params=small,
         name="edge_rows",
     )(own, before, after, lat)
@@ -328,10 +322,11 @@
     t, frame, video = at // count, (at // videos) % frames, at % videos
     chosen = jnp.where(source == video * lines + frame * 4 + t, 1.0, 0.0).astype(BF16)
     image = dot_nn(chosen, z_ref[...].reshape(videos * lines, HD)).astype(BF16)
+    above = pltpu.roll(above_ref[...].astype(F32), SIDE, 1)
     cached = own_ref[...].astype(F32)
-    for ref in (above_ref, below_ref):
-        cached = cached + ref[: cached.shape[0], :].astype(F32)
-    cached = cached.astype(BF16)
+    lane = lax.broadcasted_iota(jnp.int32, cached.shape, 1)
+    cached = jnp.where(lane < 3 * SIDE, cached, below_ref[...].astype(F32))
+    cached = jnp.where(lane < SIDE, above, cached).astype(BF16)
     held = cached.shape[0] // 3
     token = [
         jnp.concatenate(

time: 106 us -> 106 us (level)
  no operation moved by 1% of the time
where the time goes in v6:
time: 106 us; the launch traced here: 105 us
  blocking collectives  44.8 us (42%)
  starting transfers between devices  20.2 us (19%)
  waiting for transfers between devices  20.1 us (19%)
  Pallas kernels  18.8 us (18%)
    all_to_all x1, blocking collectives, on_device(): tiles = lax.all_to_all(bands_out, 'grp', 0, 0, tiled=True)  23.6 us
    all_to_all x1, blocking collectives, on_device(): parts = lax.all_to_all(attend(mine, w), 'seq', 0, 0, tiled=True)  21.2 us
    pallas_call x1, Pallas kernels, attend(): pl.pallas_call(functools.partial(attend_kernel, block_tr), in_specs=[pl.B...  12.8 us
    ppermute x2, waiting for transfers between devices, to_next(): lax.ppermute(array, axis, [(i, i + 1) for i in range(lax.axis_size(axis)...  12.1 us
    all_to_all x1, starting transfers between devices, on_device(): mine = lax.all_to_all(sent, 'seq', 0, 0, tiled=True)  11.4 us
    ppermute x2, starting transfers between devices, to_next(): lax.ppermute(array, axis, [(i, i + 1) for i in range(lax.axis_size(axis)...  5.59 us
    ppermute x2, waiting for transfers between devices, to_last(): lax.ppermute(array, axis, [(i + 1, i) for i in range(lax.axis_size(axis)...  5.34 us
    ppermute x2, starting transfers between devices, to_last(): lax.ppermute(array, axis, [(i + 1, i) for i in range(lax.axis_size(axis)...  3.21 us
  transfers between devices with their start and end apart: 5, of which 4 were waited for; matrix products, arithmetic and copies ran while one was open for 1% of the time, Pallas kernels for 1%

profile of v6, /device:TPU:1, one launch (start us, length us, event | category | flops | bytes accessed | tf_op | source)
XLA Modules:
  0.0 105.4 jit_solution(15031053807061818022)
XLA Ops:
  0.0 0.0 copy-start
  0.0 2.9 %pack_heads.1 = bf16[32,288,128]{2,1,0:T(8,128)(2,1)} custom-call(bf16[96,4096]{1,0:T(8,128)(2,1)} %bitcast.10, bf16[96,4096]{1,0:T(8,128)(2,1)} %bitcast.11, bf16[96,4096]{1,0:T(8,128)(2,1)} %bitcast.12), custom_call_target="tpu_custom_call" | custom-call | tf_op jit(solution)/shard_map/pack_heads/pallas_call | solution.py:40
  2.9 0.0 copy-start.2
  2.9 0.0 copy-start.3
  2.9 0.0 copy-start.4
  2.9 0.0 copy-start.5
  2.9 0.0 copy-start.6
  3.0 0.0 copy-start.1
  3.0 11.4 %all-to-all-start = ((bf16[32,288,128]{2,1,0:T(8,128)(2,1)}), bf16[32,288,128]{2,1,0:T(8,128)(2,1)}, u32[]{:S(2)}, u32[]{:S(2)}) async-start(bf16[32,288,128]{2,1,0:T(8,128)(2,1)} %pack_heads.1), calls=%async_computation | async-start | bytes 4718592 | tf_op jit(solution)/shard_map/all_to_all | solution.py:400
  14.4 0.0 copy-done.2
  14.4 0.1 reshape.38.tail_ref
  14.5 0.2 edge_columns.1
  14.7 1.3 %collective-permute-start = (bf16[96,128]{1,0:T(8,128)(2,1)S(1)}, bf16[96,128]{1,0:T(8,128)(2,1)S(1)}, u32[]{:S(2)}, u32[]{:S(2)}) collective-permute-start(bf16[96,128]{1,0:T(8,128)(2,1)S(1)} %get-tuple-element.23), channel_id=1, source_target_pairs={{0,1},{1,2},{2,3},{3,4},{4,5},{5,6},{6,7},{7,8},{8,9},{9,10},{10,1... | collective-permute-start | bytes 73736 | tf_op jit(solution)/shard_map/ppermute | solution.py:278
  16.0 1.3 %collective-permute-start.1 = (bf16[96,128]{1,0:T(8,128)(2,1)S(1)}, bf16[96,128]{1,0:T(8,128)(2,1)S(1)}, u32[]{:S(2)}, u32[]{:S(2)}) collective-permute-start(bf16[96,128]{1,0:T(8,128)(2,1)S(1)} %get-tuple-element.24), channel_id=1, source_target_pairs={{1,0},{2,1},{3,2},{4,3},{5,4},{6,5},{7,6},{8,7},{9,8},{10,9},{11,1... | collective-permute-start | bytes 73736 | tf_op jit(solution)/shard_map/ppermute | solution.py:282
  17.3 0.0 copy-done
  17.4 0.1 copy.19
  17.5 0.1 fusion
  17.6 0.0 copy-done.3
  17.6 0.1 pad.4.lat_ref
  17.6 0.0 collective-permute-done.before_ref
  17.7 3.3 %collective-permute-done.1.after_ref = bf16[96,128]{1,0:T(8,128)(2,1)S(1)} collective-permute-done((bf16[96,128]{1,0:T(8,128)(2,1)S(1)}, bf16[96,128]{1,0:T(8,128)(2,1)S(1)}, u32[]{:S(2)}, u32[]{:S(2)}) %collective-permute-start.1) | collective-permute-done | bytes 24608 | tf_op jit(solution)/shard_map/ppermute | solution.py:282
  21.0 0.1 edge_rows.1
  21.1 4.3 %collective-permute-start.2 = (bf16[96,128]{1,0:T(8,128)(2,1)S(1)}, bf16[96,128]{1,0:T(8,128)(2,1)S(1)}, u32[]{:S(2)}, u32[]{:S(2)}) collective-permute-start(bf16[96,128]{1,0:T(8,128)(2,1)S(1)} %get-tuple-element.26), channel_id=1, source_target_pairs={{0,16},{16,32},{32,48},{48,64},{64,80},{80,96},{96,112},{112,128},... | collective-permute-start | bytes 73736 | tf_op jit(solution)/shard_map/ppermute | solution.py:278
  25.4 1.9 %collective-permute-start.3 = (bf16[96,128]{1,0:T(8,128)(2,1)S(1)}, bf16[96,128]{1,0:T(8,128)(2,1)S(1)}, u32[]{:S(2)}, u32[]{:S(2)}) collective-permute-start(bf16[96,128]{1,0:T(8,128)(2,1)S(1)} %get-tuple-element.27), channel_id=1, source_target_pairs={{16,0},{32,16},{48,32},{64,48},{80,64},{96,80},{112,96},{128,112},... | collective-permute-start | bytes 73736 | tf_op jit(solution)/shard_map/ppermute | solution.py:282
  27.3 0.1 pad_maximum_fusion.w_ref
  28.1 0.0 copy-done.4
  28.1 0.0 copy-done.5
  28.1 0.1 reshape_tile.6.gain_ref
  28.2 0.0 copy-done.6
  28.2 0.1 reshape_tile.7.shift_ref
  28.3 0.0 copy-done.1
  28.3 0.2 spread_taps.1.taps_ref
  28.6 12.1 %collective-permute-done.2.above_ref = bf16[96,128]{1,0:T(8,128)(2,1)S(1)} collective-permute-done((bf16[96,128]{1,0:T(8,128)(2,1)S(1)}, bf16[96,128]{1,0:T(8,128)(2,1)S(1)}, u32[]{:S(2)}, u32[]{:S(2)}) %collective-permute-start.2) | collective-permute-done | bytes 24608 | tf_op jit(solution)/shard_map/ppermute | solution.py:278
  40.7 2.0 %collective-permute-done.3.below_ref = bf16[96,128]{1,0:T(8,128)(2,1)S(1)} collective-permute-done((bf16[96,128]{1,0:T(8,128)(2,1)S(1)}, bf16[96,128]{1,0:T(8,128)(2,1)S(1)}, u32[]{:S(2)}, u32[]{:S(2)}) %collective-permute-start.3) | collective-permute-done | bytes 24608 | tf_op jit(solution)/shard_map/ppermute | solution.py:282
  42.7 2.6 %all-to-all-done.x_ref = bf16[32,288,128]{2,1,0:T(8,128)(2,1)} async-done(((bf16[32,288,128]{2,1,0:T(8,128)(2,1)}), bf16[32,288,128]{2,1,0:T(8,128)(2,1)}, u32[]{:S(2)}, u32[]{:S(2)}) %all-to-all-start) | async-done | bytes 2359328 | tf_op jit(solution)/shard_map/all_to_all | solution.py:400
  45.3 12.8 %attend.1 = bf16[32,112,128]{2,1,0:T(8,128)(2,1)S(1)} custom-call(bf16[32,288,128]{2,1,0:T(8,128)(2,1)} %all-to-all-done.x_ref, bf16[128,128]{1,0:T(8,128)(2,1)S(1)} %pad_maximum_fusion.w_ref), custom_call_target="tpu_custom_call" | custom-call | flops 9663676416 | bytes 4194304 | tf_op jit(solution)/shard_map/attend/pallas_call | solution.py:136
  58.1 21.2 %all_to_all.15.y_ref = bf16[32,112,128]{2,1,0:T(8,128)(2,1)S(1)} all-to-all(bf16[32,112,128]{2,1,0:T(8,128)(2,1)S(1)} %attend.1), channel_id=1, replica_groups=mesh['seq'=32,'grp'=16] {'seq'}, dimensions={0} | all-to-all | bytes 1835008 | tf_op jit(solution)/shard_map/all_to_all | solution.py:419
  79.3 0.5 update.1
  79.8 23.6 %all_to_all.16.z_ref = bf16[16,16,128]{2,1,0:T(8,128)(2,1)S(1)} all-to-all(bf16[16,16,128]{2,1,0:T(8,128)(2,1)S(1)} %update.1), channel_id=1, replica_groups=mesh['seq'=32,'grp'=16] {'grp'}, dimensions={0} | all-to-all | bytes 131072 | tf_op jit(solution)/shard_map/all_to_all | solution.py:421
  103.4 2.0 %convolve.1 = bf16[16,4,3,2,384]{4,3,2,1,0:T(2,128)(2,1)} custom-call(s32[1]{0:T(128)} %bitcast.index_ref, bf16[16,16,128]{2,1,0:T(8,128)(2,1)S(1)} %all_to_all.16.z_ref, bf16[96,128]{1,0:T(8,128)(2,1)S(1)} %get-tuple-element.36.own_ref, bf16[96,128]{1,0:T(8,128)(2,1)S(1)} %collective-permute-done.2.above_ref, ...), custom_call_target="tpu_custom_call" | custom-call | tf_op jit(solution)/shard_map/convolve/pallas_call | solution.py:363
  (6 shorter events, 0.0 us)
Async XLA Ops:
  0.0 17.3 %copy-start = (bf16[4096,64]{0,1:T(8,128)(2,1)S(1)}, bf16[4096,64]{0,1:T(8,128)(2,1)}, u32[]{:S(2)}) copy-start(bf16[4096,64]{0,1:T(8,128)(2,1)} %param.16) | copy-start | bytes 1572868
  2.9 11.5 %copy-start.2 = (bf16[16,2,2,3,16]{4,2,3,1,0:T(2,128)(2,1)S(1)}, bf16[16,2,2,3,16]{4,2,3,1,0:T(2,128)(2,1)}, u32[]{:S(2)}) copy-start(bf16[16,2,2,3,16]{4,2,3,1,0:T(2,128)(2,1)} %param.19) | copy-start | bytes 18436
  2.9 14.6 %copy-start.3 = (f32[1,1,4,24,64]{4,3,2,1,0:T(8,128)S(1)}, f32[1,1,4,24,64]{4,3,2,1,0:T(8,128)}, u32[]{:S(2)}) copy-start(f32[1,1,4,24,64]{4,3,2,1,0:T(8,128)} %param.14) | copy-start | bytes 73732
  2.9 25.2 %copy-start.4 = (f32[384]{0:T(512)S(1)}, f32[384]{0:T(512)}, u32[]{:S(2)}) copy-start(f32[384]{0:T(512)} %param.21) | copy-start | bytes 4612
  2.9 25.2 %copy-start.5 = (f32[16]{0:T(128)S(1)}, f32[16]{0:T(128)}, u32[]{:S(2)}) copy-start(f32[16]{0:T(128)} %param.17) | copy-start | bytes 196
  2.9 25.3 %copy-start.6 = (f32[16]{0:T(128)S(1)}, f32[16]{0:T(128)}, u32[]{:S(2)}) copy-start(f32[16]{0:T(128)} %param.18) | copy-start | bytes 196
  3.0 25.3 %copy-start.1 = (bf16[432,384]{1,0:T(8,128)(2,1)S(1)}, bf16[432,384]{1,0:T(8,128)(2,1)}, u32[]{:S(2)}) copy-start(bf16[432,384]{1,0:T(8,128)(2,1)} %w_ref.1) | copy-start | bytes 995332
  3.0 42.3 %all-to-all-start = ((bf16[32,288,128]{2,1,0:T(8,128)(2,1)}), bf16[32,288,128]{2,1,0:T(8,128)(2,1)}, u32[]{:S(2)}, u32[]{:S(2)}) async-start(bf16[32,288,128]{2,1,0:T(8,128)(2,1)} %pack_heads.1), calls=%async_computation | async-start | bytes 4718592 | tf_op jit(solution)/shard_map/all_to_all | solution.py:400
  14.7 2.9 %collective-permute-start = (bf16[96,128]{1,0:T(8,128)(2,1)S(1)}, bf16[96,128]{1,0:T(8,128)(2,1)S(1)}, u32[]{:S(2)}, u32[]{:S(2)}) collective-permute-start(bf16[96,128]{1,0:T(8,128)(2,1)S(1)} %get-tuple-element.23), channel_id=1, source_target_pairs={{0,1},{1,2},{2,3},{3,4},{4,5},{5,6},{6,7},{7,8},{8,9},{9,10},{10,1... | collective-permute-start | bytes 73736 | tf_op jit(solution)/shard_map/ppermute | solution.py:278
  16.0 5.0 %collective-permute-start.1 = (bf16[96,128]{1,0:T(8,128)(2,1)S(1)}, bf16[96,128]{1,0:T(8,128)(2,1)S(1)}, u32[]{:S(2)}, u32[]{:S(2)}) collective-permute-start(bf16[96,128]{1,0:T(8,128)(2,1)S(1)} %get-tuple-element.24), channel_id=1, source_target_pairs={{1,0},{2,1},{3,2},{4,3},{5,4},{6,5},{7,6},{8,7},{9,8},{10,9},{11,1... | collective-permute-start | bytes 73736 | tf_op jit(solution)/shard_map/ppermute | solution.py:282
  21.1 19.6 %collective-permute-start.2 = (bf16[96,128]{1,0:T(8,128)(2,1)S(1)}, bf16[96,128]{1,0:T(8,128)(2,1)S(1)}, u32[]{:S(2)}, u32[]{:S(2)}) collective-permute-start(bf16[96,128]{1,0:T(8,128)(2,1)S(1)} %get-tuple-element.26), channel_id=1, source_target_pairs={{0,16},{16,32},{32,48},{48,64},{64,80},{80,96},{96,112},{112,128},... | collective-permute-start | bytes 73736 | tf_op jit(solution)/shard_map/ppermute | solution.py:278
  25.4 17.3 %collective-permute-start.3 = (bf16[96,128]{1,0:T(8,128)(2,1)S(1)}, bf16[96,128]{1,0:T(8,128)(2,1)S(1)}, u32[]{:S(2)}, u32[]{:S(2)}) collective-permute-start(bf16[96,128]{1,0:T(8,128)(2,1)S(1)} %get-tuple-element.27), channel_id=1, source_target_pairs={{16,0},{32,16},{48,32},{64,48},{80,64},{96,80},{112,96},{128,112},... | collective-permute-start | bytes 73736 | tf_op jit(solution)/shard_map/ppermute | solution.py:282

commit v7 on v6

--- a/solution.py
+++ b/solution.py
@@ -175,7 +175,7 @@
     lane = lax.broadcasted_iota(jnp.int32, (rows, HD), 1)
     up, own, down = (jnp.broadcast_to(sums[:rows, i : i + 1], (rows, HD)) for i in range(3))
     square = jnp.where(lane < SIDE, up, jnp.where(lane < 3 * SIDE, own, down))
-    velocity = velocity / jnp.sqrt(square * (1.0 / features) + NORM_EPS)
+    velocity = velocity * lax.rsqrt(square * (1.0 / features) + NORM_EPS)
     above = above_ref[...].astype(F32)
     below = below_ref[...].astype(F32)
     above = above + pltpu.roll(above, HD - SIDE, 1) + pltpu.roll(above, HD - 2 * SIDE, 1)
@@ -348,7 +348,7 @@
         for i in range(2):
             conv = part[:, i * out : (i + 1) * out] + bias_ref[...]
             mean_sq = jnp.mean(conv * conv, axis=1, keepdims=True)
-            normed = conv / jnp.sqrt(mean_sq + NORM_EPS)
+            normed = conv * lax.rsqrt(mean_sq + NORM_EPS)
             done.append(normed / (1.0 + jnp.exp(-normed)))
         for f in range(frames):
             at = slice(f * videos, (f + 1) * videos)

time: 106 us -> 106 us (level)
  no operation moved by 1% of the time
where the time goes in v7:
time: 106 us; the launch traced here: 105 us
  blocking collectives  44.8 us (42%)
  starting transfers between devices  20.2 us (19%)
  waiting for transfers between devices  20.1 us (19%)
  Pallas kernels  18.8 us (18%)
    all_to_all x1, blocking collectives, on_device(): tiles = lax.all_to_all(bands_out, 'grp', 0, 0, tiled=True)  23.6 us
    all_to_all x1, blocking collectives, on_device(): parts = lax.all_to_all(attend(mine, w), 'seq', 0, 0, tiled=True)  21.2 us
    pallas_call x1, Pallas kernels, attend(): pl.pallas_call(functools.partial(attend_kernel, block_tr), in_specs=[pl.B...  12.8 us
    ppermute x2, waiting for transfers between devices, to_next(): lax.ppermute(array, axis, [(i, i + 1) for i in range(lax.axis_size(axis)...  12.1 us
    all_to_all x1, starting transfers between devices, on_device(): mine = lax.all_to_all(sent, 'seq', 0, 0, tiled=True)  11.4 us
    ppermute x2, starting transfers between devices, to_next(): lax.ppermute(array, axis, [(i, i + 1) for i in range(lax.axis_size(axis)...  5.59 us
    ppermute x2, waiting for transfers between devices, to_last(): lax.ppermute(array, axis, [(i + 1, i) for i in range(lax.axis_size(axis)...  5.34 us
    ppermute x2, starting transfers between devices, to_last(): lax.ppermute(array, axis, [(i + 1, i) for i in range(lax.axis_size(axis)...  3.21 us
  transfers between devices with their start and end apart: 5, of which 4 were waited for; matrix products, arithmetic and copies ran while one was open for 1% of the time, Pallas kernels for 1%

profile of v7, /device:TPU:1, one launch (start us, length us, event | category | flops | bytes accessed | tf_op | source)
XLA Modules:
  0.0 105.4 jit_solution(18324067459018749481)
XLA Ops:
  0.0 0.0 copy-start
  0.0 2.9 %pack_heads.1 = bf16[32,288,128]{2,1,0:T(8,128)(2,1)} custom-call(bf16[96,4096]{1,0:T(8,128)(2,1)} %bitcast.10, bf16[96,4096]{1,0:T(8,128)(2,1)} %bitcast.11, bf16[96,4096]{1,0:T(8,128)(2,1)} %bitcast.12), custom_call_target="tpu_custom_call" | custom-call | tf_op jit(solution)/shard_map/pack_heads/pallas_call | solution.py:40
  2.9 0.0 copy-start.2
  2.9 0.0 copy-start.3
  2.9 0.0 copy-start.4
  2.9 0.0 copy-start.5
  2.9 0.0 copy-start.6
  3.0 0.0 copy-start.1
  3.0 11.4 %all-to-all-start = ((bf16[32,288,128]{2,1,0:T(8,128)(2,1)}), bf16[32,288,128]{2,1,0:T(8,128)(2,1)}, u32[]{:S(2)}, u32[]{:S(2)}) async-start(bf16[32,288,128]{2,1,0:T(8,128)(2,1)} %pack_heads.1), calls=%async_computation | async-start | bytes 4718592 | tf_op jit(solution)/shard_map/all_to_all | solution.py:400
  14.4 0.0 copy-done.2
  14.4 0.1 reshape.38.tail_ref
  14.5 0.2 edge_columns.1
  14.7 1.3 %collective-permute-start = (bf16[96,128]{1,0:T(8,128)(2,1)S(1)}, bf16[96,128]{1,0:T(8,128)(2,1)S(1)}, u32[]{:S(2)}, u32[]{:S(2)}) collective-permute-start(bf16[96,128]{1,0:T(8,128)(2,1)S(1)} %get-tuple-element.23), channel_id=1, source_target_pairs={{0,1},{1,2},{2,3},{3,4},{4,5},{5,6},{6,7},{7,8},{8,9},{9,10},{10,1... | collective-permute-start | bytes 73736 | tf_op jit(solution)/shard_map/ppermute | solution.py:278
  16.0 1.3 %collective-permute-start.1 = (bf16[96,128]{1,0:T(8,128)(2,1)S(1)}, bf16[96,128]{1,0:T(8,128)(2,1)S(1)}, u32[]{:S(2)}, u32[]{:S(2)}) collective-permute-start(bf16[96,128]{1,0:T(8,128)(2,1)S(1)} %get-tuple-element.24), channel_id=1, source_target_pairs={{1,0},{2,1},{3,2},{4,3},{5,4},{6,5},{7,6},{8,7},{9,8},{10,9},{11,1... | collective-permute-start | bytes 73736 | tf_op jit(solution)/shard_map/ppermute | solution.py:282
  17.3 0.0 copy-done
  17.4 0.1 copy.19
  17.5 0.1 fusion
  17.6 0.0 copy-done.3
  17.6 0.1 pad.4.lat_ref
  17.6 0.0 collective-permute-done.before_ref
  17.7 3.3 %collective-permute-done.1.after_ref = bf16[96,128]{1,0:T(8,128)(2,1)S(1)} collective-permute-done((bf16[96,128]{1,0:T(8,128)(2,1)S(1)}, bf16[96,128]{1,0:T(8,128)(2,1)S(1)}, u32[]{:S(2)}, u32[]{:S(2)}) %collective-permute-start.1) | collective-permute-done | bytes 24608 | tf_op jit(solution)/shard_map/ppermute | solution.py:282
  21.0 0.1 edge_rows.1
  21.1 4.3 %collective-permute-start.2 = (bf16[96,128]{1,0:T(8,128)(2,1)S(1)}, bf16[96,128]{1,0:T(8,128)(2,1)S(1)}, u32[]{:S(2)}, u32[]{:S(2)}) collective-permute-start(bf16[96,128]{1,0:T(8,128)(2,1)S(1)} %get-tuple-element.26), channel_id=1, source_target_pairs={{0,16},{16,32},{32,48},{48,64},{64,80},{80,96},{96,112},{112,128},... | collective-permute-start | bytes 73736 | tf_op jit(solution)/shard_map/ppermute | solution.py:278
  25.4 1.9 %collective-permute-start.3 = (bf16[96,128]{1,0:T(8,128)(2,1)S(1)}, bf16[96,128]{1,0:T(8,128)(2,1)S(1)}, u32[]{:S(2)}, u32[]{:S(2)}) collective-permute-start(bf16[96,128]{1,0:T(8,128)(2,1)S(1)} %get-tuple-element.27), channel_id=1, source_target_pairs={{16,0},{32,16},{48,32},{64,48},{80,64},{96,80},{112,96},{128,112},... | collective-permute-start | bytes 73736 | tf_op jit(solution)/shard_map/ppermute | solution.py:282
  27.3 0.1 pad_maximum_fusion.w_ref
  28.1 0.0 copy-done.4
  28.1 0.0 copy-done.5
  28.1 0.1 reshape_tile.6.gain_ref
  28.2 0.0 copy-done.6
  28.2 0.1 reshape_tile.7.shift_ref
  28.3 0.0 copy-done.1
  28.3 0.2 spread_taps.1.taps_ref
  28.6 12.1 %collective-permute-done.2.above_ref = bf16[96,128]{1,0:T(8,128)(2,1)S(1)} collective-permute-done((bf16[96,128]{1,0:T(8,128)(2,1)S(1)}, bf16[96,128]{1,0:T(8,128)(2,1)S(1)}, u32[]{:S(2)}, u32[]{:S(2)}) %collective-permute-start.2) | collective-permute-done | bytes 24608 | tf_op jit(solution)/shard_map/ppermute | solution.py:278
  40.7 2.0 %collective-permute-done.3.below_ref = bf16[96,128]{1,0:T(8,128)(2,1)S(1)} collective-permute-done((bf16[96,128]{1,0:T(8,128)(2,1)S(1)}, bf16[96,128]{1,0:T(8,128)(2,1)S(1)}, u32[]{:S(2)}, u32[]{:S(2)}) %collective-permute-start.3) | collective-permute-done | bytes 24608 | tf_op jit(solution)/shard_map/ppermute | solution.py:282
  42.7 2.6 %all-to-all-done.x_ref = bf16[32,288,128]{2,1,0:T(8,128)(2,1)} async-done(((bf16[32,288,128]{2,1,0:T(8,128)(2,1)}), bf16[32,288,128]{2,1,0:T(8,128)(2,1)}, u32[]{:S(2)}, u32[]{:S(2)}) %all-to-all-start) | async-done | bytes 2359328 | tf_op jit(solution)/shard_map/all_to_all | solution.py:400
  45.3 12.8 %attend.1 = bf16[32,112,128]{2,1,0:T(8,128)(2,1)S(1)} custom-call(bf16[32,288,128]{2,1,0:T(8,128)(2,1)} %all-to-all-done.x_ref, bf16[128,128]{1,0:T(8,128)(2,1)S(1)} %pad_maximum_fusion.w_ref), custom_call_target="tpu_custom_call" | custom-call | flops 9663676416 | bytes 4194304 | tf_op jit(solution)/shard_map/attend/pallas_call | solution.py:136
  58.1 21.2 %all_to_all.15.y_ref = bf16[32,112,128]{2,1,0:T(8,128)(2,1)S(1)} all-to-all(bf16[32,112,128]{2,1,0:T(8,128)(2,1)S(1)} %attend.1), channel_id=1, replica_groups=mesh['seq'=32,'grp'=16] {'seq'}, dimensions={0} | all-to-all | bytes 1835008 | tf_op jit(solution)/shard_map/all_to_all | solution.py:419
  79.3 0.5 update.1
  79.8 23.6 %all_to_all.16.z_ref = bf16[16,16,128]{2,1,0:T(8,128)(2,1)S(1)} all-to-all(bf16[16,16,128]{2,1,0:T(8,128)(2,1)S(1)} %update.1), channel_id=1, replica_groups=mesh['seq'=32,'grp'=16] {'grp'}, dimensions={0} | all-to-all | bytes 131072 | tf_op jit(solution)/shard_map/all_to_all | solution.py:421
  103.4 2.0 %convolve.1 = bf16[16,4,3,2,384]{4,3,2,1,0:T(2,128)(2,1)} custom-call(s32[1]{0:T(128)} %bitcast.index_ref, bf16[16,16,128]{2,1,0:T(8,128)(2,1)S(1)} %all_to_all.16.z_ref, bf16[96,128]{1,0:T(8,128)(2,1)S(1)} %get-tuple-element.36.own_ref, bf16[96,128]{1,0:T(8,128)(2,1)S(1)} %collective-permute-done.2.above_ref, ...), custom_call_target="tpu_custom_call" | custom-call | tf_op jit(solution)/shard_map/convolve/pallas_call | solution.py:363
  (6 shorter events, 0.0 us)
Async XLA Ops:
  0.0 17.3 %copy-start = (bf16[4096,64]{0,1:T(8,128)(2,1)S(1)}, bf16[4096,64]{0,1:T(8,128)(2,1)}, u32[]{:S(2)}) copy-start(bf16[4096,64]{0,1:T(8,128)(2,1)} %param.16) | copy-start | bytes 1572868
  2.9 11.5 %copy-start.2 = (bf16[16,2,2,3,16]{4,2,3,1,0:T(2,128)(2,1)S(1)}, bf16[16,2,2,3,16]{4,2,3,1,0:T(2,128)(2,1)}, u32[]{:S(2)}) copy-start(bf16[16,2,2,3,16]{4,2,3,1,0:T(2,128)(2,1)} %param.19) | copy-start | bytes 18436
  2.9 14.6 %copy-start.3 = (f32[1,1,4,24,64]{4,3,2,1,0:T(8,128)S(1)}, f32[1,1,4,24,64]{4,3,2,1,0:T(8,128)}, u32[]{:S(2)}) copy-start(f32[1,1,4,24,64]{4,3,2,1,0:T(8,128)} %param.14) | copy-start | bytes 73732
  2.9 25.2 %copy-start.4 = (f32[384]{0:T(512)S(1)}, f32[384]{0:T(512)}, u32[]{:S(2)}) copy-start(f32[384]{0:T(512)} %param.21) | copy-start | bytes 4612
  2.9 25.2 %copy-start.5 = (f32[16]{0:T(128)S(1)}, f32[16]{0:T(128)}, u32[]{:S(2)}) copy-start(f32[16]{0:T(128)} %param.17) | copy-start | bytes 196
  2.9 25.3 %copy-start.6 = (f32[16]{0:T(128)S(1)}, f32[16]{0:T(128)}, u32[]{:S(2)}) copy-start(f32[16]{0:T(128)} %param.18) | copy-start | bytes 196
  3.0 25.3 %copy-start.1 = (bf16[432,384]{1,0:T(8,128)(2,1)S(1)}, bf16[432,384]{1,0:T(8,128)(2,1)}, u32[]{:S(2)}) copy-start(bf16[432,384]{1,0:T(8,128)(2,1)} %w_ref.1) | copy-start | bytes 995332
  3.0 42.3 %all-to-all-start = ((bf16[32,288,128]{2,1,0:T(8,128)(2,1)}), bf16[32,288,128]{2,1,0:T(8,128)(2,1)}, u32[]{:S(2)}, u32[]{:S(2)}) async-start(bf16[32,288,128]{2,1,0:T(8,128)(2,1)} %pack_heads.1), calls=%async_computation | async-start | bytes 4718592 | tf_op jit(solution)/shard_map/all_to_all | solution.py:400
  14.7 2.9 %collective-permute-start = (bf16[96,128]{1,0:T(8,128)(2,1)S(1)}, bf16[96,128]{1,0:T(8,128)(2,1)S(1)}, u32[]{:S(2)}, u32[]{:S(2)}) collective-permute-start(bf16[96,128]{1,0:T(8,128)(2,1)S(1)} %get-tuple-element.23), channel_id=1, source_target_pairs={{0,1},{1,2},{2,3},{3,4},{4,5},{5,6},{6,7},{7,8},{8,9},{9,10},{10,1... | collective-permute-start | bytes 73736 | tf_op jit(solution)/shard_map/ppermute | solution.py:278
  16.0 5.0 %collective-permute-start.1 = (bf16[96,128]{1,0:T(8,128)(2,1)S(1)}, bf16[96,128]{1,0:T(8,128)(2,1)S(1)}, u32[]{:S(2)}, u32[]{:S(2)}) collective-permute-start(bf16[96,128]{1,0:T(8,128)(2,1)S(1)} %get-tuple-element.24), channel_id=1, source_target_pairs={{1,0},{2,1},{3,2},{4,3},{5,4},{6,5},{7,6},{8,7},{9,8},{10,9},{11,1... | collective-permute-start | bytes 73736 | tf_op jit(solution)/shard_map/ppermute | solution.py:282
  21.1 19.6 %collective-permute-start.2 = (bf16[96,128]{1,0:T(8,128)(2,1)S(1)}, bf16[96,128]{1,0:T(8,128)(2,1)S(1)}, u32[]{:S(2)}, u32[]{:S(2)}) collective-permute-start(bf16[96,128]{1,0:T(8,128)(2,1)S(1)} %get-tuple-element.26), channel_id=1, source_target_pairs={{0,16},{16,32},{32,48},{48,64},{64,80},{80,96},{96,112},{112,128},... | collective-permute-start | bytes 73736 | tf_op jit(solution)/shard_map/ppermute | solution.py:278
  25.4 17.3 %collective-permute-start.3 = (bf16[96,128]{1,0:T(8,128)(2,1)S(1)}, bf16[96,128]{1,0:T(8,128)(2,1)S(1)}, u32[]{:S(2)}, u32[]{:S(2)}) collective-permute-start(bf16[96,128]{1,0:T(8,128)(2,1)S(1)} %get-tuple-element.27), channel_id=1, source_target_pairs={{16,0},{32,16},{48,32},{64,48},{80,64},{96,80},{112,96},{128,112},... | collective-permute-start | bytes 73736 | tf_op jit(solution)/shard_map/ppermute | solution.py:282
